TPU v7x, 256 devices: a whole 4x4x8 slice. The times are simulated.
256 devices in a mesh: dp: 64 (over y, z, core), seq: 4 (over x).
Axes of the slice: x: 4, y: 4, z: 8, core: 2. Of those that a mesh axis runs over, the one named last changes fastest.
Arguments:
- tokens: bfloat16 [64, 768, 1536], P('dp', 'seq'), may hold values from -6 to 6
- cotangent: bfloat16 [64, 768, 1536], P('dp', 'seq'), may hold values from -6 to 6
- condition: bfloat16 [64, 2, 3072], P('dp'), may hold values from -6 to 6
- per_image_rows: int32 [64, 2], replicated, may hold values from 1 to 96, as said below
- query_key_value_weight: bfloat16 [1536, 4608], P('dp'), may hold values from -1 to 1
- adapter_down: bfloat16 [1536, 64], replicated, may hold values from -0.15625 to 0.15625
- adapter_up: bfloat16 [64, 4608], replicated, may hold values from -0.75 to 0.75
- modulation_matrix: bfloat16 [3072, 3072], P('dp'), may hold values from -0.109375 to 0.109375
Outputs:
- attention: bfloat16 [64, 768, 1536], P('dp', 'seq')
- token_grad: bfloat16 [64, 768, 1536], P('dp', 'seq')
- down_grad: float32 [1536, 64], P('dp')
- up_grad: float32 [64, 4608], P(None, 'dp')
- modulation_grad: float32 [3072, 3072], P('dp')
Inputs may be any that keep to these rules, and one draw needn't show every extreme that they name: Each group's two images take per_image_rows[g, 0] and per_image_rows[g, 1] rows of each of the group's 4 devices; a group fills 2 to 192 rows, the rows of all groups sum to exactly 6144, and some group fills all 192 rows.
All inputs are finite; a program needn't handle non-finite values.
Results may differ from a plain program's by a relative error of at most 0.025.
Values may be sent and summed in bfloat16 or wider, within the bound.
A program may use at most 128 MiB of HBM per device.

v0:
```python
import jax
import jax.numpy as jnp
from jax import lax
from jax.sharding import PartitionSpec as P

HEAD_SIZE = 128


EPSILON = 1e-06
PRECISE = lax.Precision.HIGHEST
MASKED = -1e30


def image_labels(row_rank, bounds):
    return jnp.sum((row_rank[:, None] >= bounds[None, :]).astype(jnp.int32), axis=1)


def projected_rows(modulated_input, weight_matrix, adapter_down, adapter_up):
    adapter_hidden = jnp.dot(
        modulated_input, adapter_down, preferred_element_type=jnp.float32
    ).astype(jnp.bfloat16)
    reduced_total = jnp.dot(
        modulated_input, weight_matrix, preferred_element_type=jnp.float32
    ) + jnp.dot(adapter_hidden, adapter_up, preferred_element_type=jnp.float32)
    return (adapter_hidden, reduced_total.astype(jnp.bfloat16))


def to_peers(block_rows, rotation, groups):
    shaped = block_rows.reshape(block_rows.shape[0] // groups, groups, block_rows.shape[1])
    return jnp.roll(shaped, rotation, axis=1)


def from_peers(received, rotation):
    unrolled = jnp.roll(received, -rotation, axis=1)
    return unrolled.reshape(-1, received.shape[2])


def pack_rows(received, places, capacity):
    flattened = received.reshape(-1, received.shape[2])
    blank_rows = jnp.zeros((capacity, flattened.shape[1]), flattened.dtype)
    return blank_rows.at[places.reshape(-1)].set(flattened, mode="drop")


def unpack_rows(packed, places, live_slots):
    picked = packed[jnp.minimum(places, packed.shape[0] - 1)]
    return jnp.where(live_slots[:, :, None], picked, jnp.zeros_like(picked))


def body(
    tokens,
    cotangent,
    condition,
    per_image_rows,
    query_key_value_weight,
    adapter_down,
    adapter_up,
    modulation_matrix,
):
    groups = lax.axis_size("dp")
    my_group = lax.axis_index("dp")
    row_count = tokens.shape[1]
    features = tokens.shape[2]
    att_width = cotangent.shape[2]
    head_count = att_width // HEAD_SIZE
    images = condition.shape[1]
    score_scale = HEAD_SIZE ** (-0.5)
    weight_matrix = lax.all_gather(query_key_value_weight, "dp", axis=0, tiled=True)
    activated = jax.nn.silu(condition[0].astype(jnp.float32)).astype(jnp.bfloat16)
    all_active = lax.all_gather(activated, "dp", axis=0, tiled=True)
    owned_rows = modulation_matrix.shape[0]
    own_active = lax.dynamic_slice_in_dim(all_active, my_group * owned_rows, owned_rows, 1)
    modulation = lax.psum_scatter(
        jnp.dot(own_active, modulation_matrix, preferred_element_type=jnp.float32),
        "dp",
        scatter_dimension=0,
        tiled=True,
    )
    my_counts = lax.dynamic_index_in_dim(per_image_rows, my_group, 0, keepdims=False)
    bounds = jnp.cumsum(my_counts)
    row_rank = jnp.arange(row_count, dtype=jnp.int32)
    labels = image_labels(row_rank, bounds)
    usable = labels < images
    one_hot = (labels[:, None] == jnp.arange(images, dtype=jnp.int32)[None, :]).astype(jnp.float32)
    shift_rows = jnp.dot(one_hot, modulation[:, :features], precision=PRECISE)
    scale_rows = jnp.dot(one_hot, modulation[:, features:], precision=PRECISE)
    inputs_wide = tokens[0].astype(jnp.float32)
    centred = inputs_wide - jnp.mean(inputs_wide, axis=1, keepdims=True)
    inverse = lax.rsqrt(jnp.mean(centred * centred, axis=1, keepdims=True) + EPSILON)
    normed = centred * inverse
    modulated_input = jnp.where(
        usable[:, None], (1.0 + scale_rows) * normed + shift_rows, 0.0
    ).astype(jnp.bfloat16)
    capacity = row_count // 2
    totals = jnp.sum(per_image_rows, axis=1)
    offsets = jnp.cumsum(totals) - totals
    rotation = offsets[my_group] % groups
    slot_rank = jnp.arange(row_count // groups, dtype=jnp.int32)[:, None]
    source_row = slot_rank * groups + ((my_group - offsets) % groups)[None, :]
    live_slots = source_row < totals[None, :]
    places = jnp.where(live_slots, (offsets[None, :] + source_row) // groups, capacity)
    arrived = lax.all_to_all(
        to_peers(modulated_input, rotation, groups), "dp", split_axis=1, concat_axis=1, tiled=True
    )
    bundled_input = pack_rows(arrived, places, capacity)
    bundled_adapter, bundled_projection = projected_rows(
        bundled_input, weight_matrix, adapter_down, adapter_up
    )
    returned = lax.all_to_all(
        unpack_rows(bundled_projection, places, live_slots),
        "dp",
        split_axis=1,
        concat_axis=1,
        tiled=True,
    )
    projected = from_peers(returned, rotation)
    queries = projected[:, :att_width].reshape(row_count, head_count, HEAD_SIZE)
    own_keys = projected[:, att_width : 2 * att_width].reshape(row_count, head_count, HEAD_SIZE)
    own_values = projected[:, 2 * att_width :].reshape(row_count, head_count, HEAD_SIZE)
    key_value = lax.all_gather(projected[:, att_width:], "seq", axis=0, tiled=True)
    seq_rows = key_value.shape[0]
    keys_all = key_value[:, :att_width].reshape(seq_rows, head_count, HEAD_SIZE)
    values_all = key_value[:, att_width:].reshape(seq_rows, head_count, HEAD_SIZE)
    key_labels = jnp.tile(labels, seq_rows // row_count)
    allowed = (labels[:, None] == key_labels[None, :]) & (key_labels[None, :] < images)
    scores = (
        jnp.einsum("qhd,khd->hqk", queries, keys_all, preferred_element_type=jnp.float32)
        * score_scale
    )
    scores = jnp.where(allowed[None], scores, MASKED)
    largest = jnp.max(scores, axis=2, keepdims=True)
    log_total = largest + jnp.log(jnp.sum(jnp.exp(scores - largest), axis=2, keepdims=True))
    attn_probs = jnp.exp(scores - log_total)
    probs_low = attn_probs.astype(jnp.bfloat16)
    attended = jnp.einsum(
        "hqk,khd->qhd", probs_low, values_all, preferred_element_type=jnp.float32
    ).reshape(row_count, att_width)
    attention_out = jnp.where(usable[:, None], attended, 0.0).astype(jnp.bfloat16)
    out_grad = jnp.where(usable[:, None], cotangent[0], jnp.zeros_like(cotangent[0]))
    head_grads = out_grad.reshape(row_count, head_count, HEAD_SIZE)
    delta_sum = jnp.sum(
        head_grads.astype(jnp.float32)
        * attention_out.reshape(row_count, head_count, HEAD_SIZE).astype(jnp.float32),
        axis=2,
    )
    prob_grads = jnp.einsum(
        "qhd,khd->hqk", head_grads, values_all, preferred_element_type=jnp.float32
    )
    score_grads = (attn_probs * (prob_grads - delta_sum.T[:, :, None]) * score_scale).astype(
        jnp.bfloat16
    )
    query_grad = jnp.einsum(
        "hqk,khd->qhd", score_grads, keys_all, preferred_element_type=jnp.float32
    )
    stat_total, stat_delta = (
        lax.all_gather(log_total[:, :, 0].T, "seq", axis=0, tiled=True),
        lax.all_gather(delta_sum, "seq", axis=0, tiled=True),
    )
    part_query = lax.all_gather(queries, "seq", axis=0, tiled=True)
    part_grad = lax.all_gather(head_grads, "seq", axis=0, tiled=True)
    amount = part_query.shape[0]
    part_labels = image_labels(jnp.arange(amount, dtype=jnp.int32) % row_count, bounds)
    part_allowed = (part_labels[:, None] == labels[None, :]) & usable[None, :]
    part_scores = (
        jnp.einsum("qhd,khd->hqk", part_query, own_keys, preferred_element_type=jnp.float32)
        * score_scale
    )
    part_scores = jnp.where(part_allowed[None], part_scores, MASKED)
    part_probs = jnp.exp(part_scores - stat_total.T[:, :, None])
    part_prob_grads = jnp.einsum(
        "qhd,khd->hqk", part_grad, own_values, preferred_element_type=jnp.float32
    )
    part_score_grads = (
        part_probs * (part_prob_grads - stat_delta.T[:, :, None]) * score_scale
    ).astype(jnp.bfloat16)
    key_term = jnp.einsum(
        "hqk,qhd->khd", part_score_grads, part_query, preferred_element_type=jnp.float32
    )
    value_term = jnp.einsum(
        "hqk,qhd->khd",
        part_probs.astype(jnp.bfloat16),
        part_grad,
        preferred_element_type=jnp.float32,
    )
    projection_grad = jnp.concatenate(
        [
            query_grad.reshape(row_count, att_width),
            key_term.reshape(row_count, att_width),
            value_term.reshape(row_count, att_width),
        ],
        axis=1,
    ).astype(jnp.bfloat16)
    arrived_grads = lax.all_to_all(
        to_peers(projection_grad, rotation, groups), "dp", split_axis=1, concat_axis=1, tiled=True
    )
    bundled_grads = pack_rows(arrived_grads, places, capacity)
    adapter_hidden_grad = jnp.dot(
        bundled_grads, adapter_up.T, preferred_element_type=jnp.float32
    ).astype(jnp.bfloat16)
    packed_modded = (
        jnp.dot(bundled_grads, weight_matrix.T, preferred_element_type=jnp.float32)
        + jnp.dot(adapter_hidden_grad, adapter_down.T, preferred_element_type=jnp.float32)
    ).astype(jnp.bfloat16)
    down_part = jnp.dot(bundled_input.T, adapter_hidden_grad, preferred_element_type=jnp.float32)
    up_part = jnp.dot(bundled_adapter.T, bundled_grads, preferred_element_type=jnp.float32)
    returned_grads = lax.all_to_all(
        unpack_rows(packed_modded, places, live_slots),
        "dp",
        split_axis=1,
        concat_axis=1,
        tiled=True,
    )
    modded_grad = from_peers(returned_grads, rotation)
    modded_wide = modded_grad.astype(jnp.float32)
    normed_grad = (1.0 + scale_rows) * modded_wide
    image_part = jnp.concatenate(
        [
            jnp.dot(one_hot.T, modded_wide, precision=PRECISE),
            jnp.dot(one_hot.T, modded_wide * normed, precision=PRECISE),
        ],
        axis=1,
    )
    image_grad = lax.psum(image_part, "seq")
    input_grad = inverse * (
        normed_grad
        - jnp.mean(normed_grad, axis=1, keepdims=True)
        - normed * jnp.mean(normed_grad * normed, axis=1, keepdims=True)
    )
    active_wide = own_active.astype(jnp.float32)
    modulation_grad = jnp.dot(
        active_wide.T, lax.all_gather(image_grad, "dp", axis=0, tiled=True), precision=PRECISE
    )
    shares_down, shares_up = (
        lax.psum_scatter(down_part, "dp", scatter_dimension=0, tiled=True),
        lax.psum_scatter(up_part, "dp", scatter_dimension=1, tiled=True),
    )
    down_grad, up_grad = lax.psum((shares_down, shares_up), "seq")
    return (
        attention_out[None],
        input_grad.astype(jnp.bfloat16)[None],
        down_grad,
        up_grad,
        modulation_grad,
    )


def solution(mesh):
    in_specs = (
        P("dp", "seq", None),
        P("dp", "seq", None),
        P("dp", None, None),
        P(),
        P("dp", None),
        P(),
        P(),
        P("dp", None),
    )
    out_specs = (
        P("dp", "seq", None),
        P("dp", "seq", None),
        P("dp", None),
        P(None, "dp"),
        P("dp", None),
    )
    return jax.shard_map(body, mesh=mesh, in_specs=in_specs, out_specs=out_specs, check_vma=False)
```

profile of v0, /device:TPU:1, one launch (start us, length us, event | category | flops | bytes accessed | tf_op | source)
XLA Modules:
  0.0 1119.2 jit_solution(13216576963434681377)
XLA Ops:
  8.1 55.2 %all-gather = bf16[64,2,3072]{2,1,0:T(2,128)(2,1)S(1)} all-gather(bf16[1,2,3072]{2,1,0:T(2,128)(2,1)S(1)} %fusion.87), channel_id=1, replica_groups=mesh['dp'=64,'seq'=4] {'dp'}, dimensions={0}, use_global_device_ids=true | all-gather | bytes 798720 | tf_op jit(solution)/shard_map/all_gather | solution.py:69
  71.2 177.8 %all-reduce.7.cloned.1.call-done = f32[128,3072]{1,0:T(8,128)} async-done(((f32[128,3072]{1,0:T(8,128)}), f32[128,3072]{1,0:T(8,128)}) %all-reduce.7.cloned.1.call-update) | async-done | bytes 1572880
  254.6 9.7 all-to-all-start
  266.1 27.4 %all-to-all-done = bf16[3,64,1536]{2,0,1:T(4,128)(2,1)S(1)} async-done(((bf16[3,64,1536]{2,0,1:T(4,128)(2,1)}), bf16[3,64,1536]{2,0,1:T(4,128)(2,1)S(1)}, u32[]{:S(2)}, u32[]{:S(2)}) %all-to-all-start) | async-done | bytes 589856 | tf_op jit(solution)/shard_map/all_to_all | solution.py:101
  297.9 52.9 %all-gather.10.cloned.1.call-done = bf16[1536,4608]{1,0:T(8,128)(2,1)} async-done(((bf16[24,4608]{1,0:T(8,128)(2,1)}), bf16[1536,4608]{1,0:T(8,128)(2,1)}) %all-gather.10.cloned.1.call-update) | async-done | bytes 14155792 | tf_op jit(solution)/shard_map/all_gather | solution.py:67
  350.8 7.4 fusion.117
  358.7 3.1 gather_fusion
  361.8 4.6 copy_select_fusion
  366.4 6.3 all-to-all-start.1
  372.7 56.5 %all-to-all-done.1 = bf16[3,64,4608]{2,0,1:T(4,128)(2,1)} async-done(((bf16[3,64,4608]{2,0,1:T(4,128)(2,1)}), bf16[3,64,4608]{2,0,1:T(4,128)(2,1)}, u32[]{:S(2)}, u32[]{:S(2)}) %all-to-all-start.1) | async-done | bytes 1769504 | tf_op jit(solution)/shard_map/all_to_all | solution.py:108
  441.4 45.3 %all-gather.12.cloned.1.call-done = bf16[768,3072]{1,0:T(8,128)(2,1)} async-done(((bf16[192,3072]{1,0:T(8,128)(2,1)}), bf16[768,3072]{1,0:T(8,128)(2,1)}) %all-gather.12.cloned.1.call-update) | async-done | bytes 4718608 | tf_op jit(solution)/shard_map/all_gather | solution.py:119
  486.8 4.9 fusion.116
  491.6 4.3 copy.110
  495.9 4.3 copy.111
  500.2 3.4 fusion.3
  507.8 3.3 multiply_reduce_fusion
  512.1 12.3 %all-gather.14.cloned.1.call-done = bf16[768,12,128]{2,0,1:T(8,128)(2,1)} async-done(((bf16[192,12,128]{2,0,1:T(8,128)(2,1)}), bf16[768,12,128]{2,0,1:T(8,128)(2,1)}) %all-gather.14.cloned.1.call-update) | async-done | bytes 2359312 | tf_op jit(solution)/shard_map/all_gather | solution.py:158
  524.5 5.7 fusion.65
  530.1 8.7 fusion.44
  541.6 10.3 all-gather.2
  552.1 10.5 all-gather.1
  563.3 8.7 fusion.45
  574.7 5.7 fusion.41
  582.0 4.0 fusion.29
  587.6 70.1 %all_to_all.20 = bf16[3,64,4608]{2,0,1:T(4,128)(2,1)S(1)} all-to-all(bf16[3,64,4608]{2,0,1:T(4,128)(2,1)S(1)} %copy.128), channel_id=1, replica_groups=mesh['dp'=64,'seq'=4] {'dp'}, dimensions={1} | all-to-all | bytes 3538944 | tf_op jit(solution)/shard_map/all_to_all | solution.py:192
  659.3 4.0 scatter_custom_fusion.1
  664.3 9.4 fusion.118
  678.7 6.2 all-to-all-start.3
  689.0 184.4 %all-reduce.9.cloned.1.call-done = f32[64,4608]{1,0:T(8,128)} async-done(((f32[64,4608]{1,0:T(8,128)}), f32[64,4608]{1,0:T(8,128)}) %all-reduce.9.cloned.1.call-update) | async-done | bytes 1179664
  879.0 129.3 %reduce-scatter.5.cloned.1.call-done = f32[24,64]{1,0:T(8,128)} async-done(((f32[1536,64]{1,0:T(8,128)}), f32[24,64]{1,0:T(8,128)}) %reduce-scatter.5.cloned.1.call-update) | async-done | bytes 6160
  1008.3 15.3 %all-reduce.3 = (f32[24,64]{1,0:T(8,128)}, f32[64,72]{1,0:T(8,128)}, f32[2,3072]{1,0:T(2,128)}) all-reduce(f32[24,64]{1,0:T(8,128)} %reduce-scatter.5.cloned.1.call-done, f32[64,72]{1,0:T(8,128)} %constant_dynamic-slice_fusion.1, f32[2,3072]{1,0:T(2,128)} %pad_maximum_fusion), channel_id=1, replica_groups=mesh['dp'=64,'seq'=4] {'seq'}, use_global_device_ids=true, to_apply=%region_16.19 | all-reduce | flops 12288 | bytes 98304 | tf_op jit(solution)/shard_map/psum | solution.py:236
  1029.1 78.0 %all-gather.18.cloned.1.call-done = f32[64,2,3072]{2,1,0:T(2,128)} async-done(((f32[1,2,3072]{2,1,0:T(2,128)}), f32[64,2,3072]{2,1,0:T(2,128)}) %all-gather.18.cloned.1.call-update) | async-done | bytes 1572880 | tf_op jit(solution)/shard_map/all_gather | solution.py:230
  (161 shorter events, 71.4 us)
Async XLA Ops:
  7.2 351.1 %copy-start = (bf16[64,4608]{1,0:T(8,128)(2,1)S(1)}, bf16[64,4608]{1,0:T(8,128)(2,1)}, u32[]{:S(2)}) copy-start(bf16[64,4608]{1,0:T(8,128)(2,1)} %param.18) | copy-start | bytes 1769476
  7.2 56.4 %copy-start.12 = (bf16[48,3072]{1,0:T(8,128)(2,1)S(1)}, bf16[48,3072]{1,0:T(8,128)(2,1)}, u32[]{:S(2)}) copy-start(bf16[48,3072]{1,0:T(8,128)(2,1)} %param.19) | copy-start | bytes 884740
  7.2 241.8 %all-reduce.7.cloned.1.call-start = ((), (), s32[]{:S(2)}) async-start(), calls=%async_computation.10 | async-start | bytes 3145728
  63.6 7.6 copy-start.8
  63.6 5.7 copy-start.29
  63.6 7.1 copy-start.2
  65.2 285.6 %all-gather.10.cloned.1.call-start = ((), (), s32[]{:S(2)}) async-start(), calls=%async_computation.5 | async-start | bytes 14376960 | tf_op jit(solution)/shard_map/all_gather | solution.py:67
  70.7 181.4 %copy-start.15 = (s32[192]{0:T(256)}, s32[192]{0:T(256)S(1)}, u32[]{:S(2)}) copy-start(s32[192]{0:T(256)S(1)} %fusion.102) | copy-start | bytes 2308
  70.9 181.8 %copy-start.18 = (f32[192]{0:T(256)}, f32[192]{0:T(256)S(1)}, u32[]{:S(2)}) copy-start(f32[192]{0:T(256)S(1)} %broadcast_multiply_fusion.2) | copy-start | bytes 2308
  71.2 181.4 %copy-start.22 = (pred[192]{0:T(512)(128)(4,1)}, pred[192]{0:T(512)(128)(4,1)S(1)}, u32[]{:S(2)}) copy-start(pred[192]{0:T(512)(128)(4,1)S(1)} %broadcast_compare_fusion.1) | copy-start | bytes 580
  71.2 181.4 %copy-start.20 = (f32[192]{0:T(256)}, f32[192]{0:T(256)S(1)}, u32[]{:S(2)}) copy-start(f32[192]{0:T(256)S(1)} %add_rsqrt_fusion) | copy-start | bytes 2308
  254.6 39.0 %all-to-all-start = ((bf16[3,64,1536]{2,0,1:T(4,128)(2,1)}), bf16[3,64,1536]{2,0,1:T(4,128)(2,1)S(1)}, u32[]{:S(2)}, u32[]{:S(2)}) async-start(bf16[3,64,1536]{2,0,1:T(4,128)(2,1)} %fusion.59), calls=%async_computation | async-start | bytes 1572864 | tf_op jit(solution)/shard_map/all_to_all | solution.py:101
  266.1 84.8 %copy-start.26 = (s32[192,1]{0,1:T(1,128)}, s32[192,1]{0,1:T(1,128)S(1)}, u32[]{:S(2)}) copy-start(s32[192,1]{0,1:T(1,128)S(1)} %compare_select_fusion) | copy-start | bytes 2308
  297.9 60.3 %copy-start.13 = (bf16[96,64]{0,1:T(8,128)(2,1)}, bf16[96,64]{0,1:T(8,128)(2,1)S(1)}, u32[]{:S(2)}) copy-start(bf16[96,64]{0,1:T(8,128)(2,1)S(1)} %convolution_convert_fusion.1) | copy-start | bytes 36868
  366.4 62.9 %all-to-all-start.1 = ((bf16[3,64,4608]{2,0,1:T(4,128)(2,1)}), bf16[3,64,4608]{2,0,1:T(4,128)(2,1)}, u32[]{:S(2)}, u32[]{:S(2)}) async-start(bf16[3,64,4608]{2,0,1:T(4,128)(2,1)} %copy_select_fusion), calls=%async_computation.1 | async-start | bytes 4718592 | tf_op jit(solution)/shard_map/all_to_all | solution.py:108
  372.7 114.1 %all-gather.12.cloned.1.call-start = ((), (), s32[]{:S(2)}) async-start(), calls=%async_computation.6 | async-start | bytes 5898240 | tf_op jit(solution)/shard_map/all_gather | solution.py:119
  434.9 89.6 %all-gather.14.cloned.1.call-start = ((), (), s32[]{:S(2)}) async-start(), calls=%async_computation.7 | async-start | bytes 2949120 | tf_op jit(solution)/shard_map/all_gather | solution.py:158
  438.5 124.9 %all-gather.16.cloned.1.call-start = ((), (), s32[]{:S(2)}) async-start(), calls=%async_computation.8 | async-start | bytes 2949120 | tf_op jit(solution)/shard_map/all_gather | solution.py:159
  503.6 4.2 copy-start.9
  503.7 4.2 copy-start.23
  507.8 16.6 %copy-start.6 = (bf16[24,12,8,128]{3,2,1,0:T(8,128)(2,1)S(1)}, bf16[24,12,8,128]{3,2,1,0:T(8,128)(2,1)}, u32[]{:S(2)}) copy-start(bf16[24,12,8,128]{3,2,1,0:T(8,128)(2,1)} %get-tuple-element.19) | copy-start | bytes 1769476
  664.3 9.4 copy-start.10
  676.0 8.9 copy-start.4
  678.7 196.3 %all-to-all-start.3 = ((bf16[3,64,1536]{2,0,1:T(4,128)(2,1)}), bf16[3,64,1536]{2,0,1:T(4,128)(2,1)}, u32[]{:S(2)}, u32[]{:S(2)}) async-start(bf16[3,64,1536]{2,0,1:T(4,128)(2,1)} %copy_select_fusion.1), calls=%async_computation.3 | async-start | bytes 1572864 | tf_op jit(solution)/shard_map/all_to_all | solution.py:205
  684.9 188.6 %all-reduce.9.cloned.1.call-start = ((), (), s32[]{:S(2)}) async-start(), calls=%async_computation.11 | async-start | bytes 2359296
  687.0 321.3 %reduce-scatter.5.cloned.1.call-start = ((), (), s32[]{:S(2)}) async-start(), calls=%async_computation.12 | async-start | bytes 798720
  688.9 188.4 %copy-start.17 = (s32[192]{0:T(256)S(1)}, s32[192]{0:T(256)}, u32[]{:S(2)}) copy-start(s32[192]{0:T(256)} %copy-done.15) | copy-start | bytes 2308
  688.9 188.7 %copy-start.19 = (f32[192]{0:T(256)S(1)}, f32[192]{0:T(256)}, u32[]{:S(2)}) copy-start(f32[192]{0:T(256)} %copy-done.18) | copy-start | bytes 2308
  688.9 188.7 %copy-start.21 = (f32[192]{0:T(256)S(1)}, f32[192]{0:T(256)}, u32[]{:S(2)}) copy-start(f32[192]{0:T(256)} %copy-done.20) | copy-start | bytes 2308
  688.9 418.1 %all-gather.18.cloned.1.call-start = ((), (), s32[]{:S(2)}) async-start(), calls=%async_computation.9 | async-start | bytes 1597440 | tf_op jit(solution)/shard_map/all_gather | solution.py:230
  875.0 148.6 %copy-start.11 = (bf16[192,12,128]{2,0,1:T(8,128)(2,1)S(1)}, bf16[192,12,128]{2,0,1:T(8,128)(2,1)}, u32[]{:S(2)}) copy-start(bf16[192,12,128]{2,0,1:T(8,128)(2,1)} %get-tuple-element.23) | copy-start | bytes 1769476
  877.3 149.1 %copy-start.24 = (pred[192]{0:T(512)(128)(4,1)S(1)}, pred[192]{0:T(512)(128)(4,1)}, u32[]{:S(2)}) copy-start(pred[192]{0:T(512)(128)(4,1)} %copy-done.22) | copy-start | bytes 580
  (9 other events, 23.4 us)
Sparse Core Ops, SparseCore 0:
  65.3 183.6 all-reduce.6
  251.7 99.0 all-gather.9
  435.0 51.7 all-gather.11
  488.4 35.9 all-gather.13
  526.7 36.6 all-gather.15
  688.8 184.5 all-reduce.8
  878.0 130.3 reduce-scatter.4
  1023.7 83.3 all-gather.17
where the time goes:
time: 1130 us; the launch traced here: 1120 us
  waiting for transfers between devices  766 us (68%)
  blocking collectives  161 us (14%)
  matrix products  65.9 us (6%)
  local copies, waits for them, and re-layouts  59.4 us (5%)
  other arithmetic  25.5 us (2%)
  starting transfers between devices  22.9 us (2%)
  between operations  18.5 us (2%)
    unnamed x11, waiting for transfers between devices  492 us
    all_gather x1, waiting for transfers between devices, body(): lax.all_gather(image_grad, 'dp', axis=0, tiled=True)  78 us
    all_to_all x1, blocking collectives, body(): lax.all_to_all(to_peers(projection_grad, rotation, groups), 'dp', split_a...  70.1 us
    all_to_all x1, waiting for transfers between devices, body(): lax.all_to_all(unpack_rows(bundled_projection, places, live_slots), 'dp',...  56.5 us
    all_gather x1, blocking collectives, body(): all_active = lax.all_gather(activated, 'dp', axis=0, tiled=True)  55.2 us
    all_gather x1, waiting for transfers between devices, body(): lax.all_gather(query_key_value_weight, 'dp', axis=0, tiled=True)  52.9 us
    all_gather x1, waiting for transfers between devices, body(): lax.all_gather(projected[:, att_width:], 'seq', axis=0, tiled=True)  45.3 us
    all_to_all x1, waiting for transfers between devices, body(): lax.all_to_all(to_peers(modulated_input, rotation, groups), 'dp', split_a...  27.4 us
  transfers between devices with their start and end apart: 11, of which 10 were waited for; matrix products, arithmetic and copies ran while one was open for 7% of the time, Pallas kernels for 0%

commit v1 on v0

v1 whole, which is shorter than its diff:
```python
import jax
import jax.numpy as jnp
from jax import lax
from jax.experimental import pallas as pl
from jax.experimental.pallas import tpu as pltpu
from jax.sharding import PartitionSpec as P

HEAD_SIZE = 128
EPSILON = 1e-06
MASKED = -1e30
MESH = pl.DeviceIdType.MESH
NX, NY, NZ, NC = 4, 4, 8, 2
F32, BF16 = jnp.float32, jnp.bfloat16
ANY = pl.BlockSpec(memory_space=pl.ANY)
VM = pl.BlockSpec(memory_space=pltpu.VMEM)


def remote(src, dst, send_sem, recv_sem, device):
    return pltpu.make_async_remote_copy(
        src_ref=src,
        dst_ref=dst,
        send_sem=send_sem,
        recv_sem=recv_sem,
        device_id=device,
        device_id_type=MESH,
    )


class Place:
    def __init__(self):
        self.dp = lax.axis_index("dp")
        self.s = lax.axis_index("seq")
        self.y = self.dp // (NZ * NC)
        self.z = (self.dp // NC) % NZ
        self.c = self.dp % NC

    def at(self, dx=0, dy=0, dz=0, flip=False):
        s = (self.s + dx) % NX if dx else self.s
        y = (self.y + dy) % NY if dy else self.y
        z = (self.z + dz) % NZ if dz else self.z
        c = 1 - self.c if flip else self.c
        return (y * (NZ * NC) + z * NC + c, s)


def enter(me):
    barrier = pltpu.get_barrier_semaphore()
    peers = [me.at(dx=i) for i in range(1, NX)]
    peers += [me.at(dy=i) for i in range(1, NY)]
    peers += [me.at(dz=i) for i in range(1, NZ)]
    peers += [me.at(flip=True)]
    for peer in peers:
        pl.semaphore_signal(barrier, inc=1, device_id=peer, device_id_type=MESH)
    pl.semaphore_wait(barrier, len(peers))


class PlaneGather:
    def __init__(self, me, buf, ysend, yrecv, zsend, zrecv, csend, crecv):
        self.me, self.buf = me, buf
        self.ysend, self.yrecv = ysend, yrecv
        self.zsend, self.zrecv = zsend, zrecv
        self.csend, self.crecv = csend, crecv
        self.sent = []

    def start_y(self, own):
        me = self.me
        for i in range(1, NY):
            copy = remote(
                own, self.buf.at[me.c, me.z, me.y], self.ysend.at[i - 1], self.yrecv.at[i - 1], me.at(dy=i)
            )
            copy.start()
            self.sent.append(copy)

    def wait_y(self):
        me = self.me
        for i in range(1, NY):
            place = self.buf.at[me.c, me.z, (me.y + NY - i) % NY]
            remote(place, place, self.ysend.at[i - 1], self.yrecv.at[i - 1], me.at(dy=i)).wait_recv()

    def ring(self, way, step, part):
        me = self.me
        if way == 0:
            source, there = (me.z + NZ - step + 1) % NZ, me.at(dz=1)
        else:
            source, there = (me.z + step - 1) % NZ, me.at(dz=NZ - 1)
        block = self.buf.at[me.c, source, part]
        at = (way * 4 + step - 1) * NY + part
        return remote(block, block, self.zsend.at[at], self.zrecv.at[at], there)

    def arrive(self, way, step, part):
        me = self.me
        source = (me.z + NZ - step) % NZ if way == 0 else (me.z + step) % NZ
        block = self.buf.at[me.c, source, part]
        at = (way * 4 + step - 1) * NY + part
        there = me.at(dz=1) if way == 0 else me.at(dz=NZ - 1)
        remote(block, block, self.zsend.at[at], self.zrecv.at[at], there).wait_recv()

    def carried(self, way, step, part):
        return step < 4 or (part // 2) == way

    def step(self, step):
        for turn in range(NY):
            for way in (0, 1):
                part = turn if way == 0 else NY - 1 - turn
                if step > 1 and self.carried(way, step - 1, part):
                    self.arrive(way, step - 1, part)
                if step <= 4 and self.carried(way, step, part):
                    copy = self.ring(way, step, part)
                    copy.start()
                    self.sent.append(copy)
        if step == 1:
            self.cross(0)
        elif step == 5:
            self.cross(4)
        else:
            self.cross(step - 1)
            self.cross(NZ - step + 1)

    def cross(self, shift):
        me = self.me
        block = self.buf.at[me.c, (me.z + shift) % NZ]
        copy = remote(block, block, self.csend.at[shift], self.crecv.at[shift], me.at(flip=True))
        copy.start()
        self.sent.append(copy)

    def wait_cross(self):
        me = self.me
        for shift in range(NZ):
            block = self.buf.at[1 - me.c, (me.z + shift) % NZ]
            remote(block, block, self.csend.at[shift], self.crecv.at[shift], me.at(flip=True)).wait_recv()

    def drain(self):
        for copy in self.sent:
            copy.wait_send()


def plane_sems():
    return [
        pltpu.SemaphoreType.DMA((NY - 1,)),
        pltpu.SemaphoreType.DMA((NY - 1,)),
        pltpu.SemaphoreType.DMA((8 * NY,)),
        pltpu.SemaphoreType.DMA((8 * NY,)),
        pltpu.SemaphoreType.DMA((NZ,)),
        pltpu.SemaphoreType.DMA((NZ,)),
    ]


def exchange(me, axis, count, source, slots, send, recv):
    copies = []
    for i in range(1, count):
        copy = remote(source(i), slots.at[i - 1], send.at[i - 1], recv.at[i - 1], me.at(**{axis: i}))
        copy.start()
        copies.append(copy)
    return copies


def finish(copies):
    for copy in copies:
        copy.wait()


def gather_kernel(
    tok, cot, wsh, act, mm,
    tok_all, cot_all, w_all, mod_all, act_own,
    act_all, act_wide, part_wide, part_low, core_in, sum_core, z_in, sum_z, y_in, own_mod,
    tsend, trecv, ksend, krecv, lsem,
    wys, wyr, wzs, wzr, wcs, wcr,
    ays, ayr, azs, azr, acs, acr,
    mcs, mcr, mzs, mzr, mys, myr, mxs, mxr,
):
    me = Place()
    s = me.s
    chunk = tok.shape[0] // 4
    head_cols = cot_all.shape[2]
    act_all[me.c, me.z, me.y] = act[...]
    enter(me)
    right, left = me.at(dx=1), me.at(dx=NX - 1)
    sl, sr = (s + NX - 1) % NX, (s + 1) % NX

    acts = PlaneGather(me, act_all, ays, ayr, azs, azr, acs, acr)
    acts.start_y(act)
    weights = PlaneGather(me, w_all, wys, wyr, wzs, wzr, wcs, wcr)
    weights.start_y(wsh)

    sent = []

    def rows(i):
        return pl.ds(i * chunk, chunk)

    def token_copy(source, owner, i, slot, there):
        return remote(source, tok_all.at[owner, rows(i)], tsend.at[slot], trecv.at[slot], there)

    for i in range(4):
        j = 3 - i
        for copy in (
            token_copy(tok.at[rows(i)], s, i, i, right),
            token_copy(tok.at[rows(j)], s, j, 4 + j, left),
        ):
            copy.start()
            sent.append(copy)
    locals_ = [
        pltpu.make_async_copy(tok, tok_all.at[s], lsem.at[0]),
        pltpu.make_async_copy(
            cot.at[:, pl.ds(pl.multiple_of(s * head_cols, 128), head_cols)], cot_all.at[s], lsem.at[1]
        ),
        pltpu.make_async_copy(wsh, w_all.at[me.c, me.z, me.y], lsem.at[2]),
    ]
    for copy in locals_:
        copy.start()

    acts.wait_y()
    acts.step(1)
    weights.wait_y()
    locals_[2].wait()
    weights.step(1)
    acts.step(2)

    for i in (0, 1):
        token_copy(tok.at[rows(i)], sl, i, i, right).wait_recv()
        copy = token_copy(tok_all.at[sl, rows(i)], sl, i, 8 + i, right)
        copy.start()
        sent.append(copy)
        j = 3 - i
        token_copy(tok.at[rows(j)], sr, j, 4 + j, left).wait_recv()
        copy = token_copy(tok_all.at[sr, rows(j)], sr, j, 8 + j, left)
        copy.start()
        sent.append(copy)

    acts.step(3)
    weights.step(2)
    acts.step(4)

    cot_sent = []
    for i in range(1, NX):
        there = me.at(dx=i)
        copy = remote(
            cot.at[:, pl.ds(pl.multiple_of(there[1] * head_cols, 128), head_cols)],
            cot_all.at[s], ksend.at[i - 1], krecv.at[i - 1], there,
        )
        copy.start()
        cot_sent.append(copy)

    acts.step(5)
    acts.wait_cross()

    act_wide[...] = act_all[...].reshape(act_wide.shape).astype(F32)
    first = 48 * me.dp
    j0 = first // 128
    j1 = (j0 + 1) % 24
    offset = first - 128 * j0
    row = lax.broadcasted_iota(jnp.int32, (128, 128), 0)
    col = lax.broadcasted_iota(jnp.int32, (128, 128), 1)
    inside = col < 48
    pick0 = jnp.where((row == col + offset) & inside, 1.0, 0.0).astype(BF16)
    pick1 = jnp.where((row + 128 == col + offset) & inside, 1.0, 0.0).astype(BF16)
    for img in range(2):
        low = act_wide[pl.ds(img * 24 + j0, 64, stride=48), :].astype(BF16)
        high = act_wide[pl.ds(img * 24 + j1, 64, stride=48), :].astype(BF16)
        act_own[img * 64 : (img + 1) * 64, :] = (
            jnp.dot(low, pick0, preferred_element_type=F32)
            + jnp.dot(high, pick1, preferred_element_type=F32)
        ).astype(BF16)
    part_wide[...] = jnp.zeros_like(part_wide)
    for j in range(6):
        columns = jnp.dot(act_own[...], mm[:, j * 128 : (j + 1) * 128], preferred_element_type=F32)
        for img in range(2):
            part_wide[pl.ds(img * 6 + j, 64, stride=16), :] = columns[img * 64 : (img + 1) * 64]
    part_low[0] = part_wide[0:512].astype(BF16)
    part_low[1] = part_wide[512:1024].astype(BF16)
    crossing = remote(part_low.at[1 - me.c], core_in, mcs, mcr, me.at(flip=True))
    crossing.start()
    weights.step(3)
    crossing.wait()
    sum_core[...] = (
        (part_low[me.c].astype(F32) + core_in[...].astype(F32)).astype(BF16).reshape(sum_core.shape)
    )
    copies = exchange(me, "dz", NZ, lambda i: sum_core.at[(me.z + i) % NZ], z_in, mzs, mzr)
    finish(copies)
    total = sum_core[me.z].astype(F32)
    for i in range(NZ - 1):
        total += z_in[i].astype(F32)
    sum_z[...] = total.reshape(sum_z.shape)
    copies = exchange(me, "dy", NY, lambda i: sum_z.at[(me.y + i) % NY], y_in, mys, myr)
    finish(copies)
    own_mod[...] = sum_z[me.y] + y_in[0] + y_in[1] + y_in[2]
    mod_all[s] = own_mod[...]
    mod_sent = []
    for i in range(1, NX):
        copy = remote(own_mod, mod_all.at[s], mxs.at[i - 1], mxr.at[i - 1], me.at(dx=i))
        copy.start()
        mod_sent.append(copy)

    weights.step(4)
    weights.step(5)

    for i in (0, 1):
        opposite = (s + 2) % NX
        token_copy(tok.at[rows(i)], opposite, i, 8 + i, right).wait_recv()
        token_copy(tok.at[rows(3 - i)], opposite, 3 - i, 8 + 3 - i, left).wait_recv()
    for i in (2, 3):
        token_copy(tok.at[rows(i)], sl, i, i, right).wait_recv()
        token_copy(tok.at[rows(3 - i)], sr, 3 - i, 4 + 3 - i, left).wait_recv()
    for copy in sent:
        copy.wait_send()
    finish(cot_sent)
    finish(mod_sent)
    weights.wait_cross()
    acts.drain()
    weights.drain()
    locals_[0].wait()
    locals_[1].wait()


def gather_all(tok, cot, wsh, act, mm):
    rows, width = tok.shape
    dma = pltpu.SemaphoreType.DMA
    return pl.pallas_call(
        gather_kernel,
        out_shape=(
            jax.ShapeDtypeStruct((NX, rows, width), BF16),
            jax.ShapeDtypeStruct((NX, rows, width // NX), BF16),
            jax.ShapeDtypeStruct((NC, NZ, NY) + wsh.shape, BF16),
            jax.ShapeDtypeStruct((NX, 16, 128), F32),
            jax.ShapeDtypeStruct((128, 128), BF16),
        ),
        in_specs=[ANY, ANY, ANY, VM, VM],
        out_specs=(ANY, ANY, ANY, VM, VM),
        scratch_shapes=[
            pltpu.VMEM((NC, NZ, NY, 48, 128), BF16),
            pltpu.VMEM((3072, 128), F32),
            pltpu.VMEM((1024, 128), F32),
            pltpu.VMEM((NC, 512, 128), BF16),
            pltpu.VMEM((512, 128), BF16),
            pltpu.VMEM((NZ, 64, 128), BF16),
            pltpu.VMEM((NZ - 1, 64, 128), BF16),
            pltpu.VMEM((NY, 16, 128), F32),
            pltpu.VMEM((NY - 1, 16, 128), F32),
            pltpu.VMEM((16, 128), F32),
            dma((12,)), dma((12,)), dma((3,)), dma((3,)), dma((3,)),
            *plane_sems(),
            *plane_sems(),
            dma, dma, dma((NZ - 1,)), dma((NZ - 1,)), dma((NY - 1,)), dma((NY - 1,)), dma((3,)), dma((3,)),
        ],
        compiler_params=pltpu.CompilerParams(
            collective_id=1, has_side_effects=True, vmem_limit_bytes=24 * 1024 * 1024
        ),
        name="gather_all",
    )(tok, cot, wsh, act, mm)


def nt(a, b):
    return lax.dot_general(a, b, (((1,), (1,)), ((), ())), preferred_element_type=F32)


def tn(a, b):
    return lax.dot_general(a, b, (((0,), (0,)), ((), ())), preferred_element_type=F32)


def labels_of(rank, c0, c1):
    return (rank >= c0).astype(jnp.int32) + (rank >= c0 + c1).astype(jnp.int32)


def local_kernel(
    counts, tok, mod, cot, w, down, up,
    attn, pg, ip, up_part, down_part,
    modded, stats, low, proj, proj_grad, kv_grad, low_grad,
):
    c0, c1 = counts[0], counts[1]
    rows, width = tok.shape[1], tok.shape[2]
    heads = cot.shape[2] // HEAD_SIZE
    att = heads * HEAD_SIZE
    scale = HEAD_SIZE ** (-0.5)
    label = labels_of(lax.broadcasted_iota(jnp.int32, (rows, 1), 0), c0, c1)
    usable = label < 2
    is0 = label == 0
    lane = lax.broadcasted_iota(jnp.int32, (8, NX * rows), 1)
    for _ in range(NX - 1):
        lane = jnp.where(lane >= rows, lane - rows, lane)
    key_label = labels_of(lane, c0, c1)

    @pl.loop(0, NX)
    def _(block):
        x = tok[block].astype(F32)
        mean = jnp.mean(x, axis=1, keepdims=True)
        centred = x - mean
        inverse = lax.rsqrt(jnp.mean(centred * centred, axis=1, keepdims=True) + EPSILON)
        normed = centred * inverse
        shift = jnp.where(is0, mod[0:1, :width], mod[1:2, :width])
        gain = 1.0 + jnp.where(is0, mod[0:1, width:], mod[1:2, width:])
        value = jnp.where(usable, gain * normed + shift, 0.0).astype(BF16)
        at = pl.ds(pl.multiple_of(block * rows, rows), rows)
        modded[at, :] = value
        stats[at, 0:1] = mean
        stats[at, 1:2] = inverse

    low[...] = jnp.dot(modded[...], down[...], preferred_element_type=F32).astype(BF16)

    @pl.loop(0, 3)
    def _(n):
        at = pl.ds(pl.multiple_of(n * att, 128), att)
        proj[:, at] = (
            jnp.dot(modded[...], w[:, at], preferred_element_type=F32)
            + jnp.dot(low[...], up[:, at], preferred_element_type=F32)
        ).astype(BF16)

    kv_grad[...] = jnp.zeros_like(kv_grad)

    @pl.loop(0, NX)
    def _(block):
        at = pl.ds(pl.multiple_of(block * rows, rows), rows)
        allowed = (label == key_label[0:1]) & (key_label[0:1] < 2)
        for h in range(heads):
            c = slice(h * 128, (h + 1) * 128)
            q = proj[at, c]
            k = proj[:, att + h * 128 : att + (h + 1) * 128]
            v = proj[:, 2 * att + h * 128 : 2 * att + (h + 1) * 128]
            scores = jnp.where(allowed, nt(q, k) * scale, MASKED)
            largest = jnp.max(scores, axis=1, keepdims=True)
            raw = jnp.exp(scores - largest)
            probs = raw * (1.0 / jnp.sum(raw, axis=1, keepdims=True))
            probs_low = probs.astype(BF16)
            out = jnp.where(usable, jnp.dot(probs_low, v, preferred_element_type=F32), 0.0).astype(BF16)
            attn[block, :, c] = out
            out_grad = jnp.where(usable, cot[block, :, c].astype(F32), 0.0)
            delta = jnp.sum(out_grad * out.astype(F32), axis=1, keepdims=True)
            out_grad = out_grad.astype(BF16)
            score_grads = (probs * (nt(out_grad, v) - delta) * scale).astype(BF16)
            proj_grad[at, c] = jnp.dot(score_grads, k, preferred_element_type=F32).astype(BF16)
            kv_grad[:, h * 128 : (h + 1) * 128] += tn(score_grads, q)
            kv_grad[:, att + h * 128 : att + (h + 1) * 128] += tn(probs_low, out_grad)

    proj_grad[:, att:] = kv_grad[...].astype(BF16)
    low_grad[...] = nt(proj_grad[...], up[...]).astype(BF16)

    one_hot = jnp.where(
        key_label == lax.broadcasted_iota(jnp.int32, key_label.shape, 0), 1.0, 0.0
    )
    one_hot = jnp.where(key_label < 2, one_hot, 0.0).astype(BF16)

    for n in range(width // att):
        f = slice(n * att, (n + 1) * att)
        grad = nt(proj_grad[...], w[f, :]) + nt(low_grad[...], down[f, :])
        grad_low = grad.astype(BF16)
        for block in range(NX):
            pg[block, :, f] = grad_low[block * rows : (block + 1) * rows]
        x = tok[:, :, f].reshape(NX * rows, att).astype(F32)
        normed = (x - stats[:, 0:1]) * stats[:, 1:2]
        ip[:, f] = jnp.dot(one_hot, grad_low, preferred_element_type=F32)
        ip[:, width + n * att : width + (n + 1) * att] = jnp.dot(
            one_hot, (grad * normed).astype(BF16), preferred_element_type=F32
        )

    up_total = tn(low[...], proj_grad[...])
    for t in range(3 * heads):
        up_part[t * 64 : (t + 1) * 64, :] = up_total[:, t * 128 : (t + 1) * 128]
    down_total = tn(low_grad[...], modded[...])
    for t in range(width // 128):
        down_part[t * 64 : (t + 1) * 64, :] = down_total[:, t * 128 : (t + 1) * 128]


def local_all(counts, tok, mod, cot, w, down, up):
    _, rows, width = tok.shape
    att = cot.shape[2]
    all_rows = NX * rows
    return pl.pallas_call(
        local_kernel,
        out_shape=(
            jax.ShapeDtypeStruct((NX, rows, att), BF16),
            jax.ShapeDtypeStruct((NX, rows, width), BF16),
            jax.ShapeDtypeStruct((8, 2 * width), F32),
            jax.ShapeDtypeStruct((3 * att // 2, 128), F32),
            jax.ShapeDtypeStruct((width // 2, 128), F32),
        ),
        in_specs=[pl.BlockSpec(memory_space=pltpu.SMEM)] + [VM] * 6,
        out_specs=(VM,) * 5,
        scratch_shapes=[
            pltpu.VMEM((all_rows, width), BF16),
            pltpu.VMEM((all_rows, 128), F32),
            pltpu.VMEM((all_rows, 64), BF16),
            pltpu.VMEM((all_rows, 3 * att), BF16),
            pltpu.VMEM((all_rows, 3 * att), BF16),
            pltpu.VMEM((all_rows, 2 * att), F32),
            pltpu.VMEM((all_rows, 64), BF16),
        ],
        compiler_params=pltpu.CompilerParams(vmem_limit_bytes=56 * 1024 * 1024),
        name="local_all",
    )(counts, tok, mod, cot, w, down, up)


def scatter_kernel(
    pg, attn, ip, up_part, down_part,
    grad, attn_out, ig_all, trip,
    half_l, half_r, comb_l, comb_r, from_l, from_r,
    ip_in, own_ig, lora, down_in, y_in, plane, z_in, own_piece, core_in,
    gsend, grecv, osend, orecv, lsem,
    ips, ipr, gys, gyr, gzs, gzr, gcs, gcr,
    dxs, dxr, lys, lyr, lzs, lzr, lcs, lcr, lgs, lgr, lxs, lxr,
):
    me = Place()
    s, y, z = me.s, me.y, me.z
    rows = pg.shape[1]
    half = rows // 2
    head_cols = attn.shape[2]
    first, second = pl.ds(0, half), pl.ds(half, half)
    sl, sr, so = (s + NX - 1) % NX, (s + 1) % NX, (s + 2) % NX
    right, left = me.at(dx=1), me.at(dx=NX - 1)
    enter(me)

    ip_sent = exchange(me, "dx", NX, lambda i: ip, ip_in, ips, ipr)
    down_sent = exchange(me, "dx", NX, lambda i: down_part.at[(NX - 1) - (s + i) % NX], down_in, dxs, dxr)

    def grad_copy(src, dst, slot, there):
        copy = remote(src, dst, gsend.at[slot], grecv.at[slot], there)
        copy.start()
        return copy

    step1_r = grad_copy(pg.at[so, first], half_l, 0, right)
    step1_l = grad_copy(pg.at[so, second], half_r, 1, left)
    plain_r = grad_copy(pg.at[sr, second], from_l.at[second], 2, right)
    plain_l = grad_copy(pg.at[sl, first], from_r.at[first], 3, left)

    out_sent = []
    columns = pl.ds(pl.multiple_of(s * head_cols, 128), head_cols)
    for i in range(1, NX):
        there = me.at(dx=i)
        copy = remote(attn.at[there[1]], attn_out.at[:, columns], osend.at[i - 1], orecv.at[i - 1], there)
        copy.start()
        out_sent.append(copy)
    own_out = pltpu.make_async_copy(attn.at[s], attn_out.at[:, columns], lsem)
    own_out.start()

    finish(ip_sent)
    own_ig[...] = (ip[...] + ip_in[0] + ip_in[1] + ip_in[2]).astype(BF16)
    ig_all[me.c, z, y] = own_ig[...]
    images = PlaneGather(me, ig_all, gys, gyr, gzs, gzr, gcs, gcr)
    images.start_y(own_ig)

    finish(down_sent)
    lora[0:3] = up_part[...]
    lora[3] = down_part[(NX - 1) - s] + down_in[0] + down_in[1] + down_in[2]

    def triple(there):
        step = (s + there) % 4
        down = step // 3
        return ((3 * there + step) // 4) * (1 - down) + 3 * down

    y_sent = exchange(me, "dy", NY, lambda i: lora.at[triple((y + i) % NY)], y_in, lys, lyr)
    images.wait_y()
    images.step(1)
    finish(y_sent)
    plane[...] = (lora[triple(y)] + y_in[0] + y_in[1] + y_in[2]).reshape(plane.shape)
    z_sent = exchange(me, "dz", NZ, lambda i: plane.at[(z + i) % NZ], z_in, lzs, lzr)
    images.step(2)

    step1_r.wait_recv()
    comb_r[...] = (pg[sr, 0:half].astype(F32) + half_l[...].astype(F32)).astype(BF16)
    comb_copy_r = grad_copy(comb_r, from_l.at[first], 4, right)
    step1_l.wait_recv()
    comb_l[...] = (pg[sl, half:rows].astype(F32) + half_r[...].astype(F32)).astype(BF16)
    comb_copy_l = grad_copy(comb_l, from_r.at[second], 5, left)

    images.step(3)
    finish(z_sent)
    total = plane[z]
    for i in range(NZ - 1):
        total += z_in[i]
    own_piece[0] = total
    core_copy = remote(own_piece.at[0], core_in, lcs, lcr, me.at(flip=True))
    core_copy.start()
    images.step(4)
    core_copy.wait()
    own_piece[1] = own_piece[0] + core_in[...]
    trip[s, z] = own_piece[1]
    piece_sent = []
    for i in range(1, NZ):
        copy = remote(own_piece.at[1], trip.at[s, z], lgs.at[i - 1], lgr.at[i - 1], me.at(dz=i))
        copy.start()
        piece_sent.append(copy)
    images.step(5)
    finish(piece_sent)
    trip_sent = []
    for i in range(1, NX):
        copy = remote(trip.at[s], trip.at[s], lxs.at[i - 1], lxr.at[i - 1], me.at(dx=i))
        copy.start()
        trip_sent.append(copy)
    images.wait_cross()

    plain_r.wait_recv()
    plain_l.wait_recv()
    comb_copy_r.wait_recv()
    comb_copy_l.wait_recv()
    grad[...] = pg[s].astype(F32) + from_l[...].astype(F32) + from_r[...].astype(F32)

    for copy in (step1_r, step1_l, plain_r, plain_l, comb_copy_r, comb_copy_l):
        copy.wait_send()
    finish(out_sent)
    own_out.wait()
    finish(trip_sent)
    images.drain()


def scatter_all(pg, attn, ip, up_part, down_part):
    _, rows, width = pg.shape
    dma = pltpu.SemaphoreType.DMA
    half = rows // 2
    return pl.pallas_call(
        scatter_kernel,
        out_shape=(
            jax.ShapeDtypeStruct((rows, width), F32),
            jax.ShapeDtypeStruct((rows, width), BF16),
            jax.ShapeDtypeStruct((NC, NZ, NY, 48, 128), BF16),
            jax.ShapeDtypeStruct((NX, NZ, 24, 128), F32),
        ),
        in_specs=[VM, VM, VM, VM, VM],
        out_specs=(VM, ANY, VM, VM),
        scratch_shapes=[
            pltpu.VMEM((half, width), BF16),
            pltpu.VMEM((half, width), BF16),
            pltpu.VMEM((half, width), BF16),
            pltpu.VMEM((half, width), BF16),
            pltpu.VMEM((rows, width), BF16),
            pltpu.VMEM((rows, width), BF16),
            pltpu.VMEM((3, 48, 128), F32),
            pltpu.VMEM((48, 128), BF16),
            pltpu.VMEM((4, 192, 128), F32),
            pltpu.VMEM((3, 192, 128), F32),
            pltpu.VMEM((3, 192, 128), F32),
            pltpu.VMEM((NZ, 24, 128), F32),
            pltpu.VMEM((NZ - 1, 24, 128), F32),
            pltpu.VMEM((2, 24, 128), F32),
            pltpu.VMEM((24, 128), F32),
            dma((6,)), dma((6,)), dma((3,)), dma((3,)), dma,
            dma((3,)), dma((3,)),
            *plane_sems(),
            dma((3,)), dma((3,)), dma((3,)), dma((3,)), dma((7,)), dma((7,)),
            dma, dma, dma((7,)), dma((7,)), dma((3,)), dma((3,)),
        ],
        compiler_params=pltpu.CompilerParams(
            collective_id=2, has_side_effects=True, vmem_limit_bytes=32 * 1024 * 1024
        ),
        name="scatter_all",
    )(pg, attn, ip, up_part, down_part)


def tail_kernel(counts, grad, tok, mod, act, ig, token_grad, mod_grad, wide):
    rows, width = tok.shape
    c0, c1 = counts[0], counts[1]
    label = labels_of(lax.broadcasted_iota(jnp.int32, (rows, 1), 0), c0, c1)
    x = tok[...].astype(F32)
    centred = x - jnp.mean(x, axis=1, keepdims=True)
    inverse = lax.rsqrt(jnp.mean(centred * centred, axis=1, keepdims=True) + EPSILON)
    normed = centred * inverse
    gain = 1.0 + jnp.where(label == 0, mod[0:1, width:], mod[1:2, width:])
    g = jnp.where(label < 2, gain * grad[...], 0.0)
    token_grad[...] = (
        inverse
        * (
            g
            - jnp.mean(g, axis=1, keepdims=True)
            - normed * jnp.mean(g * normed, axis=1, keepdims=True)
        )
    ).astype(BF16)
    wide[...] = ig[...].astype(F32)
    for j in range(24):
        total = jnp.zeros((128, 128), F32)
        for img in range(2):
            part = wide[pl.ds(img * 24 + j, 64, stride=48), :].astype(BF16)
            total += tn(act[img * 64 : (img + 1) * 64], part)
        mod_grad[:, j * 128 : (j + 1) * 128] = total[0:48]


def tail_all(counts, grad, tok, mod, act, ig):
    rows, width = tok.shape
    return pl.pallas_call(
        tail_kernel,
        out_shape=(
            jax.ShapeDtypeStruct((rows, width), BF16),
            jax.ShapeDtypeStruct((48, 3072), F32),
        ),
        in_specs=[pl.BlockSpec(memory_space=pltpu.SMEM)] + [VM] * 5,
        out_specs=(VM, VM),
        scratch_shapes=[pltpu.VMEM((3072, 128), F32)],
        compiler_params=pltpu.CompilerParams(vmem_limit_bytes=32 * 1024 * 1024),
        name="tail_all",
    )(counts, grad, tok, mod, act, ig)


def body(
    tokens,
    cotangent,
    condition,
    per_image_rows,
    query_key_value_weight,
    adapter_down,
    adapter_up,
    modulation_matrix,
):
    dp = lax.axis_index("dp")
    s = lax.axis_index("seq")
    y, place = dp // (NZ * NC), dp % (NZ * NC)
    tok, cot = tokens[0], cotangent[0]
    width = tok.shape[1]
    att = cot.shape[1] // NX

    def head_columns(matrix):
        shaped = matrix.reshape(matrix.shape[0], 3, NX, att)
        return lax.dynamic_index_in_dim(shaped, s, 2, keepdims=False)

    counts = lax.dynamic_index_in_dim(per_image_rows, dp, 0, keepdims=False)
    act = jax.nn.silu(condition[0].astype(F32)).astype(BF16).reshape(48, 128)
    mm = lax.dynamic_slice_in_dim(modulation_matrix, s * 768, 768, 1)
    mm = jnp.pad(mm, ((0, 128 - mm.shape[0]), (0, 0)))
    shard_rows = query_key_value_weight.shape[0]
    wsh = head_columns(query_key_value_weight).reshape(shard_rows, 9, 128)
    wsh = wsh.transpose(1, 0, 2).reshape(9 * shard_rows, 128)
    wsh = jnp.pad(wsh, ((0, 224 - 9 * shard_rows), (0, 0)))
    up = head_columns(adapter_up).reshape(64, 3 * att)

    tok_all, cot_all, w_all, mod_all, act_own = gather_all(tok, cot, wsh, act, mm)

    w = w_all[:, :, :, : 9 * shard_rows].reshape(NC, NZ, NY, 9, shard_rows, 128)
    w = w.transpose(2, 1, 0, 4, 3, 5).reshape(width, 3 * att)
    mod = mod_all[:, :12].reshape(NX, 2, 768).transpose(1, 0, 2).reshape(2, 2 * width)
    mod = jnp.pad(mod, ((0, 6), (0, 0)))

    attn, pg, ip, up_part, down_part = local_all(counts, tok_all, mod, cot_all, w, adapter_down, up)

    grad, attention, ig_all, trip = scatter_all(
        pg,
        attn,
        ip[:2].reshape(48, 128),
        up_part.reshape(3, 192, 128),
        down_part.reshape(4, 192, 128),
    )
    token_grad, mod_grad = tail_all(counts, grad, tok, mod, act_own, ig_all.reshape(3072, 128))

    trip = trip.reshape(NX, 3, 64, 128)
    order = (3 * y + jnp.arange(3)) % 4
    slab = trip[order].reshape(9, 64, 128).transpose(1, 0, 2).reshape(64, 1152)
    up_grad = lax.dynamic_slice_in_dim(slab, place * 72, 72, 1)
    down = lax.dynamic_index_in_dim(trip, 3 - y, 0, keepdims=False)
    down = down.transpose(1, 0, 2).reshape(64, 384)
    down_grad = lax.dynamic_slice_in_dim(down, place * 24, 24, 1).T
    return attention[None], token_grad[None], down_grad, up_grad, mod_grad


def solution(mesh):
    in_specs = (
        P("dp", "seq", None),
        P("dp", "seq", None),
        P("dp", None, None),
        P(),
        P("dp", None),
        P(),
        P(),
        P("dp", None),
    )
    out_specs = (
        P("dp", "seq", None),
        P("dp", "seq", None),
        P("dp", None),
        P(None, "dp"),
        P("dp", None),
    )
    return jax.shard_map(body, mesh=mesh, in_specs=in_specs, out_specs=out_specs, check_vma=False)
```

time: 1130 us -> 162 us (0.14)
  waiting for transfers between devices: 766 us -> 0 us
  blocking collectives: 161 us -> 0 us
  Pallas kernels: 0 us -> 131 us
  matrix products: 65.9 us -> 0 us
  local copies, waits for them, and re-layouts: 59.4 us -> 29.7 us
  other arithmetic: 25.5 us -> 0.04 us
  starting transfers between devices: 22.9 us -> 0 us
  between operations: 18.5 us -> 0.88 us
    unnamed x11 -> x0, waiting for transfers between devices: 492 us -> none
    all_gather x5 -> x0, waiting for transfers between devices: 189 us -> none  [the longest x1 78 us: body(): lax.all_gather(image_grad, 'dp', axis=0, tiled=True)]
    pallas_call x0 -> x4, Pallas kernels: none -> 131 us  [the longest x1 52.2 us: gather_all(): pl.pallas_call(gather_kernel, out_shape=(jax.ShapeDtypeStruct((NX, rows,...]
    all_to_all x3 -> x0, waiting for transfers between devices: 84 us -> none  [the longest x1 56.5 us: body(): lax.all_to_all(unpack_rows(bundled_projection, places, live_slots), 'dp',...]
    all_gather x3 -> x0, blocking collectives: 76 us -> none  [the longest x1 55.2 us: body(): all_active = lax.all_gather(activated, 'dp', axis=0, tiled=True)]
    all_to_all x1 -> x0, blocking collectives: 70.1 us -> none  [body(): lax.all_to_all(to_peers(projection_grad, rotation, groups), 'dp', split_a...]
    dot_general x20 -> x0, matrix products: 65.9 us -> none  [the longest x1 9.41 us: body(): jnp.dot(bundled_grads, weight_matrix.T, preferred_element_type=jnp.float32)]
    all_to_all x3 -> x0, starting transfers between devices: 22.2 us -> none  [the longest x1 9.68 us: body(): lax.all_to_all(to_peers(modulated_input, rotation, groups), 'dp', split_a...]
  transfers between devices with their start and end apart: 11 -> 0, of which waited for: 10 -> 0; matrix products, arithmetic and copies ran while one was open for 7% -> 0% of each run, Pallas kernels for 0% -> 0%
where the time goes in v1:
time: 162 us; the launch traced here: 161 us
  Pallas kernels  131 us (81%)
  local copies, waits for them, and re-layouts  29.7 us (18%)
    pallas_call x1, Pallas kernels, gather_all(): pl.pallas_call(gather_kernel, out_shape=(jax.ShapeDtypeStruct((NX, rows,...  52.2 us
    pallas_call x1, Pallas kernels, scatter_all(): pl.pallas_call(scatter_kernel, out_shape=(jax.ShapeDtypeStruct((rows, wid...  42.6 us
    pallas_call x1, Pallas kernels, local_all(): pl.pallas_call(local_kernel, out_shape=(jax.ShapeDtypeStruct((NX, rows, a...  33 us
    unnamed x39, local copies, waits for them, and re-layouts  18.8 us

profile of v1, /device:TPU:1, one launch (start us, length us, event | category | flops | bytes accessed | tf_op | source)
XLA Modules:
  0.0 161.3 jit_solution(11885767278237640257)
XLA Ops:
  0.7 0.9 copy-done
  1.6 1.0 reshape.116
  2.6 0.1 constant_dynamic-slice_fusion.2
  2.9 0.7 reshape.133
  3.7 1.1 copy-done.4
  4.7 1.1 copy-done.9
  5.8 52.2 %gather_all.1 = (bf16[4,192,1536]{2,1,0:T(8,128)(2,1)S(1)}, bf16[4,192,384]{2,1,0:T(8,128)(2,1)S(1)}, bf16[2,8,4,224,128]{4,3,2,1,0:T(8,128)(2,1)S(1)}, f32[4,16,128]{2,1,0:T(8,128)S(1)}, bf16[128,128]{1,0:T(8,128)(2,1)S(1)}) custom-call(bf16[192,1536]{1,0:T(8,128)(2,1)S(1)} %bitcast.43, bf16[192,1536]{1,0:T(8,128)(2,1)S(1)} %bitcast.46, ...), custom_call_target="tpu_custom_call" | custom-call | tf_op jit(solution)/shard_map/gather_all/pallas_call | solution.py:316
  58.0 1.9 %copy-done.1 = bf16[2,8,4,224,128]{4,3,2,1,0:T(8,128)(2,1)} copy-done((bf16[2,8,4,224,128]{4,3,2,1,0:T(8,128)(2,1)}, bf16[2,8,4,224,128]{4,3,2,1,0:T(8,128)(2,1)S(1)}, u32[]{:S(2)}) %copy-start.1) | copy-done | bytes 3670040
  59.8 1.4 copy-done.2
  61.2 0.8 copy-done.7
  62.1 0.6 pad.14.mod
  62.7 2.2 %slice.10 = bf16[2,8,4,216,128]{4,3,2,1,0:T(8,128)(2,1)S(1)} slice(bf16[2,8,4,224,128]{4,3,2,1,0:T(8,128)(2,1)} %copy-done.1), slice={[0:2], [0:8], [0:4], [0:216], [0:128]} | slice | bytes 7077888 | tf_op jit(solution)/shard_map/slice | solution.py:720
  65.0 1.8 %copy.26 = bf16[2,8,4,9,24,128]{5,3,4,0,1,2:T(8,128)(2,1)S(1)} copy(bf16[2,8,4,9,24,128]{5,4,3,2,1,0:T(8,128)(2,1)S(1)} %bitcast.55) | data formatting | bytes 7077888 | tf_op jit(solution)/shard_map/reshape | solution.py:720
  66.8 3.7 %copy.41 = bf16[192,8,9,128]{3,1,2,0:T(8,128)(2,1)} copy(bf16[192,8,9,128]{3,2,1,0:T(8,128)(2,1)S(1)} %bitcast.53) | data formatting | bytes 7077888
  70.5 0.7 fusion.counts
  71.1 0.1 reshape.123
  71.3 1.0 dynamic-slice_reduce_fusion
  72.3 0.7 copy.36
  72.9 0.9 copy.28.down
  73.9 33.0 %local_all.1 = (bf16[4,192,384]{2,1,0:T(8,128)(2,1)}, bf16[4,192,1536]{2,1,0:T(8,128)(2,1)}, f32[8,3072]{1,0:T(8,128)}, f32[576,128]{1,0:T(8,128)}, f32[768,128]{1,0:T(8,128)}) custom-call(s32[2]{0:T(128)} %fusion.counts, bf16[4,192,1536]{2,1,0:T(8,128)(2,1)} %copy-done.2, f32[8,3072]{1,0:T(8,128)} %pad.14.mod, bf16[4,192,384]{2,1,0:T(8,128)(2,1)} %copy-done.7, ...), custom_call_target="tpu_custom_call" | custom-call | tf_op jit(solution)/shard_map/local_all/pallas_call | solution.py:464
  106.9 0.9 slice.11
  107.9 1.7 %copy-done.3 = bf16[4,192,1536]{2,1,0:T(8,128)(2,1)S(1)} copy-done((bf16[4,192,1536]{2,1,0:T(8,128)(2,1)S(1)}, bf16[4,192,1536]{2,1,0:T(8,128)(2,1)}, u32[]{:S(2)}) %copy-start.3) | copy-done | bytes 2359320
  109.5 1.1 copy-done.8
  110.6 1.0 copy-done.10
  111.6 1.0 copy-done.11
  112.5 42.6 %scatter_all.1 = (f32[192,1536]{1,0:T(8,128)S(1)}, bf16[192,1536]{1,0:T(8,128)(2,1)S(1)}, bf16[2,8,4,48,128]{4,3,2,1,0:T(8,128)(2,1)S(1)}, f32[4,8,24,128]{3,2,1,0:T(8,128)S(1)}) custom-call(bf16[4,192,1536]{2,1,0:T(8,128)(2,1)S(1)} %copy-done.3, bf16[4,192,384]{2,1,0:T(8,128)(2,1)S(1)} %copy-done.8, f32[48,128]{1,0:T(8,128)S(1)} %reshape.125.ip, ...), custom_call_target="tpu_custom_call" | custom-call | tf_op jit(solution)/shard_map/scatter_all/pallas_call | solution.py:605
  155.2 2.9 %tail_all.1 = (bf16[192,1536]{1,0:T(8,128)(2,1)}, f32[48,3072]{1,0:T(8,128)}) custom-call(s32[2]{0:T(128)S(1)} %copy-done.12, f32[192,1536]{1,0:T(8,128)S(1)} %get-tuple-element.31.grad, bf16[192,1536]{1,0:T(8,128)(2,1)S(1)} %bitcast.44, f32[8,3072]{1,0:T(8,128)S(1)} %copy-done.6, bf16[128,128]{1,0:T(8,128)(2,1)S(1)} %get-tuple-element.32.act, ...), custom_call_target="tpu_custom_call" | custom-call | tf_op jit(solution)/shard_map/tail_all/pallas_call | solution.py:673
  158.1 0.6 gather_fusion
  158.7 0.2 copy.30
  159.0 0.7 constant_dynamic-slice_fusion
  159.8 0.7 copy.31
  160.5 0.8 copy.44
  (36 shorter events, 0.5 us)
Async XLA Ops:
  0.6 1.0 copy-start
  3.6 1.1 copy-start.4
  4.7 1.1 copy-start.9
  57.9 1.9 %copy-start.1 = (bf16[2,8,4,224,128]{4,3,2,1,0:T(8,128)(2,1)}, bf16[2,8,4,224,128]{4,3,2,1,0:T(8,128)(2,1)S(1)}, u32[]{:S(2)}) copy-start(bf16[2,8,4,224,128]{4,3,2,1,0:T(8,128)(2,1)S(1)} %get-tuple-element.24) | copy-start | bytes 11010052
  59.8 1.4 copy-start.2
  61.2 0.8 copy-start.7
  66.8 3.7 %copy-start.15 = (s32[64,2]{0,1:T(2,128)S(1)}, s32[64,2]{0,1:T(2,128)}, u32[]{:S(2)}) copy-start(s32[64,2]{0,1:T(2,128)} %param.11) | copy-start | bytes 1540
  66.8 4.4 %copy-start.13 = (bf16[64,4608]{1,0:T(8,128)(2,1)S(1)}, bf16[64,4608]{1,0:T(8,128)(2,1)}, u32[]{:S(2)}) copy-start(bf16[64,4608]{1,0:T(8,128)(2,1)} %param.14) | copy-start | bytes 1769476
  66.8 6.2 %copy-start.14 = (bf16[1536,64]{0,1:T(8,128)(2,1)S(1)}, bf16[1536,64]{0,1:T(8,128)(2,1)}, u32[]{:S(2)}) copy-start(bf16[1536,64]{0,1:T(8,128)(2,1)} %param.13) | copy-start | bytes 589828
  73.9 81.3 %copy-start.5 = (bf16[1,192,1536]{2,1,0:T(8,128)(2,1)S(1)}, bf16[1,192,1536]{2,1,0:T(8,128)(2,1)}, u32[]{:S(2)}) copy-start(bf16[1,192,1536]{2,1,0:T(8,128)(2,1)} %param.8) | copy-start | bytes 1769476
  106.9 48.3 %copy-start.6 = (f32[8,3072]{1,0:T(8,128)S(1)}, f32[8,3072]{1,0:T(8,128)}, u32[]{:S(2)}) copy-start(f32[8,3072]{1,0:T(8,128)} %pad.14.mod) | copy-start | bytes 294916
  106.9 48.3 %copy-start.12 = (s32[2]{0:T(128)S(1)}, s32[2]{0:T(128)}, u32[]{:S(2)}) copy-start(s32[2]{0:T(128)} %fusion.counts) | copy-start | bytes 28
  107.8 1.7 %copy-start.3 = (bf16[4,192,1536]{2,1,0:T(8,128)(2,1)S(1)}, bf16[4,192,1536]{2,1,0:T(8,128)(2,1)}, u32[]{:S(2)}) copy-start(bf16[4,192,1536]{2,1,0:T(8,128)(2,1)} %get-tuple-element.25.pg) | copy-start | bytes 7077892
  109.5 1.1 copy-start.8
  110.6 1.0 copy-start.10
  111.6 1.0 copy-start.11

commit v2 on v0

v2 whole, which is shorter than its diff:
```python
import jax
import jax.numpy as jnp
from jax import lax
from jax.experimental import pallas as pl
from jax.experimental.pallas import tpu as pltpu
from jax.sharding import PartitionSpec as P

HEAD_SIZE = 128
EPSILON = 1e-06
MASKED = -1e30
MESH = pl.DeviceIdType.MESH
NX, NY, NZ, NC = 4, 4, 8, 2
F32, BF16 = jnp.float32, jnp.bfloat16
ANY = pl.BlockSpec(memory_space=pl.ANY)
VM = pl.BlockSpec(memory_space=pltpu.VMEM)


def remote(src, dst, send_sem, recv_sem, device):
    return pltpu.make_async_remote_copy(
        src_ref=src,
        dst_ref=dst,
        send_sem=send_sem,
        recv_sem=recv_sem,
        device_id=device,
        device_id_type=MESH,
    )


class Place:
    def __init__(self):
        self.dp = lax.axis_index("dp")
        self.s = lax.axis_index("seq")
        self.y = self.dp // (NZ * NC)
        self.z = (self.dp // NC) % NZ
        self.c = self.dp % NC

    def at(self, dx=0, dy=0, dz=0, flip=False):
        s = (self.s + dx) % NX if dx else self.s
        y = (self.y + dy) % NY if dy else self.y
        z = (self.z + dz) % NZ if dz else self.z
        c = 1 - self.c if flip else self.c
        return (y * (NZ * NC) + z * NC + c, s)


def enter(me):
    barrier = pltpu.get_barrier_semaphore()
    peers = [me.at(dx=i) for i in range(1, NX)]
    peers += [me.at(dy=i) for i in range(1, NY)]
    peers += [me.at(dz=i) for i in range(1, NZ)]
    peers += [me.at(flip=True)]
    for peer in peers:
        pl.semaphore_signal(barrier, inc=1, device_id=peer, device_id_type=MESH)
    pl.semaphore_wait(barrier, len(peers))


class PlaneGather:
    def __init__(self, me, buf, ysend, yrecv, zsend, zrecv, csend, crecv):
        self.me, self.buf = me, buf
        self.ysend, self.yrecv = ysend, yrecv
        self.zsend, self.zrecv = zsend, zrecv
        self.csend, self.crecv = csend, crecv
        self.sent = []

    def start_y(self, own):
        me = self.me
        for i in range(1, NY):
            copy = remote(
                own, self.buf.at[me.c, me.z, me.y], self.ysend.at[i - 1], self.yrecv.at[i - 1], me.at(dy=i)
            )
            copy.start()
            self.sent.append(copy)

    def wait_y(self):
        me = self.me
        for i in range(1, NY):
            place = self.buf.at[me.c, me.z, (me.y + NY - i) % NY]
            remote(place, place, self.ysend.at[i - 1], self.yrecv.at[i - 1], me.at(dy=i)).wait_recv()

    def ring(self, way, step, part):
        me = self.me
        if way == 0:
            source, there = (me.z + NZ - step + 1) % NZ, me.at(dz=1)
        else:
            source, there = (me.z + step - 1) % NZ, me.at(dz=NZ - 1)
        block = self.buf.at[me.c, source, part]
        at = (way * 4 + step - 1) * NY + part
        return remote(block, block, self.zsend.at[at], self.zrecv.at[at], there)

    def arrive(self, way, step, part):
        me = self.me
        source = (me.z + NZ - step) % NZ if way == 0 else (me.z + step) % NZ
        block = self.buf.at[me.c, source, part]
        at = (way * 4 + step - 1) * NY + part
        there = me.at(dz=1) if way == 0 else me.at(dz=NZ - 1)
        remote(block, block, self.zsend.at[at], self.zrecv.at[at], there).wait_recv()

    def carried(self, way, step, part):
        return step < 4 or (part // 2) == way

    def step(self, step):
        for turn in range(NY):
            for way in (0, 1):
                part = turn if way == 0 else NY - 1 - turn
                if step > 1 and self.carried(way, step - 1, part):
                    self.arrive(way, step - 1, part)
                if step <= 4 and self.carried(way, step, part):
                    copy = self.ring(way, step, part)
                    copy.start()
                    self.sent.append(copy)
        if step == 1:
            self.cross(0)
        elif step == 5:
            self.cross(4)
        else:
            self.cross(step - 1)
            self.cross(NZ - step + 1)

    def cross(self, shift):
        me = self.me
        block = self.buf.at[me.c, (me.z + shift) % NZ]
        copy = remote(block, block, self.csend.at[shift], self.crecv.at[shift], me.at(flip=True))
        copy.start()
        self.sent.append(copy)

    def wait_cross(self):
        me = self.me
        for shift in range(NZ):
            block = self.buf.at[1 - me.c, (me.z + shift) % NZ]
            remote(block, block, self.csend.at[shift], self.crecv.at[shift], me.at(flip=True)).wait_recv()

    def drain(self):
        for copy in self.sent:
            copy.wait_send()


def plane_sems():
    return [
        pltpu.SemaphoreType.DMA((NY - 1,)),
        pltpu.SemaphoreType.DMA((NY - 1,)),
        pltpu.SemaphoreType.DMA((8 * NY,)),
        pltpu.SemaphoreType.DMA((8 * NY,)),
        pltpu.SemaphoreType.DMA((NZ,)),
        pltpu.SemaphoreType.DMA((NZ,)),
    ]


def exchange(me, axis, count, source, slots, send, recv):
    copies = []
    for i in range(1, count):
        copy = remote(source(i), slots.at[i - 1], send.at[i - 1], recv.at[i - 1], me.at(**{axis: i}))
        copy.start()
        copies.append(copy)
    return copies


def finish(copies):
    for copy in copies:
        copy.wait()


def exchange_at(me, axis, count, source, target, send, recv):
    copies = []
    for i in range(1, count):
        copy = remote(source(i), target, send.at[i - 1], recv.at[i - 1], me.at(**{axis: i}))
        copy.start()
        copies.append(copy)
    return copies


def nt(a, b):
    return lax.dot_general(a, b, (((1,), (1,)), ((), ())), preferred_element_type=F32)


def tn(a, b):
    return lax.dot_general(a, b, (((0,), (0,)), ((), ())), preferred_element_type=F32)


def nn(a, b):
    return jnp.dot(a, b, preferred_element_type=F32)


def labels_of(rank, c0, c1):
    return (rank >= c0).astype(jnp.int32) + (rank >= c0 + c1).astype(jnp.int32)


def aligned(start, size):
    return pl.ds(pl.multiple_of(start, 128), size)


class Refs:
    pass


SCRATCH = dict(
    tok_all=pltpu.VMEM((NX, 192, 1536), BF16),
    cot_all=pltpu.VMEM((NX, 192, 384), BF16),
    w_all=pltpu.VMEM((NC, NZ, NY, 224, 128), BF16),
    w=pltpu.VMEM((1536, 1152), BF16),
    up=pltpu.VMEM((64, 1152), BF16),
    down=pltpu.VMEM((64, 1536), BF16),
    mm=pltpu.VMEM((128, 768), BF16),
    a_z=pltpu.VMEM((NZ, NY, 8, 128), F32),
    a_y=pltpu.VMEM((NC, NZ, NY, 8, 128), F32),
    a_wide=pltpu.VMEM((512, 128), F32),
    a_own=pltpu.VMEM((128, 128), BF16),
    part_wide=pltpu.VMEM((1024, 128), F32),
    part_low=pltpu.VMEM((NC, NZ, NY, 16, 128), BF16),
    m_core=pltpu.VMEM((NZ, NY, 16, 128), BF16),
    m_sum=pltpu.VMEM((NZ, NY, 16, 128), BF16),
    m_y=pltpu.VMEM((NY - 1, NZ, 16, 128), BF16),
    m_plane=pltpu.VMEM((NZ, 16, 128), F32),
    m_z=pltpu.VMEM((NZ - 1, 16, 128), F32),
    m_own=pltpu.VMEM((16, 128), F32),
    m_all=pltpu.VMEM((NX, 16, 128), F32),
    mod=pltpu.VMEM((8, 3072), F32),
    modded=pltpu.VMEM((768, 1536), BF16),
    stats=pltpu.VMEM((768, 128), F32),
    low=pltpu.VMEM((768, 64), BF16),
    proj=pltpu.VMEM((768, 1152), BF16),
    proj_grad=pltpu.VMEM((768, 1152), BF16),
    kv_grad=pltpu.VMEM((768, 768), F32),
    low_grad=pltpu.VMEM((768, 64), BF16),
    attn=pltpu.VMEM((NX, 192, 384), BF16),
    pg=pltpu.VMEM((NX, 192, 1536), BF16),
    ip=pltpu.VMEM((8, 3072), F32),
    half_l=pltpu.VMEM((96, 1536), BF16),
    half_r=pltpu.VMEM((96, 1536), BF16),
    comb_l=pltpu.VMEM((96, 1536), BF16),
    comb_r=pltpu.VMEM((96, 1536), BF16),
    from_l=pltpu.VMEM((192, 1536), BF16),
    from_r=pltpu.VMEM((192, 1536), BF16),
    ip_own=pltpu.VMEM((48, 128), F32),
    ip_in=pltpu.VMEM((3, 48, 128), F32),
    ig_all=pltpu.VMEM((NC, NZ, NY, 48, 128), BF16),
    ig_wide=pltpu.VMEM((3072, 128), F32),
    lora=pltpu.VMEM((4, 192, 128), F32),
    down_part=pltpu.VMEM((4, 192, 128), F32),
    down_in=pltpu.VMEM((3, 192, 128), F32),
    l_y=pltpu.VMEM((3, 192, 128), F32),
    l_plane=pltpu.VMEM((NZ, 24, 128), F32),
    l_z=pltpu.VMEM((NZ - 1, 24, 128), F32),
    l_own=pltpu.VMEM((2, 24, 128), F32),
    l_core=pltpu.VMEM((24, 128), F32),
    trip=pltpu.VMEM((NX, NZ, 24, 128), F32),
)
PAIRS = dict(tk=12, ck=3, az=7, ay=3, ac=1, mc=1, my=3, mz=7, mx=3, gr=6, ot=3, ip=3, dx=3, ly=3, lz=7, lc=1, lg=7, lx=3)
PLANES = dict(wp=1, gp=1)
LOCAL = 8


def scratch_list():
    dma = pltpu.SemaphoreType.DMA
    out = list(SCRATCH.values())
    for count in PAIRS.values():
        out += [dma((count,)), dma((count,))]
    for _ in PLANES:
        out += plane_sems()
    return out + [dma((LOCAL,))]


def named(refs):
    r = Refs()
    refs = list(refs)
    for name in SCRATCH:
        setattr(r, name, refs.pop(0))
    for name in PAIRS:
        setattr(r, name + "_s", refs.pop(0))
        setattr(r, name + "_r", refs.pop(0))
    for name in PLANES:
        setattr(r, name, [refs.pop(0) for _ in range(6)])
    r.local = refs.pop(0)
    return r


def whole_kernel(
    rows_ref, tok, cot, act, wq, up_in, down_in, mm_in,
    attn_out, token_grad, down_out, up_out, mod_grad,
    *refs,
):
    r = named(refs)
    me = Place()
    s, y, z, c = me.s, me.y, me.z, me.c
    rows, width, att, heads = 192, 1536, 384, 3
    chunk = rows // 4
    scale = HEAD_SIZE ** (-0.5)
    right, left = me.at(dx=1), me.at(dx=NX - 1)
    sl, sr, so = (s + NX - 1) % NX, (s + 1) % NX, (s + 2) % NX
    c0, c1 = rows_ref[me.dp, 0], rows_ref[me.dp, 1]

    r.mm[...] = jnp.zeros_like(r.mm)
    locals_ = [
        pltpu.make_async_copy(tok, r.tok_all.at[s], r.local.at[0]),
        pltpu.make_async_copy(cot.at[:, aligned(s * att, att)], r.cot_all.at[s], r.local.at[1]),
        pltpu.make_async_copy(
            mm_in.at[:, aligned(s * 768, 768)], r.mm.at[pl.ds(pl.multiple_of(48 * c, 16), 48)], r.local.at[2]
        ),
        pltpu.make_async_copy(down_in, r.down, r.local.at[3]),
    ]
    for b in range(3):
        locals_.append(
            pltpu.make_async_copy(
                up_in.at[:, aligned(b * width + s * att, att)], r.up.at[:, b * att : (b + 1) * att], r.local.at[4 + b]
            )
        )
    for copy in locals_:
        copy.start()
    pieces = []
    for b in range(3):
        block = wq[:, aligned(b * width + s * att, att)].astype(F32)
        pieces += [block[:, i * 128 : (i + 1) * 128] for i in range(3)]
    pieces.append(jnp.zeros((8, 128), F32))
    r.w_all[c, z, y] = jnp.concatenate(pieces, axis=0).astype(BF16)
    r.a_z[z] = act[z]

    enter(me)

    az = exchange_at(me, "dz", NZ, lambda i: act.at[(z + i) % NZ], r.a_z.at[z], r.az_s, r.az_r)
    weights = PlaneGather(me, r.w_all, *r.wp)
    weights.start_y(r.w_all.at[c, z, y])

    def row_chunk(i):
        return pl.ds(i * chunk, chunk)

    def token_copy(source, owner, i, slot, there):
        return remote(source, r.tok_all.at[owner, row_chunk(i)], r.tk_s.at[slot], r.tk_r.at[slot], there)

    sent = []

    def launch(copy):
        copy.start()
        sent.append(copy)

    for i in range(4):
        launch(token_copy(tok.at[row_chunk(i)], s, i, i, right))
        launch(token_copy(tok.at[row_chunk(3 - i)], s, 3 - i, 4 + 3 - i, left))

    def forward(i):
        token_copy(tok.at[row_chunk(i)], sl, i, i, right).wait_recv()
        launch(token_copy(r.tok_all.at[sl, row_chunk(i)], sl, i, 8 + i, right))
        j = 3 - i
        token_copy(tok.at[row_chunk(j)], sr, j, 4 + j, left).wait_recv()
        launch(token_copy(r.tok_all.at[sr, row_chunk(j)], sr, j, 8 + j, left))

    finish(az)
    ay = exchange_at(
        me, "dy", NY, lambda i: r.a_z.at[:, (y + i) % NY], r.a_y.at[c, :, y], r.ay_s, r.ay_r
    )
    r.a_y[c, :, y] = r.a_z[:, y]
    weights.wait_y()
    weights.step(1)
    finish(ay)
    ac = remote(r.a_y.at[c], r.a_y.at[c], r.ac_s.at[0], r.ac_r.at[0], me.at(flip=True))
    ac.start()
    forward(0)
    ac.wait()
    locals_[2].wait()
    r.a_wide[...] = r.a_y[...].reshape(512, 128)
    for img in range(2):
        r.a_own[img * 64 : (img + 1) * 64, :] = r.a_wide[pl.ds(img, 64, stride=8), :].astype(BF16)
    r.part_wide[...] = jnp.zeros_like(r.part_wide)
    for j in range(6):
        columns = nn(r.a_own[...], r.mm[:, j * 128 : (j + 1) * 128])
        for img in range(2):
            r.part_wide[pl.ds(img * 6 + j, 64, stride=16), :] = columns[img * 64 : (img + 1) * 64]
    r.part_low[...] = r.part_wide[...].astype(BF16).reshape(r.part_low.shape)
    mc = remote(r.part_low.at[1 - c], r.m_core, r.mc_s.at[0], r.mc_r.at[0], me.at(flip=True))
    mc.start()
    forward(1)
    weights.step(2)
    for i in range(1, NX):
        there = me.at(dx=i)
        launch(
            remote(
                cot.at[:, aligned(there[1] * att, att)], r.cot_all.at[s], r.ck_s.at[i - 1], r.ck_r.at[i - 1], there
            )
        )
    mc.wait()
    r.m_sum[...] = (r.part_low[c].astype(F32) + r.m_core[...].astype(F32)).astype(BF16)
    my = exchange(me, "dy", NY, lambda i: r.m_sum.at[:, (y + i) % NY], r.m_y, r.my_s, r.my_r)
    finish(my)
    total = r.m_sum[:, y].astype(F32)
    for i in range(NY - 1):
        total += r.m_y[i].astype(F32)
    r.m_plane[...] = total
    mz = exchange(me, "dz", NZ, lambda i: r.m_plane.at[(z + i) % NZ], r.m_z, r.mz_s, r.mz_r)
    weights.step(3)
    finish(mz)
    total = r.m_plane[z]
    for i in range(NZ - 1):
        total += r.m_z[i]
    r.m_own[...] = total
    r.m_all[s] = total
    mx = exchange_at(me, "dx", NX, lambda i: r.m_own, r.m_all.at[s], r.mx_s, r.mx_r)
    weights.step(4)

    label = labels_of(lax.broadcasted_iota(jnp.int32, (rows, 1), 0), c0, c1)
    usable = label < 2
    is0 = label == 0
    lane = lax.broadcasted_iota(jnp.int32, (8, NX * rows), 1)
    for _ in range(NX - 1):
        lane = jnp.where(lane >= rows, lane - rows, lane)
    key_label = labels_of(lane, c0, c1)
    key_label = jnp.where(key_label < 2, key_label, 8)

    finish(mx)
    for k in range(NX):
        for img in range(2):
            for j in range(6):
                at = 768 * k + 128 * j
                r.mod[img : img + 1, at : at + 128] = r.m_all[k, img * 6 + j : img * 6 + j + 1, :]

    def normalize(block):
        x = r.tok_all[block].astype(F32)
        mean = jnp.mean(x, axis=1, keepdims=True)
        centred = x - mean
        inverse = lax.rsqrt(jnp.mean(centred * centred, axis=1, keepdims=True) + EPSILON)
        shift = jnp.where(is0, r.mod[0:1, :width], r.mod[1:2, :width])
        gain = 1.0 + jnp.where(is0, r.mod[0:1, width:], r.mod[1:2, width:])
        value = jnp.where(usable, gain * (centred * inverse) + shift, 0.0).astype(BF16)
        at = pl.ds(pl.multiple_of(block * rows, rows), rows)
        r.modded[at, :] = value
        r.stats[at, 0:1] = mean
        r.stats[at, 1:2] = inverse

    locals_[0].wait()
    normalize(s)
    for i in range(4):
        token_copy(tok.at[row_chunk(i)], sl, i, i, right).wait_recv() if i >= 2 else None
    normalize(sl)
    weights.step(5)
    for i in range(4):
        token_copy(tok.at[row_chunk(3 - i)], sr, 3 - i, 4 + 3 - i, left).wait_recv() if i >= 2 else None
    normalize(sr)
    for i in (0, 1):
        token_copy(tok.at[row_chunk(i)], so, i, 8 + i, right).wait_recv()
        token_copy(tok.at[row_chunk(3 - i)], so, 3 - i, 8 + 3 - i, left).wait_recv()
    normalize(so)
    weights.wait_cross()

    @pl.loop(0, NZ * NY)
    def _(pair):
        first = r.w_all[0, pair % NZ, pair // NZ].astype(F32)
        other = r.w_all[1, pair % NZ, pair // NZ].astype(F32)
        at = pl.ds(pl.multiple_of(48 * pair, 16), 48)
        for t in range(9):
            both = jnp.concatenate([first[24 * t : 24 * t + 24], other[24 * t : 24 * t + 24]], axis=0)
            r.w[at, t * 128 : (t + 1) * 128] = both.astype(BF16)

    for copy in locals_[3:]:
        copy.wait()
    r.low[...] = nt(r.modded[...], r.down[...]).astype(BF16)

    @pl.loop(0, 3)
    def _(n):
        at = aligned(n * att, att)
        r.proj[:, at] = (nn(r.modded[...], r.w[:, at]) + nn(r.low[...], r.up[:, at])).astype(BF16)

    r.kv_grad[...] = jnp.zeros_like(r.kv_grad)
    locals_[1].wait()
    for i in range(1, NX):
        remote(
            cot.at[:, aligned(0, att)], r.cot_all.at[(s + NX - i) % NX], r.ck_s.at[i - 1], r.ck_r.at[i - 1], me.at(dx=i)
        ).wait_recv()

    def attend(block):
        at = pl.ds(pl.multiple_of(block * rows, rows), rows)
        allowed = label == key_label[0:1]
        for h in range(heads):
            cols = slice(h * 128, (h + 1) * 128)
            q = r.proj[at, cols]
            k = r.proj[:, att + h * 128 : att + (h + 1) * 128]
            v = r.proj[:, 2 * att + h * 128 : 2 * att + (h + 1) * 128]
            scores = jnp.where(allowed, nt(q, k), MASKED)
            largest = jnp.max(scores, axis=1, keepdims=True)
            raw = jnp.exp((scores - largest) * scale)
            probs = raw * (1.0 / jnp.sum(raw, axis=1, keepdims=True))
            probs_low = probs.astype(BF16)
            out = jnp.where(usable, nn(probs_low, v), 0.0).astype(BF16)
            r.attn[block, :, cols] = out
            out_grad = jnp.where(usable, r.cot_all[block, :, cols].astype(F32), 0.0)
            delta = jnp.sum(out_grad * out.astype(F32), axis=1, keepdims=True)
            out_grad = out_grad.astype(BF16)
            score_grads = (probs * (nt(out_grad, v) - delta)).astype(BF16)
            r.proj_grad[at, cols] = (nn(score_grads, k) * scale).astype(BF16)
            r.kv_grad[:, h * 128 : (h + 1) * 128] += tn(score_grads, q)
            r.kv_grad[:, att + h * 128 : att + (h + 1) * 128] += tn(probs_low, out_grad)

    mine = aligned(s * att, att)

    @pl.loop(0, NX - 1)
    def _(i):
        block = (s + 1 + i) % NX
        attend(block)
        remote(r.attn.at[block], attn_out.at[:, mine], r.ot_s.at[i], r.ot_r.at[i], (me.dp, block)).start()

    attend(s)
    own_out = pltpu.make_async_copy(r.attn.at[s], attn_out.at[:, mine], r.local.at[7])
    own_out.start()

    r.proj_grad[:, att : 2 * att] = (r.kv_grad[:, :att] * scale).astype(BF16)
    r.proj_grad[:, 2 * att :] = r.kv_grad[:, att:].astype(BF16)
    r.low_grad[...] = nt(r.proj_grad[...], r.up[...]).astype(BF16)

    down_total = tn(r.low_grad[...], r.modded[...])
    for t in range(12):
        r.down_part[t // 3, (t % 3) * 64 : (t % 3 + 1) * 64, :] = down_total[:, t * 128 : (t + 1) * 128]
    dx = exchange(me, "dx", NX, lambda i: r.down_part.at[(NX - 1) - (s + i) % NX], r.down_in, r.dx_s, r.dx_r)

    one_hot = jnp.where(
        key_label == lax.broadcasted_iota(jnp.int32, key_label.shape, 0), 1.0, 0.0
    ).astype(BF16)[:, :rows]

    def grads(block):
        at = pl.ds(pl.multiple_of(block * rows, rows), rows)

        @pl.loop(0, width // att)
        def _(n):
            f = aligned(n * att, att)
            grad = nt(r.proj_grad[at, :], r.w[f, :]) + nn(r.low_grad[at, :], r.down[:, f])
            grad_low = grad.astype(BF16)
            r.pg[block, :, f] = grad_low
            normed = (r.tok_all[block, :, f].astype(F32) - r.stats[at, 0:1]) * r.stats[at, 1:2]
            r.ip[:, f] += nn(one_hot, grad_low)
            r.ip[:, aligned(width + n * att, att)] += nn(one_hot, (grad * normed).astype(BF16))

    def grad_copy(src, dst, slot, there):
        return remote(src, dst, r.gr_s.at[slot], r.gr_r.at[slot], there)

    half = rows // 2
    first, second = pl.ds(0, half), pl.ds(half, half)
    r.ip[...] = jnp.zeros_like(r.ip)
    grads(so)
    step1_r = grad_copy(r.pg.at[so, first], r.half_l, 0, right)
    step1_l = grad_copy(r.pg.at[so, second], r.half_r, 1, left)
    launch(step1_r)
    launch(step1_l)

    up_total = tn(r.low[...], r.proj_grad[...])
    for t in range(9):
        r.lora[t // 3, (t % 3) * 64 : (t % 3 + 1) * 64, :] = up_total[:, t * 128 : (t + 1) * 128]
    finish(dx)
    r.lora[3] = r.down_part[(NX - 1) - s] + r.down_in[0] + r.down_in[1] + r.down_in[2]

    def triple(there):
        step = (s + there) % 4
        down = step // 3
        return ((3 * there + step) // 4) * (1 - down) + 3 * down

    ly = exchange(me, "dy", NY, lambda i: r.lora.at[triple((y + i) % NY)], r.l_y, r.ly_s, r.ly_r)

    grads(sr)
    plain_r = grad_copy(r.pg.at[sr, second], r.from_l.at[second], 2, right)
    launch(plain_r)
    grads(sl)
    plain_l = grad_copy(r.pg.at[sl, first], r.from_r.at[first], 3, left)
    launch(plain_l)
    step1_r.wait_recv()
    r.comb_r[...] = (r.pg[sr, 0:half].astype(F32) + r.half_l[...].astype(F32)).astype(BF16)
    comb_copy_r = grad_copy(r.comb_r, r.from_l.at[first], 4, right)
    launch(comb_copy_r)
    step1_l.wait_recv()
    r.comb_l[...] = (r.pg[sl, half:rows].astype(F32) + r.half_r[...].astype(F32)).astype(BF16)
    comb_copy_l = grad_copy(r.comb_l, r.from_r.at[second], 5, left)
    launch(comb_copy_l)

    finish(ly)
    r.l_plane[...] = (r.lora[triple(y)] + r.l_y[0] + r.l_y[1] + r.l_y[2]).reshape(r.l_plane.shape)
    lz = exchange(me, "dz", NZ, lambda i: r.l_plane.at[(z + i) % NZ], r.l_z, r.lz_s, r.lz_r)

    grads(s)
    for img in range(2):
        for j in range(24):
            r.ip_own[img * 24 + j : img * 24 + j + 1, :] = r.ip[img : img + 1, j * 128 : (j + 1) * 128]
    ip = exchange(me, "dx", NX, lambda i: r.ip_own, r.ip_in, r.ip_s, r.ip_r)
    finish(lz)
    total = r.l_plane[z]
    for i in range(NZ - 1):
        total += r.l_z[i]
    r.l_own[0] = total
    lc = remote(r.l_own.at[0], r.l_core, r.lc_s.at[0], r.lc_r.at[0], me.at(flip=True))
    lc.start()

    finish(ip)
    r.ig_all[c, z, y] = (r.ip_own[...] + r.ip_in[0] + r.ip_in[1] + r.ip_in[2]).astype(BF16)
    images = PlaneGather(me, r.ig_all, *r.gp)
    images.start_y(r.ig_all.at[c, z, y])

    lc.wait()
    r.l_own[1] = r.l_own[0] + r.l_core[...]
    r.trip[s, z] = r.l_own[1]
    lg = exchange_at(me, "dz", NZ, lambda i: r.l_own.at[1], r.trip.at[s, z], r.lg_s, r.lg_r)
    images.wait_y()
    images.step(1)
    finish(lg)
    lx = exchange_at(me, "dx", NX, lambda i: r.trip.at[s], r.trip.at[s], r.lx_s, r.lx_r)
    images.step(2)

    def prepare():
        x = tok_own()
        mean, inverse = own_stats()
        gain = 1.0 + jnp.where(is0, r.mod[0:1, width:], r.mod[1:2, width:])
        return (x - mean) * inverse, inverse, jnp.where(usable, gain, 0.0)

    def own_stats():
        at = pl.ds(pl.multiple_of(s * rows, rows), rows)
        return r.stats[at, 0:1], r.stats[at, 1:2]

    def tok_own():
        return r.tok_all[s].astype(F32)

    images.step(3)
    images.step(4)
    plain_r.wait_recv()
    plain_l.wait_recv()
    comb_copy_r.wait_recv()
    comb_copy_l.wait_recv()
    normed, inverse, gain = prepare()
    g = gain * (r.pg[s].astype(F32) + r.from_l[...].astype(F32) + r.from_r[...].astype(F32))
    token_grad[...] = (
        inverse
        * (g - jnp.mean(g, axis=1, keepdims=True) - normed * jnp.mean(g * normed, axis=1, keepdims=True))
    ).astype(BF16)

    finish(lx)
    start = 72 * (z * NC + c)
    row = lax.broadcasted_iota(jnp.int32, (128, 128), 0)
    col = lax.broadcasted_iota(jnp.int32, (128, 128), 1)

    def picked(tiles, first_column):
        total = jnp.zeros((64, 128), F32)
        for i, tile in enumerate(tiles):
            pick = jnp.where(row + 128 * i == col + first_column, 1.0, 0.0).astype(BF16)
            large = tile.astype(BF16)
            rest = (tile - large.astype(F32)).astype(BF16)
            total += nn(large, pick) + nn(rest, pick)
        return total

    def tiles_of(index):
        flat = r.trip[index].reshape(192, 128)
        return [flat[i * 64 : (i + 1) * 64] for i in range(3)]

    up_tiles = tiles_of((3 * y) % 4) + tiles_of((3 * y + 1) % 4) + tiles_of((3 * y + 2) % 4)
    up_out[...] = picked(up_tiles, 72 * (z * NC + c))[:, :72]
    down_out[...] = picked(tiles_of(3 - y), 24 * (z * NC + c))[:, :24]

    images.step(5)
    images.wait_cross()
    r.ig_wide[...] = r.ig_all[...].reshape(3072, 128).astype(F32)
    for j in range(24):
        total = jnp.zeros((128, 128), F32)
        for img in range(2):
            part = r.ig_wide[pl.ds(img * 24 + j, 64, stride=48), :].astype(BF16)
            total += tn(r.a_own[img * 64 : (img + 1) * 64], part)
        r.part_wide[0:128, :] = total
        mod_grad[:, j * 128 : (j + 1) * 128] = r.part_wide[pl.ds(pl.multiple_of(48 * c, 8), 48), :]

    for copy in sent:
        copy.wait_send()
    for i in range(NX - 1):
        remote(
            r.attn.at[0], attn_out.at[:, aligned(((s + 3 - i) % NX) * att, att)], r.ot_s.at[i], r.ot_r.at[i], right
        ).wait()
    own_out.wait()
    weights.drain()
    images.drain()


def whole(per_image_rows, tok, cot, act, wq, up, down, mm):
    return pl.pallas_call(
        whole_kernel,
        out_shape=(
            jax.ShapeDtypeStruct((192, 1536), BF16),
            jax.ShapeDtypeStruct((192, 1536), BF16),
            jax.ShapeDtypeStruct((64, 24), F32),
            jax.ShapeDtypeStruct((64, 72), F32),
            jax.ShapeDtypeStruct((48, 3072), F32),
        ),
        in_specs=[pl.BlockSpec(memory_space=pltpu.SMEM), ANY, ANY, VM, VM, ANY, ANY, ANY],
        out_specs=(ANY, VM, VM, VM, VM),
        scratch_shapes=scratch_list(),
        compiler_params=pltpu.CompilerParams(
            collective_id=1, has_side_effects=True, vmem_limit_bytes=60 * 1024 * 1024
        ),
        name="whole",
    )(per_image_rows, tok, cot, act, wq, up, down, mm)


def body(
    tokens,
    cotangent,
    condition,
    per_image_rows,
    query_key_value_weight,
    adapter_down,
    adapter_up,
    modulation_matrix,
):
    act = jax.nn.silu(condition[0].astype(F32)).astype(BF16).astype(F32)
    act = act.reshape(2, NY, NZ, 96).transpose(2, 1, 0, 3)
    act = jnp.pad(act, ((0, 0), (0, 0), (0, 6), (0, 32)))
    attention, token_grad, down_grad, up_grad, mod_grad = whole(
        per_image_rows,
        tokens[0],
        cotangent[0],
        act,
        query_key_value_weight,
        adapter_up,
        adapter_down.T,
        modulation_matrix,
    )
    return attention[None], token_grad[None], down_grad.T, up_grad, mod_grad


def solution(mesh):
    in_specs = (
        P("dp", "seq", None),
        P("dp", "seq", None),
        P("dp", None, None),
        P(),
        P("dp", None),
        P(),
        P(),
        P("dp", None),
    )
    out_specs = (
        P("dp", "seq", None),
        P("dp", "seq", None),
        P("dp", None),
        P(None, "dp"),
        P("dp", None),
    )
    return jax.shard_map(body, mesh=mesh, in_specs=in_specs, out_specs=out_specs, check_vma=False)
```

time: 1130 us -> 123 us (0.11)
  waiting for transfers between devices: 766 us -> 0 us
  blocking collectives: 161 us -> 0 us
  Pallas kernels: 0 us -> 113 us
  matrix products: 65.9 us -> 0 us
  local copies, waits for them, and re-layouts: 59.4 us -> 7.79 us
  other arithmetic: 25.5 us -> 0.72 us
  starting transfers between devices: 22.9 us -> 0 us
  between operations: 18.5 us -> 0.65 us
    unnamed x11 -> x0, waiting for transfers between devices: 492 us -> none
    all_gather x5 -> x0, waiting for transfers between devices: 189 us -> none  [the longest x1 78 us: body(): lax.all_gather(image_grad, 'dp', axis=0, tiled=True)]
    pallas_call x0 -> x1, Pallas kernels: none -> 113 us  [whole(): pl.pallas_call(whole_kernel, out_shape=(jax.ShapeDtypeStruct((192, 1536),...]
    all_to_all x3 -> x0, waiting for transfers between devices: 84 us -> none  [the longest x1 56.5 us: body(): lax.all_to_all(unpack_rows(bundled_projection, places, live_slots), 'dp',...]
    all_gather x3 -> x0, blocking collectives: 76 us -> none  [the longest x1 55.2 us: body(): all_active = lax.all_gather(activated, 'dp', axis=0, tiled=True)]
    all_to_all x1 -> x0, blocking collectives: 70.1 us -> none  [body(): lax.all_to_all(to_peers(projection_grad, rotation, groups), 'dp', split_a...]
    dot_general x20 -> x0, matrix products: 65.9 us -> none  [the longest x1 9.41 us: body(): jnp.dot(bundled_grads, weight_matrix.T, preferred_element_type=jnp.float32)]
    all_to_all x3 -> x0, starting transfers between devices: 22.2 us -> none  [the longest x1 9.68 us: body(): lax.all_to_all(to_peers(modulated_input, rotation, groups), 'dp', split_a...]
  transfers between devices with their start and end apart: 11 -> 0, of which waited for: 10 -> 0; matrix products, arithmetic and copies ran while one was open for 7% -> 0% of each run, Pallas kernels for 0% -> 0%
where the time goes in v2:
time: 123 us; the launch traced here: 122 us
  Pallas kernels  113 us (92%)
  local copies, waits for them, and re-layouts  7.79 us (6%)
    pallas_call x1, Pallas kernels, whole(): pl.pallas_call(whole_kernel, out_shape=(jax.ShapeDtypeStruct((192, 1536),...  113 us
    unnamed x14, local copies, waits for them, and re-layouts  7 us

profile of v2, /device:TPU:1, one launch (start us, length us, event | category | flops | bytes accessed | tf_op | source)
XLA Modules:
  0.0 121.9 jit_solution(3233227673261927008)
XLA Ops:
  0.6 0.8 reshape.14
  1.4 0.0 copy-start.3
  1.4 0.1 fusion.1
  1.5 0.6 copy-done.3
  2.1 0.7 copy.23.rows_ref
  2.8 0.7 pad_convert_fusion.act
  3.5 112.7 %whole.1 = (bf16[192,1536]{1,0:T(8,128)(2,1)}, bf16[192,1536]{1,0:T(8,128)(2,1)}, f32[64,24]{1,0:T(8,128)}, f32[64,72]{1,0:T(8,128)}, f32[48,3072]{1,0:T(8,128)}) custom-call(s32[64,2]{1,0:T(8,128)} %copy.23.rows_ref, bf16[192,1536]{1,0:T(8,128)(2,1)} %bitcast.8, bf16[192,1536]{1,0:T(8,128)(2,1)} %bitcast.9, f32[8,4,8,128]{3,2,1,0:T(8,128)} %pad_convert_fusion.act, ...), custom_call_target="tpu_custom_call" | custom-call | tf_op jit(solution)/shard_map/whole/pallas_call | solution.py:669
  116.2 1.4 %copy.24 = f32[24,64]{1,0:T(8,128)} copy(f32[24,64]{0,1:T(8,128)} %bitcast.13) | data formatting | bytes 12288
  117.6 0.0 copy-start.1
  117.6 2.0 %copy.34 = bf16[1,192,1536]{2,1,0:T(8,128)(2,1)} copy(bf16[1,192,1536]{2,1,0:T(8,128)(2,1)} %bitcast.11) | data formatting | bytes 1179648
  119.6 0.0 copy-done.1
  119.6 0.0 copy-start.2
  119.6 0.0 copy-start
  119.6 0.8 copy.35
  120.4 0.0 copy-done.2
  120.4 0.6 copy.36
  121.1 0.0 copy-done
  121.1 0.8 copy.37
Async XLA Ops:
  1.4 0.7 copy-start.3
  117.6 2.0 %copy-start.1 = (bf16[192,1536]{1,0:T(8,128)(2,1)S(1)}, bf16[192,1536]{1,0:T(8,128)(2,1)}, u32[]{:S(2)}) copy-start(bf16[192,1536]{1,0:T(8,128)(2,1)} %get-tuple-element.11) | copy-start | bytes 1769476
  119.6 0.8 copy-start.2
  119.6 1.4 %copy-start = (f32[48,3072]{1,0:T(8,128)S(1)}, f32[48,3072]{1,0:T(8,128)}, u32[]{:S(2)}) copy-start(f32[48,3072]{1,0:T(8,128)} %get-tuple-element.39) | copy-start | bytes 1769476

commit v3 on v2

--- a/solution.py
+++ b/solution.py
@@ -122,11 +122,10 @@
         copy.start()
         self.sent.append(copy)
 
-    def wait_cross(self):
+    def wait_cross(self, shift):
         me = self.me
-        for shift in range(NZ):
-            block = self.buf.at[1 - me.c, (me.z + shift) % NZ]
-            remote(block, block, self.csend.at[shift], self.crecv.at[shift], me.at(flip=True)).wait_recv()
+        block = self.buf.at[1 - me.c, (me.z + shift) % NZ]
+        remote(block, block, self.csend.at[shift], self.crecv.at[shift], me.at(flip=True)).wait_recv()
 
     def drain(self):
         for copy in self.sent:
@@ -153,11 +152,6 @@
     return copies
 
 
-def finish(copies):
-    for copy in copies:
-        copy.wait()
-
-
 def exchange_at(me, axis, count, source, target, send, recv):
     copies = []
     for i in range(1, count):
@@ -198,21 +192,21 @@
     w=pltpu.VMEM((1536, 1152), BF16),
     up=pltpu.VMEM((64, 1152), BF16),
     down=pltpu.VMEM((64, 1536), BF16),
-    mm=pltpu.VMEM((128, 768), BF16),
+    mm=pltpu.VMEM((256, 768), BF16),
+    a_src=pltpu.VMEM((NZ, NY, 8, 128), F32),
     a_z=pltpu.VMEM((NZ, NY, 8, 128), F32),
-    a_y=pltpu.VMEM((NC, NZ, NY, 8, 128), F32),
+    a_y=pltpu.VMEM((NC, NY, NZ, 8, 128), F32),
     a_wide=pltpu.VMEM((512, 128), F32),
-    a_own=pltpu.VMEM((128, 128), BF16),
+    a_pair=pltpu.VMEM((128, 256), BF16),
     part_wide=pltpu.VMEM((1024, 128), F32),
-    part_low=pltpu.VMEM((NC, NZ, NY, 16, 128), BF16),
-    m_core=pltpu.VMEM((NZ, NY, 16, 128), BF16),
-    m_sum=pltpu.VMEM((NZ, NY, 16, 128), BF16),
+    part_low=pltpu.VMEM((NC, NY, NZ, 16, 128), BF16),
+    m_core=pltpu.VMEM((NY, NZ, 16, 128), BF16),
+    m_sum=pltpu.VMEM((NY, NZ, 16, 128), BF16),
     m_y=pltpu.VMEM((NY - 1, NZ, 16, 128), BF16),
     m_plane=pltpu.VMEM((NZ, 16, 128), F32),
     m_z=pltpu.VMEM((NZ - 1, 16, 128), F32),
     m_own=pltpu.VMEM((16, 128), F32),
     m_all=pltpu.VMEM((NX, 16, 128), F32),
-    mod=pltpu.VMEM((8, 3072), F32),
     modded=pltpu.VMEM((768, 1536), BF16),
     stats=pltpu.VMEM((768, 128), F32),
     low=pltpu.VMEM((768, 64), BF16),
@@ -231,20 +225,17 @@
     from_r=pltpu.VMEM((192, 1536), BF16),
     ip_own=pltpu.VMEM((48, 128), F32),
     ip_in=pltpu.VMEM((3, 48, 128), F32),
-    ig_all=pltpu.VMEM((NC, NZ, NY, 48, 128), BF16),
-    ig_wide=pltpu.VMEM((3072, 128), F32),
-    lora=pltpu.VMEM((4, 192, 128), F32),
-    down_part=pltpu.VMEM((4, 192, 128), F32),
-    down_in=pltpu.VMEM((3, 192, 128), F32),
-    l_y=pltpu.VMEM((3, 192, 128), F32),
-    l_plane=pltpu.VMEM((NZ, 24, 128), F32),
-    l_z=pltpu.VMEM((NZ - 1, 24, 128), F32),
-    l_own=pltpu.VMEM((2, 24, 128), F32),
-    l_core=pltpu.VMEM((24, 128), F32),
-    trip=pltpu.VMEM((NX, NZ, 24, 128), F32),
+    lo=pltpu.VMEM((NY, 2, 192, 128), BF16),
+    l_y=pltpu.VMEM((NY - 1, 2, 192, 128), BF16),
+    l_plane=pltpu.VMEM((NZ, 48, 128), BF16),
+    l_z=pltpu.VMEM((NZ - 1, 48, 128), BF16),
+    l_own=pltpu.VMEM((48, 128), F32),
+    l_core=pltpu.VMEM((48, 128), F32),
+    l_piece=pltpu.VMEM((48, 128), BF16),
+    l_x=pltpu.VMEM((NX, 48, 128), BF16),
 )
-PAIRS = dict(tk=12, ck=3, az=7, ay=3, ac=1, mc=1, my=3, mz=7, mx=3, gr=6, ot=3, ip=3, dx=3, ly=3, lz=7, lc=1, lg=7, lx=3)
-PLANES = dict(wp=1, gp=1)
+PAIRS = dict(tk=12, ck=3, az=7, ay=3, ac=1, mc=1, my=3, mz=7, mx=3, gr=6, ot=3, ip=3, iz=7, iy=3, ic=1, ly=3, lz=7, lc=1, lx=3, lg=7)
+PLANES = dict(wp=1)
 LOCAL = 8
 
 
@@ -273,8 +264,8 @@
 
 
 def whole_kernel(
-    rows_ref, tok, cot, act, wq, up_in, down_in, mm_in,
-    attn_out, token_grad, down_out, up_out, mod_grad,
+    rows_ref, tok, cot, cond, wq, up_in, down_in, mm_in,
+    attn_out, grad_out, mod, a_own, ig_all, f_all,
     *refs,
 ):
     r = named(refs)
@@ -285,14 +276,15 @@
     scale = HEAD_SIZE ** (-0.5)
     right, left = me.at(dx=1), me.at(dx=NX - 1)
     sl, sr, so = (s + NX - 1) % NX, (s + 1) % NX, (s + 2) % NX
-    c0, c1 = rows_ref[me.dp, 0], rows_ref[me.dp, 1]
-
+    c0, c1 = rows_ref[0, me.dp], rows_ref[1, me.dp]
+
+    offset = 48 * me.dp - 128 * ((96 * (me.dp // 2)) // 128)
     r.mm[...] = jnp.zeros_like(r.mm)
     locals_ = [
         pltpu.make_async_copy(tok, r.tok_all.at[s], r.local.at[0]),
         pltpu.make_async_copy(cot.at[:, aligned(s * att, att)], r.cot_all.at[s], r.local.at[1]),
         pltpu.make_async_copy(
-            mm_in.at[:, aligned(s * 768, 768)], r.mm.at[pl.ds(pl.multiple_of(48 * c, 16), 48)], r.local.at[2]
+            mm_in.at[:, aligned(s * 768, 768)], r.mm.at[pl.ds(pl.multiple_of(offset, 16), 48)], r.local.at[2]
         ),
         pltpu.make_async_copy(down_in, r.down, r.local.at[3]),
     ]
@@ -310,11 +302,29 @@
         pieces += [block[:, i * 128 : (i + 1) * 128] for i in range(3)]
     pieces.append(jnp.zeros((8, 128), F32))
     r.w_all[c, z, y] = jnp.concatenate(pieces, axis=0).astype(BF16)
-    r.a_z[z] = act[z]
+    wide = cond[...].astype(F32)
+    wide = (wide / (1.0 + jnp.exp(-wide))).astype(BF16).astype(F32)
+    r.a_src[...] = jnp.zeros_like(r.a_src)
+    for p in range(NZ * NY):
+        j = (96 * p) // 128
+        for img in range(2):
+            for t in range(2):
+                if j + t < 24:
+                    r.a_src[p % NZ, p // NZ, 2 * img + t : 2 * img + t + 1, :] = wide[
+                        img : img + 1, (j + t) * 128 : (j + t + 1) * 128
+                    ]
+    r.a_z[z] = r.a_src[z]
 
     enter(me)
 
-    az = exchange_at(me, "dz", NZ, lambda i: act.at[(z + i) % NZ], r.a_z.at[z], r.az_s, r.az_r)
+    sent = []
+
+    def arrived(copies):
+        for copy in copies:
+            copy.wait_recv()
+            sent.append(copy)
+
+    az = exchange_at(me, "dz", NZ, lambda i: r.a_src.at[(z + i) % NZ], r.a_z.at[z], r.az_s, r.az_r)
     weights = PlaneGather(me, r.w_all, *r.wp)
     weights.start_y(r.w_all.at[c, z, y])
 
@@ -323,8 +333,6 @@
 
     def token_copy(source, owner, i, slot, there):
         return remote(source, r.tok_all.at[owner, row_chunk(i)], r.tk_s.at[slot], r.tk_r.at[slot], there)
-
-    sent = []
 
     def launch(copy):
         copy.start()
@@ -341,30 +349,38 @@
         token_copy(tok.at[row_chunk(j)], sr, j, 4 + j, left).wait_recv()
         launch(token_copy(r.tok_all.at[sr, row_chunk(j)], sr, j, 8 + j, left))
 
-    finish(az)
+    arrived(az)
     ay = exchange_at(
-        me, "dy", NY, lambda i: r.a_z.at[:, (y + i) % NY], r.a_y.at[c, :, y], r.ay_s, r.ay_r
+        me, "dy", NY, lambda i: r.a_z.at[:, (y + i) % NY], r.a_y.at[c, y], r.ay_s, r.ay_r
     )
-    r.a_y[c, :, y] = r.a_z[:, y]
+    r.a_y[c, y] = r.a_z[:, y]
     weights.wait_y()
     weights.step(1)
-    finish(ay)
+    arrived(ay)
     ac = remote(r.a_y.at[c], r.a_y.at[c], r.ac_s.at[0], r.ac_r.at[0], me.at(flip=True))
     ac.start()
     forward(0)
-    ac.wait()
+    arrived([ac])
     locals_[2].wait()
     r.a_wide[...] = r.a_y[...].reshape(512, 128)
     for img in range(2):
-        r.a_own[img * 64 : (img + 1) * 64, :] = r.a_wide[pl.ds(img, 64, stride=8), :].astype(BF16)
+        for t in range(2):
+            r.a_pair[img * 64 : (img + 1) * 64, t * 128 : (t + 1) * 128] = r.a_wide[
+                pl.ds(2 * img + t, 64, stride=8), :
+            ].astype(BF16)
     r.part_wide[...] = jnp.zeros_like(r.part_wide)
     for j in range(6):
-        columns = nn(r.a_own[...], r.mm[:, j * 128 : (j + 1) * 128])
+        columns = nn(r.a_pair[...], r.mm[:, j * 128 : (j + 1) * 128])
         for img in range(2):
             r.part_wide[pl.ds(img * 6 + j, 64, stride=16), :] = columns[img * 64 : (img + 1) * 64]
     r.part_low[...] = r.part_wide[...].astype(BF16).reshape(r.part_low.shape)
     mc = remote(r.part_low.at[1 - c], r.m_core, r.mc_s.at[0], r.mc_r.at[0], me.at(flip=True))
     mc.start()
+    row = lax.broadcasted_iota(jnp.int32, (256, 128), 0)
+    col = lax.broadcasted_iota(jnp.int32, (256, 128), 1)
+    pick = jnp.where((row == col + offset) & (col < 48), 1.0, 0.0).astype(BF16)
+    a_own[...] = nn(r.a_pair[...], pick).astype(BF16)
+    r.kv_grad[...] = jnp.zeros_like(r.kv_grad)
     forward(1)
     weights.step(2)
     for i in range(1, NX):
@@ -374,17 +390,17 @@
                 cot.at[:, aligned(there[1] * att, att)], r.cot_all.at[s], r.ck_s.at[i - 1], r.ck_r.at[i - 1], there
             )
         )
-    mc.wait()
+    arrived([mc])
     r.m_sum[...] = (r.part_low[c].astype(F32) + r.m_core[...].astype(F32)).astype(BF16)
-    my = exchange(me, "dy", NY, lambda i: r.m_sum.at[:, (y + i) % NY], r.m_y, r.my_s, r.my_r)
-    finish(my)
-    total = r.m_sum[:, y].astype(F32)
+    my = exchange(me, "dy", NY, lambda i: r.m_sum.at[(y + i) % NY], r.m_y, r.my_s, r.my_r)
+    arrived(my)
+    total = r.m_sum[y].astype(F32)
     for i in range(NY - 1):
         total += r.m_y[i].astype(F32)
     r.m_plane[...] = total
     mz = exchange(me, "dz", NZ, lambda i: r.m_plane.at[(z + i) % NZ], r.m_z, r.mz_s, r.mz_r)
     weights.step(3)
-    finish(mz)
+    arrived(mz)
     total = r.m_plane[z]
     for i in range(NZ - 1):
         total += r.m_z[i]
@@ -392,6 +408,19 @@
     r.m_all[s] = total
     mx = exchange_at(me, "dx", NX, lambda i: r.m_own, r.m_all.at[s], r.mx_s, r.mx_r)
     weights.step(4)
+
+    def place(shift):
+        weights.wait_cross(shift)
+        at_z = (z + shift) % NZ
+
+        @pl.loop(0, NY)
+        def _(at_y):
+            first = r.w_all[0, at_z, at_y].astype(F32)
+            other = r.w_all[1, at_z, at_y].astype(F32)
+            at = pl.ds(pl.multiple_of(48 * (NZ * at_y + at_z), 16), 48)
+            for t in range(9):
+                both = jnp.concatenate([first[24 * t : 24 * t + 24], other[24 * t : 24 * t + 24]], axis=0)
+                r.w[at, t * 128 : (t + 1) * 128] = both.astype(BF16)
 
     label = labels_of(lax.broadcasted_iota(jnp.int32, (rows, 1), 0), c0, c1)
     usable = label < 2
@@ -402,20 +431,24 @@
     key_label = labels_of(lane, c0, c1)
     key_label = jnp.where(key_label < 2, key_label, 8)
 
-    finish(mx)
+    place(0)
+    place(1)
+    place(NZ - 1)
+    arrived(mx)
+    mod[...] = jnp.zeros_like(mod)
     for k in range(NX):
         for img in range(2):
             for j in range(6):
                 at = 768 * k + 128 * j
-                r.mod[img : img + 1, at : at + 128] = r.m_all[k, img * 6 + j : img * 6 + j + 1, :]
+                mod[img : img + 1, at : at + 128] = r.m_all[k, img * 6 + j : img * 6 + j + 1, :]
 
     def normalize(block):
         x = r.tok_all[block].astype(F32)
         mean = jnp.mean(x, axis=1, keepdims=True)
         centred = x - mean
         inverse = lax.rsqrt(jnp.mean(centred * centred, axis=1, keepdims=True) + EPSILON)
-        shift = jnp.where(is0, r.mod[0:1, :width], r.mod[1:2, :width])
-        gain = 1.0 + jnp.where(is0, r.mod[0:1, width:], r.mod[1:2, width:])
+        shift = jnp.where(is0, mod[0:1, :width], mod[1:2, :width])
+        gain = 1.0 + jnp.where(is0, mod[0:1, width:], mod[1:2, width:])
         value = jnp.where(usable, gain * (centred * inverse) + shift, 0.0).astype(BF16)
         at = pl.ds(pl.multiple_of(block * rows, rows), rows)
         r.modded[at, :] = value
@@ -428,6 +461,8 @@
         token_copy(tok.at[row_chunk(i)], sl, i, i, right).wait_recv() if i >= 2 else None
     normalize(sl)
     weights.step(5)
+    place(2)
+    place(NZ - 2)
     for i in range(4):
         token_copy(tok.at[row_chunk(3 - i)], sr, 3 - i, 4 + 3 - i, left).wait_recv() if i >= 2 else None
     normalize(sr)
@@ -435,17 +470,9 @@
         token_copy(tok.at[row_chunk(i)], so, i, 8 + i, right).wait_recv()
         token_copy(tok.at[row_chunk(3 - i)], so, 3 - i, 8 + 3 - i, left).wait_recv()
     normalize(so)
-    weights.wait_cross()
-
-    @pl.loop(0, NZ * NY)
-    def _(pair):
-        first = r.w_all[0, pair % NZ, pair // NZ].astype(F32)
-        other = r.w_all[1, pair % NZ, pair // NZ].astype(F32)
-        at = pl.ds(pl.multiple_of(48 * pair, 16), 48)
-        for t in range(9):
-            both = jnp.concatenate([first[24 * t : 24 * t + 24], other[24 * t : 24 * t + 24]], axis=0)
-            r.w[at, t * 128 : (t + 1) * 128] = both.astype(BF16)
-
+    place(3)
+    place(5)
+    place(4)
     for copy in locals_[3:]:
         copy.wait()
     r.low[...] = nt(r.modded[...], r.down[...]).astype(BF16)
@@ -455,7 +482,6 @@
         at = aligned(n * att, att)
         r.proj[:, at] = (nn(r.modded[...], r.w[:, at]) + nn(r.low[...], r.up[:, at])).astype(BF16)
 
-    r.kv_grad[...] = jnp.zeros_like(r.kv_grad)
     locals_[1].wait()
     for i in range(1, NX):
         remote(
@@ -482,8 +508,8 @@
             out_grad = out_grad.astype(BF16)
             score_grads = (probs * (nt(out_grad, v) - delta)).astype(BF16)
             r.proj_grad[at, cols] = (nn(score_grads, k) * scale).astype(BF16)
-            r.kv_grad[:, h * 128 : (h + 1) * 128] += tn(score_grads, q)
-            r.kv_grad[:, att + h * 128 : att + (h + 1) * 128] += tn(probs_low, out_grad)
+            r.kv_grad[h * 128 : (h + 1) * 128, :] += tn(q, score_grads)
+            r.kv_grad[att + h * 128 : att + (h + 1) * 128, :] += tn(out_grad, probs_low)
 
     mine = aligned(s * att, att)
 
@@ -497,14 +523,12 @@
     own_out = pltpu.make_async_copy(r.attn.at[s], attn_out.at[:, mine], r.local.at[7])
     own_out.start()
 
-    r.proj_grad[:, att : 2 * att] = (r.kv_grad[:, :att] * scale).astype(BF16)
-    r.proj_grad[:, 2 * att :] = r.kv_grad[:, att:].astype(BF16)
+    for h in range(2 * heads):
+        turned = r.kv_grad[h * 128 : (h + 1) * 128, :].T
+        if h < heads:
+            turned = turned * scale
+        r.proj_grad[:, att + h * 128 : att + (h + 1) * 128] = turned.astype(BF16)
     r.low_grad[...] = nt(r.proj_grad[...], r.up[...]).astype(BF16)
-
-    down_total = tn(r.low_grad[...], r.modded[...])
-    for t in range(12):
-        r.down_part[t // 3, (t % 3) * 64 : (t % 3 + 1) * 64, :] = down_total[:, t * 128 : (t + 1) * 128]
-    dx = exchange(me, "dx", NX, lambda i: r.down_part.at[(NX - 1) - (s + i) % NX], r.down_in, r.dx_s, r.dx_r)
 
     one_hot = jnp.where(
         key_label == lax.broadcasted_iota(jnp.int32, key_label.shape, 0), 1.0, 0.0
@@ -535,25 +559,22 @@
     launch(step1_r)
     launch(step1_l)
 
-    up_total = tn(r.low[...], r.proj_grad[...])
-    for t in range(9):
-        r.lora[t // 3, (t % 3) * 64 : (t % 3 + 1) * 64, :] = up_total[:, t * 128 : (t + 1) * 128]
-    finish(dx)
-    r.lora[3] = r.down_part[(NX - 1) - s] + r.down_in[0] + r.down_in[1] + r.down_in[2]
-
-    def triple(there):
-        step = (s + there) % 4
-        down = step // 3
-        return ((3 * there + step) // 4) * (1 - down) + 3 * down
-
-    ly = exchange(me, "dy", NY, lambda i: r.lora.at[triple((y + i) % NY)], r.l_y, r.ly_s, r.ly_r)
-
     grads(sr)
     plain_r = grad_copy(r.pg.at[sr, second], r.from_l.at[second], 2, right)
     launch(plain_r)
     grads(sl)
     plain_l = grad_copy(r.pg.at[sl, first], r.from_r.at[first], 3, left)
     launch(plain_l)
+
+    r.lo[NX - 1 - s, 0] = jnp.zeros((192, 128), BF16)
+    up_total = tn(r.low[...], r.proj_grad[...]).astype(BF16)
+    for t in range(9):
+        r.lo[(4 * (t // 3) + s) // 3, 0, (t % 3) * 64 : (t % 3 + 1) * 64, :] = up_total[:, t * 128 : (t + 1) * 128]
+    down_total = tn(r.low_grad[...], r.modded[...]).astype(BF16)
+    for t in range(12):
+        r.lo[t // 3, 1, (t % 3) * 64 : (t % 3 + 1) * 64, :] = down_total[:, t * 128 : (t + 1) * 128]
+    ly = exchange(me, "dy", NY, lambda i: r.lo.at[(y + i) % NY], r.l_y, r.ly_s, r.ly_r)
+
     step1_r.wait_recv()
     r.comb_r[...] = (r.pg[sr, 0:half].astype(F32) + r.half_l[...].astype(F32)).astype(BF16)
     comb_copy_r = grad_copy(r.comb_r, r.from_l.at[first], 4, right)
@@ -563,96 +584,62 @@
     comb_copy_l = grad_copy(r.comb_l, r.from_r.at[second], 5, left)
     launch(comb_copy_l)
 
-    finish(ly)
-    r.l_plane[...] = (r.lora[triple(y)] + r.l_y[0] + r.l_y[1] + r.l_y[2]).reshape(r.l_plane.shape)
-    lz = exchange(me, "dz", NZ, lambda i: r.l_plane.at[(z + i) % NZ], r.l_z, r.lz_s, r.lz_r)
-
     grads(s)
     for img in range(2):
         for j in range(24):
             r.ip_own[img * 24 + j : img * 24 + j + 1, :] = r.ip[img : img + 1, j * 128 : (j + 1) * 128]
     ip = exchange(me, "dx", NX, lambda i: r.ip_own, r.ip_in, r.ip_s, r.ip_r)
-    finish(lz)
-    total = r.l_plane[z]
+
+    arrived(ly)
+    total = r.lo[y].astype(F32)
+    for i in range(NY - 1):
+        total += r.l_y[i].astype(F32)
+    for i in range(NZ):
+        at = slice(24 * i, 24 * i + 24)
+        r.l_plane[i] = jnp.concatenate([total[0, at], total[1, at]], axis=0).astype(BF16)
+    lz = exchange(me, "dz", NZ, lambda i: r.l_plane.at[(z + i) % NZ], r.l_z, r.lz_s, r.lz_r)
+
+    arrived(ip)
+    ig_all[c, y, z] = (r.ip_own[...] + r.ip_in[0] + r.ip_in[1] + r.ip_in[2]).astype(BF16)
+    own_ig = ig_all.at[c, y, z]
+    iz = exchange_at(me, "dz", NZ, lambda i: own_ig, own_ig, r.iz_s, r.iz_r)
+
+    arrived(lz)
+    total = r.l_plane[z].astype(F32)
     for i in range(NZ - 1):
-        total += r.l_z[i]
-    r.l_own[0] = total
-    lc = remote(r.l_own.at[0], r.l_core, r.lc_s.at[0], r.lc_r.at[0], me.at(flip=True))
+        total += r.l_z[i].astype(F32)
+    r.l_own[...] = total
+    lc = remote(r.l_own, r.l_core, r.lc_s.at[0], r.lc_r.at[0], me.at(flip=True))
     lc.start()
 
-    finish(ip)
-    r.ig_all[c, z, y] = (r.ip_own[...] + r.ip_in[0] + r.ip_in[1] + r.ip_in[2]).astype(BF16)
-    images = PlaneGather(me, r.ig_all, *r.gp)
-    images.start_y(r.ig_all.at[c, z, y])
-
-    lc.wait()
-    r.l_own[1] = r.l_own[0] + r.l_core[...]
-    r.trip[s, z] = r.l_own[1]
-    lg = exchange_at(me, "dz", NZ, lambda i: r.l_own.at[1], r.trip.at[s, z], r.lg_s, r.lg_r)
-    images.wait_y()
-    images.step(1)
-    finish(lg)
-    lx = exchange_at(me, "dx", NX, lambda i: r.trip.at[s], r.trip.at[s], r.lx_s, r.lx_r)
-    images.step(2)
-
-    def prepare():
-        x = tok_own()
-        mean, inverse = own_stats()
-        gain = 1.0 + jnp.where(is0, r.mod[0:1, width:], r.mod[1:2, width:])
-        return (x - mean) * inverse, inverse, jnp.where(usable, gain, 0.0)
-
-    def own_stats():
-        at = pl.ds(pl.multiple_of(s * rows, rows), rows)
-        return r.stats[at, 0:1], r.stats[at, 1:2]
-
-    def tok_own():
-        return r.tok_all[s].astype(F32)
-
-    images.step(3)
-    images.step(4)
+    arrived(iz)
+    column = ig_all.at[c, y]
+    iy = exchange_at(me, "dy", NY, lambda i: column, column, r.iy_s, r.iy_r)
+
+    arrived([lc])
+    r.l_piece[...] = (r.l_own[...] + r.l_core[...]).astype(BF16)
+    r.l_x[s] = r.l_piece[...]
+    lx = exchange_at(me, "dx", NX, lambda i: r.l_piece, r.l_x.at[s], r.lx_s, r.lx_r)
+
+    arrived(iy)
+    ic = remote(ig_all.at[c], ig_all.at[c], r.ic_s.at[0], r.ic_r.at[0], me.at(flip=True))
+    ic.start()
+
+    arrived(lx)
+    pieces = [r.l_x[(3 * y + i) % 4].astype(F32)[0:24] for i in range(3)]
+    total = r.l_x[0].astype(F32)[24:48]
+    for i in range(1, NX):
+        total += r.l_x[i].astype(F32)[24:48]
+    f_all[z] = jnp.concatenate(pieces + [total], axis=0).astype(BF16)
+    lg = exchange_at(me, "dz", NZ, lambda i: f_all.at[z], f_all.at[z], r.lg_s, r.lg_r)
+
     plain_r.wait_recv()
     plain_l.wait_recv()
     comb_copy_r.wait_recv()
     comb_copy_l.wait_recv()
-    normed, inverse, gain = prepare()
-    g = gain * (r.pg[s].astype(F32) + r.from_l[...].astype(F32) + r.from_r[...].astype(F32))
-    token_grad[...] = (
-        inverse
-        * (g - jnp.mean(g, axis=1, keepdims=True) - normed * jnp.mean(g * normed, axis=1, keepdims=True))
-    ).astype(BF16)
-
-    finish(lx)
-    start = 72 * (z * NC + c)
-    row = lax.broadcasted_iota(jnp.int32, (128, 128), 0)
-    col = lax.broadcasted_iota(jnp.int32, (128, 128), 1)
-
-    def picked(tiles, first_column):
-        total = jnp.zeros((64, 128), F32)
-        for i, tile in enumerate(tiles):
-            pick = jnp.where(row + 128 * i == col + first_column, 1.0, 0.0).astype(BF16)
-            large = tile.astype(BF16)
-            rest = (tile - large.astype(F32)).astype(BF16)
-            total += nn(large, pick) + nn(rest, pick)
-        return total
-
-    def tiles_of(index):
-        flat = r.trip[index].reshape(192, 128)
-        return [flat[i * 64 : (i + 1) * 64] for i in range(3)]
-
-    up_tiles = tiles_of((3 * y) % 4) + tiles_of((3 * y + 1) % 4) + tiles_of((3 * y + 2) % 4)
-    up_out[...] = picked(up_tiles, 72 * (z * NC + c))[:, :72]
-    down_out[...] = picked(tiles_of(3 - y), 24 * (z * NC + c))[:, :24]
-
-    images.step(5)
-    images.wait_cross()
-    r.ig_wide[...] = r.ig_all[...].reshape(3072, 128).astype(F32)
-    for j in range(24):
-        total = jnp.zeros((128, 128), F32)
-        for img in range(2):
-            part = r.ig_wide[pl.ds(img * 24 + j, 64, stride=48), :].astype(BF16)
-            total += tn(r.a_own[img * 64 : (img + 1) * 64], part)
-        r.part_wide[0:128, :] = total
-        mod_grad[:, j * 128 : (j + 1) * 128] = r.part_wide[pl.ds(pl.multiple_of(48 * c, 8), 48), :]
+    grad_out[...] = (r.pg[s].astype(F32) + r.from_l[...].astype(F32) + r.from_r[...].astype(F32)).astype(BF16)
+    arrived([ic])
+    arrived(lg)
 
     for copy in sent:
         copy.wait_send()
@@ -662,27 +649,95 @@
         ).wait()
     own_out.wait()
     weights.drain()
-    images.drain()
-
-
-def whole(per_image_rows, tok, cot, act, wq, up, down, mm):
+
+
+def whole(counts, tok, cot, cond, wq, up, down, mm):
     return pl.pallas_call(
         whole_kernel,
         out_shape=(
             jax.ShapeDtypeStruct((192, 1536), BF16),
             jax.ShapeDtypeStruct((192, 1536), BF16),
-            jax.ShapeDtypeStruct((64, 24), F32),
-            jax.ShapeDtypeStruct((64, 72), F32),
-            jax.ShapeDtypeStruct((48, 3072), F32),
+            jax.ShapeDtypeStruct((8, 3072), F32),
+            jax.ShapeDtypeStruct((128, 128), BF16),
+            jax.ShapeDtypeStruct((NC, NY, NZ, 48, 128), BF16),
+            jax.ShapeDtypeStruct((NZ, 96, 128), BF16),
         ),
         in_specs=[pl.BlockSpec(memory_space=pltpu.SMEM), ANY, ANY, VM, VM, ANY, ANY, ANY],
-        out_specs=(ANY, VM, VM, VM, VM),
+        out_specs=(ANY, VM, VM, VM, VM, VM),
         scratch_shapes=scratch_list(),
         compiler_params=pltpu.CompilerParams(
             collective_id=1, has_side_effects=True, vmem_limit_bytes=60 * 1024 * 1024
         ),
         name="whole",
-    )(per_image_rows, tok, cot, act, wq, up, down, mm)
+    )(counts, tok, cot, cond, wq, up, down, mm)
+
+
+def tail_kernel(
+    counts, attn, grad, tok, mod, act, ig, pieces,
+    attn_out, token_grad, down_out, up_out, mod_grad,
+    ig_wide, sem,
+):
+    copy = pltpu.make_async_copy(attn, attn_out, sem)
+    copy.start()
+    rows, width = tok.shape
+    dp = lax.axis_index("dp")
+    c0, c1 = counts[0, dp], counts[1, dp]
+    label = labels_of(lax.broadcasted_iota(jnp.int32, (rows, 1), 0), c0, c1)
+    x = tok[...].astype(F32)
+    centred = x - jnp.mean(x, axis=1, keepdims=True)
+    inverse = lax.rsqrt(jnp.mean(centred * centred, axis=1, keepdims=True) + EPSILON)
+    normed = centred * inverse
+    gain = 1.0 + jnp.where(label == 0, mod[0:1, width:], mod[1:2, width:])
+    g = jnp.where(label < 2, gain * grad[...].astype(F32), 0.0)
+    token_grad[...] = (
+        inverse
+        * (g - jnp.mean(g, axis=1, keepdims=True) - normed * jnp.mean(g * normed, axis=1, keepdims=True))
+    ).astype(BF16)
+
+    ig_wide[...] = ig[...].reshape(3072, 128).astype(F32)
+    for j in range(24):
+        total = jnp.zeros((128, 128), F32)
+        for img in range(2):
+            part = ig_wide[pl.ds(img * 24 + j, 64, stride=48), :].astype(BF16)
+            total += tn(act[img * 64 : (img + 1) * 64], part)
+        mod_grad[:, j * 128 : (j + 1) * 128] = total[0:48]
+
+    place = dp % (NZ * NC)
+    flat = pieces[...].astype(F32)
+
+    def tiles(i):
+        triple = jnp.concatenate([flat[k, 24 * i : 24 * i + 24] for k in range(NZ)], axis=0).astype(BF16)
+        return [triple[j * 64 : (j + 1) * 64] for j in range(3)]
+
+    row = lax.broadcasted_iota(jnp.int32, (128, 128), 0)
+    col = lax.broadcasted_iota(jnp.int32, (128, 128), 1)
+    total = jnp.zeros((64, 128), F32)
+    for i, tile in enumerate(tiles(0) + tiles(1) + tiles(2)):
+        total += nn(tile, jnp.where(row + 128 * i == col + 72 * place, 1.0, 0.0).astype(BF16))
+    up_out[...] = total[:, :72]
+    total = jnp.zeros((128, 64), F32)
+    for i, tile in enumerate(tiles(3)):
+        total += nt(jnp.where(col + 128 * i == row + 24 * place, 1.0, 0.0).astype(BF16), tile)
+    down_out[...] = total[:24]
+    copy.wait()
+
+
+def tail(counts, attn, grad, tok, mod, act, ig, pieces):
+    return pl.pallas_call(
+        tail_kernel,
+        out_shape=(
+            jax.ShapeDtypeStruct((192, 1536), BF16),
+            jax.ShapeDtypeStruct((192, 1536), BF16),
+            jax.ShapeDtypeStruct((24, 64), F32),
+            jax.ShapeDtypeStruct((64, 72), F32),
+            jax.ShapeDtypeStruct((48, 3072), F32),
+        ),
+        in_specs=[pl.BlockSpec(memory_space=pltpu.SMEM), ANY] + [VM] * 6,
+        out_specs=(ANY, VM, VM, VM, VM),
+        scratch_shapes=[pltpu.VMEM((3072, 128), F32), pltpu.SemaphoreType.DMA],
+        compiler_params=pltpu.CompilerParams(vmem_limit_bytes=32 * 1024 * 1024),
+        name="tail",
+    )(counts, attn, grad, tok, mod, act, ig, pieces)
 
 
 def body(
@@ -695,20 +750,21 @@
     adapter_up,
     modulation_matrix,
 ):
-    act = jax.nn.silu(condition[0].astype(F32)).astype(BF16).astype(F32)
-    act = act.reshape(2, NY, NZ, 96).transpose(2, 1, 0, 3)
-    act = jnp.pad(act, ((0, 0), (0, 0), (0, 6), (0, 32)))
-    attention, token_grad, down_grad, up_grad, mod_grad = whole(
-        per_image_rows,
+    counts = per_image_rows.T
+    attn, grad, mod, act, ig, pieces = whole(
+        counts,
         tokens[0],
         cotangent[0],
-        act,
+        condition[0],
         query_key_value_weight,
         adapter_up,
         adapter_down.T,
         modulation_matrix,
     )
-    return attention[None], token_grad[None], down_grad.T, up_grad, mod_grad
+    attention, token_grad, down_grad, up_grad, mod_grad = tail(
+        counts, attn, grad, tokens[0], mod, act, ig, pieces
+    )
+    return attention[None], token_grad[None], down_grad, up_grad, mod_grad
 
 
 def solution(mesh):

time: 123 us -> 116 us (0.943)
  the two profiles are of different devices: /device:TPU:1 before, /device:TPU:4 now
where the time goes in v3:
time: 116 us
  Pallas kernels  108 us (93%)
  local copies, waits for them, and re-layouts  6.5 us (6%)
    pallas_call x1, Pallas kernels, whole(): pl.pallas_call(whole_kernel, out_shape=(jax.ShapeDtypeStruct((192, 1536),...  105 us
    unnamed x16, local copies, waits for them, and re-layouts  6.5 us
    pallas_call x1, Pallas kernels, tail(): pl.pallas_call(tail_kernel, out_shape=(jax.ShapeDtypeStruct((192, 1536),...  3.29 us

profile of v3, /device:TPU:4, one launch (start us, length us, event | category | flops | bytes accessed | tf_op | source)
XLA Modules:
  0.0 115.5 jit_solution(5363414283197656976)
XLA Ops:
  0.6 0.0 copy-start
  0.6 104.9 %whole.1 = (bf16[192,1536]{1,0:T(8,128)(2,1)}, bf16[192,1536]{1,0:T(8,128)(2,1)}, f32[8,3072]{1,0:T(8,128)}, bf16[128,128]{1,0:T(8,128)(2,1)}, bf16[2,4,8,48,128...) custom-call(s32[2,64]{1,0:T(2,128)} %bitcast.9, bf16[192,1536]{1,0:T(8,128)(2,1)} %bitcast.7, bf16[192,1536]{1,0:T(8,128)(2,1)} %bitcast.11, ...), custom_call_target="tpu_custom_call" | custom-call | tf_op jit(solution)/shard_map/whole/pallas_call | solution.py:655
  105.6 0.0 copy-start.7
  105.6 0.0 copy-done
  105.6 0.7 copy-done.7
  106.3 0.0 copy-start.1
  106.3 1.1 copy-done.1
  107.4 0.0 copy-start.2
  107.4 1.1 copy-done.2
  108.5 0.0 copy-start.3
  108.5 1.1 copy-done.3
  109.5 0.0 copy-start.4
  109.5 0.9 copy-done.4
  110.4 0.0 copy-start.5
  110.5 0.9 copy-done.5
  111.3 0.0 copy-start.6
  111.3 0.8 copy-done.6
  112.1 3.3 %tail.1 = (bf16[192,1536]{1,0:T(8,128)(2,1)}, bf16[192,1536]{1,0:T(8,128)(2,1)}, f32[24,64]{1,0:T(8,128)}, f32[64,72]{1,0:T(8,128)}, f32[48,3072]{1,0:T(8,128)}) custom-call(s32[2,64]{1,0:T(2,128)S(1)} %bitcast.10, bf16[192,1536]{1,0:T(8,128)(2,1)S(1)} %copy-done.2, bf16[192,1536]{1,0:T(8,128)(2,1)S(1)} %copy-done.3, bf16[192,1536]{1,0:T(8,128)(2,1)S(1)} %bitcast.8, ...), custom_call_target="tpu_custom_call" | custom-call | tf_op jit(solution)/shard_map/tail/pallas_call | solution.py:726
Async XLA Ops:
  0.6 105.0 %copy-start = (bf16[1,192,1536]{2,1,0:T(8,128)(2,1)S(1)}, bf16[1,192,1536]{2,1,0:T(8,128)(2,1)}, u32[]{:S(2)}) copy-start(bf16[1,192,1536]{2,1,0:T(8,128)(2,1)} %param.8) | copy-start | bytes 1769476
  105.6 0.7 copy-start.7
  106.3 1.1 copy-start.1
  107.4 1.1 copy-start.2
  108.5 1.1 copy-start.3
  109.5 0.9 copy-start.4
  110.4 0.9 copy-start.5
  111.3 0.8 copy-start.6

commit v4 on v3

v4 whole, which is shorter than its diff:
```python
import jax
import jax.numpy as jnp
from jax import lax
from jax.experimental import pallas as pl
from jax.experimental.pallas import tpu as pltpu
from jax.sharding import PartitionSpec as P

HEAD_SIZE = 128
EPSILON = 1e-06
MASKED = -1e30
MESH = pl.DeviceIdType.MESH
NX, NY, NZ, NC = 4, 4, 8, 2
F32, BF16 = jnp.float32, jnp.bfloat16
ANY = pl.BlockSpec(memory_space=pl.ANY)
VM = pl.BlockSpec(memory_space=pltpu.VMEM)


def remote(src, dst, send_sem, recv_sem, device):
    return pltpu.make_async_remote_copy(
        src_ref=src,
        dst_ref=dst,
        send_sem=send_sem,
        recv_sem=recv_sem,
        device_id=device,
        device_id_type=MESH,
    )


class Place:
    def __init__(self):
        self.dp = lax.axis_index("dp")
        self.s = lax.axis_index("seq")
        self.y = self.dp // (NZ * NC)
        self.z = (self.dp // NC) % NZ
        self.c = self.dp % NC

    def at(self, dx=0, dy=0, dz=0, flip=False):
        s = (self.s + dx) % NX if dx else self.s
        y = (self.y + dy) % NY if dy else self.y
        z = (self.z + dz) % NZ if dz else self.z
        c = 1 - self.c if flip else self.c
        return (y * (NZ * NC) + z * NC + c, s)


def enter(me):
    barrier = pltpu.get_barrier_semaphore()
    peers = [me.at(dx=i) for i in range(1, NX)]
    peers += [me.at(dy=i) for i in range(1, NY)]
    peers += [me.at(dz=i) for i in range(1, NZ)]
    peers += [me.at(dy=i, flip=True) for i in range(NY)]
    for peer in peers:
        pl.semaphore_signal(barrier, inc=1, device_id=peer, device_id_type=MESH)
    pl.semaphore_wait(barrier, len(peers))


HALF = 112


class RowGather:
    def __init__(self, me, buf, ysend, yrecv, zsend, zrecv):
        self.me, self.buf = me, buf
        self.ysend, self.yrecv = ysend, yrecv
        self.zsend, self.zrecv = zsend, zrecv
        self.sent = []

    def block(self, at_z, at_y):
        return self.buf.at[self.me.c, at_z, at_y, pl.ds(0, HALF)]

    def launch(self, copy):
        copy.start()
        self.sent.append(copy)

    def start_y(self):
        me = self.me
        own = self.block(me.z, me.y)
        for i in range(1, NY):
            self.launch(remote(own, own, self.ysend.at[i - 1], self.yrecv.at[i - 1], me.at(dy=i)))

    def wait_y(self):
        me = self.me
        for i in range(1, NY):
            block = self.block(me.z, (me.y + NY - i) % NY)
            remote(block, block, self.ysend.at[i - 1], self.yrecv.at[i - 1], me.at(dy=i)).wait_recv()

    def ring(self, way, step, part, arriving):
        me = self.me
        far = step if arriving else step - 1
        source = (me.z + NZ - far) % NZ if way == 0 else (me.z + far) % NZ
        block = self.block(source, part)
        at = (way * 4 + step - 1) * NY + part
        there = me.at(dz=1) if way == 0 else me.at(dz=NZ - 1)
        return remote(block, block, self.zsend.at[at], self.zrecv.at[at], there)

    def carried(self, way, step, part):
        return step < 4 or (part // 2) == way

    def step(self, step):
        for turn in range(NY):
            for way in (0, 1):
                part = turn if way == 0 else NY - 1 - turn
                if step > 1 and self.carried(way, step - 1, part):
                    self.ring(way, step - 1, part, True).wait_recv()
                if step <= 4 and self.carried(way, step, part):
                    self.launch(self.ring(way, step, part, False))


class ColumnGather:
    def __init__(self, me, buf, zsend, zrecv, ysend, yrecv):
        self.me, self.buf = me, buf
        self.ysend, self.yrecv = ysend, yrecv
        self.zsend, self.zrecv = zsend, zrecv
        self.sent = []

    def block(self, shift, at_y):
        return self.buf.at[self.me.c, (self.me.z + shift) % NZ, at_y, pl.ds(HALF, HALF)]

    def launch(self, copy):
        copy.start()
        self.sent.append(copy)

    def ring(self, way, step, arriving):
        far = step if arriving else step - 1
        block = self.block((NZ - far) % NZ if way == 0 else far, self.me.y)
        at = way * 4 + step - 1
        there = self.me.at(dz=1) if way == 0 else self.me.at(dz=NZ - 1)
        return remote(block, block, self.zsend.at[at], self.zrecv.at[at], there)

    def spread(self, shift):
        block = self.block(shift, self.me.y)
        for i in range(1, NY):
            at = shift * (NY - 1) + i - 1
            self.launch(remote(block, block, self.ysend.at[at], self.yrecv.at[at], self.me.at(dy=i)))

    def wait_spread(self, shift):
        for i in range(1, NY):
            block = self.block(shift, (self.me.y + NY - i) % NY)
            at = shift * (NY - 1) + i - 1
            remote(block, block, self.ysend.at[at], self.yrecv.at[at], self.me.at(dy=i)).wait_recv()

    def step(self, step):
        for way in (0, 1):
            last = 4 - way
            if 1 < step <= last + 1:
                self.ring(way, step - 1, True).wait_recv()
            if step <= last:
                self.launch(self.ring(way, step, False))
        if step == 1:
            self.spread(0)
        else:
            self.spread(NZ - step + 1)
            if step < 5:
                self.spread(step - 1)


class CoreSwap:
    def __init__(self, me, buf, send, recv):
        self.me, self.buf, self.send, self.recv = me, buf, send, recv
        self.sent = []

    def copy(self, at_c, shift):
        block = self.buf.at[at_c, (self.me.z + shift) % NZ]
        return remote(block, block, self.send.at[shift], self.recv.at[shift], self.me.at(flip=True))

    def start(self, shift):
        copy = self.copy(self.me.c, shift)
        copy.start()
        self.sent.append(copy)

    def wait(self, shift):
        self.copy(1 - self.me.c, shift).wait_recv()


def exchange(me, axis, count, source, slots, send, recv):
    copies = []
    for i in range(1, count):
        copy = remote(source(i), slots.at[i - 1], send.at[i - 1], recv.at[i - 1], me.at(**{axis: i}))
        copy.start()
        copies.append(copy)
    return copies


def exchange_at(me, axis, count, source, target, send, recv):
    copies = []
    for i in range(1, count):
        copy = remote(source(i), target, send.at[i - 1], recv.at[i - 1], me.at(**{axis: i}))
        copy.start()
        copies.append(copy)
    return copies


def nt(a, b):
    return lax.dot_general(a, b, (((1,), (1,)), ((), ())), preferred_element_type=F32)


def tn(a, b):
    return lax.dot_general(a, b, (((0,), (0,)), ((), ())), preferred_element_type=F32)


def nn(a, b):
    return jnp.dot(a, b, preferred_element_type=F32)


def sorting(c0, c1, rows):
    here = lax.broadcasted_iota(jnp.int32, (rows, rows), 0)
    source = lax.broadcasted_iota(jnp.int32, (rows, rows), 1)
    later = here >= rows // 2
    rank = jnp.where(later, here - rows // 2, here)
    live = rank < jnp.where(later, c1, c0)
    return jnp.where((source == rank + jnp.where(later, c0, 0)) & live, 1.0, 0.0).astype(BF16)


def aligned(start, size):
    return pl.ds(pl.multiple_of(start, 128), size)


class Refs:
    pass


SCRATCH = dict(
    tok_all=pltpu.VMEM((NX, 192, 1536), BF16),
    cot_all=pltpu.VMEM((NX, 192, 384), BF16),
    w_all=pltpu.VMEM((NC, NZ, NY, 224, 128), BF16),
    w=pltpu.VMEM((1536, 1152), BF16),
    up=pltpu.VMEM((64, 1152), BF16),
    down=pltpu.VMEM((64, 1536), BF16),
    mm=pltpu.VMEM((256, 768), BF16),
    a_rows=pltpu.VMEM((NZ, 16, 128), F32),
    a_src=pltpu.VMEM((NZ, 16, 128), BF16),
    a_z=pltpu.VMEM((NZ, 16, 128), BF16),
    a_turn=pltpu.VMEM((NY, 32, 128), F32),
    a_low=pltpu.VMEM((NY, 32, 128), BF16),
    a_y=pltpu.VMEM((NC, NY, 32, 128), BF16),
    a_wide=pltpu.VMEM((256, 128), F32),
    a_pair=pltpu.VMEM((128, 256), BF16),
    part_wide=pltpu.VMEM((768, 128), F32),
    part_low=pltpu.VMEM((NC, NY, 96, 128), BF16),
    m_in=pltpu.VMEM((7, 96, 128), BF16),
    m_plane=pltpu.VMEM((NZ, 16, 128), F32),
    m_z=pltpu.VMEM((NZ - 1, 16, 128), F32),
    m_own=pltpu.VMEM((16, 128), F32),
    m_all=pltpu.VMEM((NX, 16, 128), F32),
    modded=pltpu.VMEM((768, 1536), BF16),
    stats=pltpu.VMEM((768, 128), F32),
    low=pltpu.VMEM((768, 64), BF16),
    proj=pltpu.VMEM((768, 1152), BF16),
    proj_grad=pltpu.VMEM((768, 1152), BF16),
    low_grad=pltpu.VMEM((768, 64), BF16),
    cot_own=pltpu.VMEM((192, 1536), BF16),
    attn=pltpu.VMEM((NX, 2, 96, 384), BF16),
    pg=pltpu.VMEM((2, NX, 96, 1536), BF16),
    ip=pltpu.VMEM((8, 3072), F32),
    half_l=pltpu.VMEM((2, 48, 1536), BF16),
    half_r=pltpu.VMEM((2, 48, 1536), BF16),
    comb_l=pltpu.VMEM((2, 48, 1536), BF16),
    comb_r=pltpu.VMEM((2, 48, 1536), BF16),
    from_l=pltpu.VMEM((2, 96, 1536), BF16),
    from_r=pltpu.VMEM((2, 96, 1536), BF16),
    ip_own=pltpu.VMEM((48, 128), F32),
    ip_in=pltpu.VMEM((3, 48, 128), F32),
    lo=pltpu.VMEM((NY, 2, 192, 128), BF16),
    l_y=pltpu.VMEM((NY - 1, 2, 192, 128), BF16),
    l_plane=pltpu.VMEM((NZ, 48, 128), BF16),
    l_z=pltpu.VMEM((NZ - 1, 48, 128), BF16),
    l_own=pltpu.VMEM((48, 128), F32),
    l_core=pltpu.VMEM((48, 128), F32),
    l_piece=pltpu.VMEM((48, 128), BF16),
    l_x=pltpu.VMEM((NX, 48, 128), BF16),
)
PAIRS = dict(tk=12, ck=6, az=7, ay=7, my=7, mz=7, mx=3, gr=12, ot=6, ip=3, iz=7, iy=3, ic=1, ly=3, lz=7, lc=1, lx=3, lg=7)
PLANES = dict(wy=3, wz=32, vz=8, vy=24, wc=8)
LOCAL = 8


def scratch_list():
    dma = pltpu.SemaphoreType.DMA
    out = list(SCRATCH.values())
    for count in PAIRS.values():
        out += [dma((count,)), dma((count,))]
    for count in PLANES.values():
        out += [dma((count,)), dma((count,))]
    return out + [dma((LOCAL,))]


def named(refs):
    r = Refs()
    refs = list(refs)
    for name in SCRATCH:
        setattr(r, name, refs.pop(0))
    for name in PAIRS:
        setattr(r, name + "_s", refs.pop(0))
        setattr(r, name + "_r", refs.pop(0))
    for name in PLANES:
        setattr(r, name, [refs.pop(0), refs.pop(0)])
    r.local = refs.pop(0)
    return r


def whole_kernel(
    rows_ref, tok, cot, cond, wq, up_in, down_in, mm_in,
    attn_out, grad_out, mod, a_own, ig_all, f_all,
    *refs,
):
    r = named(refs)
    me = Place()
    s, y, z, c = me.s, me.y, me.z, me.c
    rows, width, att, heads = 192, 1536, 384, 3
    part = rows // 2
    image_rows = NX * part
    chunk = rows // 4
    scale = HEAD_SIZE ** (-0.5)
    right, left = me.at(dx=1), me.at(dx=NX - 1)
    sl, sr, so = (s + NX - 1) % NX, (s + 1) % NX, (s + 2) % NX
    c0, c1 = rows_ref[0, me.dp], rows_ref[1, me.dp]

    offset = 48 * me.dp - 128 * ((96 * (me.dp // 2)) // 128)
    r.mm[...] = jnp.zeros_like(r.mm)
    locals_ = [
        pltpu.make_async_copy(
            mm_in.at[:, aligned(s * 768, 768)], r.mm.at[pl.ds(pl.multiple_of(offset, 16), 48)], r.local.at[0]
        ),
        pltpu.make_async_copy(down_in, r.down, r.local.at[1]),
    ]
    for b in range(3):
        locals_.append(
            pltpu.make_async_copy(
                up_in.at[:, aligned(b * width + s * att, att)], r.up.at[:, b * att : (b + 1) * att], r.local.at[2 + b]
            )
        )
    for copy in locals_:
        copy.start()
    pieces = []
    for b in range(3):
        block = wq[:, aligned(b * width + s * att, att)].astype(F32)
        pieces += [block[:, i * 128 : (i + 1) * 128] for i in range(3)]
    pieces.append(jnp.zeros((8, 128), F32))
    r.w_all[c, z, y] = jnp.concatenate(pieces, axis=0).astype(BF16)
    wide = cond[...].astype(F32)
    wide = (wide / (1.0 + jnp.exp(-wide))).astype(BF16).astype(F32)
    r.a_rows[...] = jnp.zeros_like(r.a_rows)
    for p in range(NZ * NY):
        j = (96 * p) // 128
        for img in range(2):
            for t in range(2):
                if j + t < 24:
                    at = 4 * (p // NZ) + 2 * img + t
                    r.a_rows[p % NZ, at : at + 1, :] = wide[img : img + 1, (j + t) * 128 : (j + t + 1) * 128]
    r.a_src[...] = r.a_rows[...].astype(BF16)
    r.a_z[z] = r.a_src[z]
    r.m_plane[...] = jnp.zeros_like(r.m_plane)
    perm = sorting(c0, c1, rows)
    r.tok_all[s] = nn(perm, tok[...]).astype(BF16)

    enter(me)

    sent = []

    def arrived(copies):
        for copy in copies:
            copy.wait_recv()
            sent.append(copy)

    az = exchange_at(me, "dz", NZ, lambda i: r.a_src.at[(z + i) % NZ], r.a_z.at[z], r.az_s, r.az_r)
    weights = RowGather(me, r.w_all, *r.wy, *r.wz)
    weights.start_y()
    others = ColumnGather(me, r.w_all, *r.vz, *r.vy)
    others.step(1)
    swap = CoreSwap(me, r.w_all, *r.wc)

    def row_chunk(i):
        return pl.ds(i * chunk, chunk)

    def token_copy(source, owner, i, slot, there):
        return remote(source, r.tok_all.at[owner, row_chunk(i)], r.tk_s.at[slot], r.tk_r.at[slot], there)

    def launch(copy):
        copy.start()
        sent.append(copy)

    def own_tokens(img):
        i = 2 * img
        launch(token_copy(r.tok_all.at[s, row_chunk(i)], s, i, i, right))
        launch(token_copy(r.tok_all.at[s, row_chunk(i + 1)], s, i + 1, 4 + i + 1, left))
        launch(token_copy(r.tok_all.at[s, row_chunk(i + 1)], s, i + 1, i + 1, right))
        launch(token_copy(r.tok_all.at[s, row_chunk(i)], s, i, 4 + i, left))

    def forward(img):
        i = 2 * img
        token_copy(r.tok_all.at[s, row_chunk(i)], sl, i, i, right).wait_recv()
        launch(token_copy(r.tok_all.at[sl, row_chunk(i)], sl, i, 8 + i, right))
        i = i + 1
        token_copy(r.tok_all.at[s, row_chunk(i)], sr, i, 4 + i, left).wait_recv()
        launch(token_copy(r.tok_all.at[sr, row_chunk(i)], sr, i, 8 + i, left))

    def wait_tokens(img):
        i = 2 * img
        own = r.tok_all.at[s, row_chunk(i)]
        token_copy(own, sl, i + 1, i + 1, right).wait_recv()
        token_copy(own, sr, i, 4 + i, left).wait_recv()
        token_copy(own, so, i, 8 + i, right).wait_recv()
        token_copy(own, so, i + 1, 8 + i + 1, left).wait_recv()

    def cot_copy(img, i, columns, source):
        at = pl.ds(img * part, part)
        return remote(
            r.cot_own.at[at, columns], r.cot_all.at[source, at],
            r.ck_s.at[3 * img + i - 1], r.ck_r.at[3 * img + i - 1], me.at(dx=i),
        )

    def own_cotangent(img):
        for i in range(1, NX):
            launch(cot_copy(img, i, aligned(((s + i) % NX) * att, att), s))

    def wait_cotangent(img):
        for i in range(1, NX):
            cot_copy(img, i, aligned(0, att), (s + NX - i) % NX).wait_recv()

    own_tokens(0)
    r.cot_own[...] = nn(perm, cot[...]).astype(BF16)
    arrived(az)
    turned = r.a_z[...].astype(F32)
    for at_y in range(NY):
        for at_z in range(NZ):
            r.a_turn[at_y, 4 * at_z : 4 * at_z + 4, :] = turned[at_z, 4 * at_y : 4 * at_y + 4]
    r.a_low[...] = r.a_turn[...].astype(BF16)
    r.a_y[c, y] = r.a_low[y]

    def plane_exchange(source, target, send, recv):
        copies = []
        for i in range(1, 2 * NY):
            dy, flip = i // 2, i % 2 == 1
            there = (y + dy) % NY
            at = (1 - c) if flip else c
            copy = remote(
                source(at, there), target(i - 1), send.at[i - 1], recv.at[i - 1], me.at(dy=dy, flip=flip)
            )
            copy.start()
            copies.append(copy)
        return copies

    ay = plane_exchange(lambda at, there: r.a_low.at[there], lambda i: r.a_y.at[c, y], r.ay_s, r.ay_r)
    weights.wait_y()
    weights.step(1)
    others.step(2)
    arrived(ay)
    locals_[0].wait()
    r.a_wide[...] = r.a_y[...].reshape(256, 128).astype(F32)
    for img in range(2):
        for t in range(2):
            r.a_pair[img * 64 : (img + 1) * 64, t * 128 : (t + 1) * 128] = r.a_wide[
                pl.ds(2 * img + t, 64, stride=4), :
            ].astype(BF16)
    for j in range(6):
        columns = nn(r.a_pair[...], r.mm[:, j * 128 : (j + 1) * 128])
        for img in range(2):
            r.part_wide[pl.ds(img * 6 + j, 64, stride=12), :] = columns[img * 64 : (img + 1) * 64]
    r.part_low[...] = r.part_wide[...].astype(BF16).reshape(r.part_low.shape)
    my = plane_exchange(lambda at, there: r.part_low.at[at, there], lambda i: r.m_in.at[i], r.my_s, r.my_r)
    forward(0)
    own_cotangent(0)
    own_tokens(1)
    others.step(3)
    row = lax.broadcasted_iota(jnp.int32, (256, 128), 0)
    col = lax.broadcasted_iota(jnp.int32, (256, 128), 1)
    pick = jnp.where((row == col + offset) & (col < 48), 1.0, 0.0).astype(BF16)
    a_own[...] = nn(r.a_pair[...], pick).astype(BF16)
    weights.step(2)
    r.cot_all[s] = r.cot_own[:, aligned(s * att, att)]
    arrived(my)
    total = r.part_low[c, y].astype(F32)
    for i in range(7):
        total += r.m_in[i].astype(F32)
    for at_z in range(NZ):
        r.m_plane[at_z, 0:12, :] = total[12 * at_z : 12 * at_z + 12]
    mz = exchange(me, "dz", NZ, lambda i: r.m_plane.at[(z + i) % NZ], r.m_z, r.mz_s, r.mz_r)
    others.step(4)
    weights.step(3)
    arrived(mz)
    total = r.m_plane[z]
    for i in range(NZ - 1):
        total += r.m_z[i]
    r.m_own[...] = total
    r.m_all[s] = total
    mx = exchange_at(me, "dx", NX, lambda i: r.m_own, r.m_all.at[s], r.mx_s, r.mx_r)
    others.step(5)
    weights.step(4)
    for shift in (0, 1, NZ - 1, 2, NZ - 2):
        others.wait_spread(shift)
        swap.start(shift)

    def place(shift):
        swap.wait(shift)
        at_z = (z + shift) % NZ

        @pl.loop(0, NY)
        def _(at_y):
            first = r.w_all[0, at_z, at_y].astype(F32)
            other = r.w_all[1, at_z, at_y].astype(F32)
            at = pl.ds(pl.multiple_of(48 * (NZ * at_y + at_z), 16), 48)
            for t in range(9):
                both = jnp.concatenate([first[24 * t : 24 * t + 24], other[24 * t : 24 * t + 24]], axis=0)
                r.w[at, t * 128 : (t + 1) * 128] = both.astype(BF16)

    arrived(mx)
    mod[...] = jnp.zeros_like(mod)
    for k in range(NX):
        for img in range(2):
            for j in range(6):
                at = 768 * k + 128 * j
                mod[img : img + 1, at : at + 128] = r.m_all[k, img * 6 + j : img * 6 + j + 1, :]

    def normalize(img):
        @pl.loop(0, NX)
        def _(block):
            x = r.tok_all[block, img * part : (img + 1) * part, :].astype(F32)
            mean = jnp.mean(x, axis=1, keepdims=True)
            centred = x - mean
            inverse = lax.rsqrt(jnp.mean(centred * centred, axis=1, keepdims=True) + EPSILON)
            rank = lax.broadcasted_iota(jnp.int32, (part, 1), 0)
            gain = 1.0 + mod[img : img + 1, width:]
            value = gain * (centred * inverse) + mod[img : img + 1, :width]
            at = pl.ds(pl.multiple_of(img * image_rows + block * part, 32), part)
            r.modded[at, :] = jnp.where(rank < (c0, c1)[img], value, 0.0).astype(BF16)
            r.stats[at, 0:1] = mean
            r.stats[at, 1:2] = inverse

    weights.step(5)
    for shift in (3, 5, 4):
        others.wait_spread(shift)
        swap.start(shift)
    wait_tokens(0)
    normalize(0)
    forward(1)
    own_cotangent(1)
    for shift in (0, 1, NZ - 1, 2, NZ - 2, 3, 5, 4):
        place(shift)
    for copy in locals_[1:]:
        copy.wait()

    def project(img):
        at = slice(img * image_rows, (img + 1) * image_rows)
        r.low[at, :] = nt(r.modded[at, :], r.down[...]).astype(BF16)

        @pl.loop(0, 3)
        def _(n):
            cols = aligned(n * att, att)
            r.proj[at, cols] = (nn(r.modded[at, :], r.w[:, cols]) + nn(r.low[at, :], r.up[:, cols])).astype(BF16)

    lane = lax.broadcasted_iota(jnp.int32, (1, image_rows), 1)
    for _ in range(NX - 1):
        lane = jnp.where(lane >= part, lane - part, lane)

    def attend(img):
        at = slice(img * image_rows, (img + 1) * image_rows)
        allowed = lane < (c0, c1)[img]
        for h in range(heads):
            cols = slice(h * 128, (h + 1) * 128)
            key_cols = slice(att + h * 128, att + (h + 1) * 128)
            value_cols = slice(2 * att + h * 128, 2 * att + (h + 1) * 128)
            q, k, v = r.proj[at, cols], r.proj[at, key_cols], r.proj[at, value_cols]
            scores = jnp.where(allowed, nt(q, k), MASKED)
            largest = jnp.max(scores, axis=1, keepdims=True)
            raw = jnp.exp((scores - largest) * scale)
            probs = raw * (1.0 / jnp.sum(raw, axis=1, keepdims=True))
            probs_low = probs.astype(BF16)
            out = nn(probs_low, v).astype(BF16)
            r.attn[:, img, :, cols] = out.reshape(NX, part, 128)
            out_grad = r.cot_all[:, img * part : (img + 1) * part, cols].reshape(image_rows, 128)
            delta = jnp.sum(out_grad.astype(F32) * out.astype(F32), axis=1, keepdims=True)
            score_grads = (probs * (nt(out_grad, v) - delta)).astype(BF16)
            r.proj_grad[at, cols] = (nn(score_grads, k) * scale).astype(BF16)
            r.proj_grad[at, key_cols] = (tn(q, score_grads) * scale).T.astype(BF16)
            r.proj_grad[at, value_cols] = tn(out_grad, probs_low).T.astype(BF16)

    mine = aligned(s * att, att)

    def give(img):
        for i in range(1, NX):
            there = me.at(dx=i)
            launch(
                remote(
                    r.attn.at[there[1], img],
                    attn_out.at[img * part : (img + 1) * part, mine],
                    r.ot_s.at[3 * img + i - 1], r.ot_r.at[3 * img + i - 1], there,
                )
            )
        attn_out[img * part : (img + 1) * part, mine] = r.attn[s, img]

    def grads(img):
        at = slice(img * image_rows, (img + 1) * image_rows)
        r.low_grad[at, :] = nt(r.proj_grad[at, :], r.up[...]).astype(BF16)

        @pl.loop(0, width // att)
        def _(n):
            f = aligned(n * att, att)
            grad = nt(r.proj_grad[at, :], r.w[f, :]) + nn(r.low_grad[at, :], r.down[:, f])
            r.pg[img, :, :, f] = grad.astype(BF16).reshape(NX, part, att)
            x = r.tok_all[:, img * part : (img + 1) * part, f].reshape(image_rows, att).astype(F32)
            normed = (x - r.stats[at, 0:1]) * r.stats[at, 1:2]
            r.ip[img : img + 1, f] = jnp.sum(grad, axis=0, keepdims=True)
            r.ip[img : img + 1, aligned(width + n * att, att)] = jnp.sum(grad * normed, axis=0, keepdims=True)

    half = part // 2
    first, second = pl.ds(0, half), pl.ds(half, half)

    def grad_copy(img, slot):
        src, dst, there = (
            (r.pg.at[img, so, first], r.half_l.at[img], right),
            (r.pg.at[img, so, second], r.half_r.at[img], left),
            (r.pg.at[img, sr, second], r.from_l.at[img, second], right),
            (r.pg.at[img, sl, first], r.from_r.at[img, first], left),
            (r.comb_r.at[img], r.from_l.at[img, first], right),
            (r.comb_l.at[img], r.from_r.at[img, second], left),
        )[slot]
        return remote(src, dst, r.gr_s.at[6 * img + slot], r.gr_r.at[6 * img + slot], there)

    def reduce_first(img):
        for slot in range(4):
            launch(grad_copy(img, slot))

    def reduce_second(img):
        grad_copy(img, 0).wait_recv()
        r.comb_r[img] = (r.pg[img, sr, 0:half].astype(F32) + r.half_l[img].astype(F32)).astype(BF16)
        launch(grad_copy(img, 4))
        grad_copy(img, 1).wait_recv()
        r.comb_l[img] = (r.pg[img, sl, half:part].astype(F32) + r.half_r[img].astype(F32)).astype(BF16)
        launch(grad_copy(img, 5))

    project(0)
    wait_cotangent(0)
    attend(0)
    give(0)
    grads(0)
    reduce_first(0)
    wait_tokens(1)
    normalize(1)
    project(1)
    wait_cotangent(1)
    attend(1)
    give(1)
    reduce_second(0)
    grads(1)
    reduce_first(1)

    for img in range(2):
        for j in range(24):
            r.ip_own[img * 24 + j : img * 24 + j + 1, :] = r.ip[img : img + 1, j * 128 : (j + 1) * 128]
    ip = exchange(me, "dx", NX, lambda i: r.ip_own, r.ip_in, r.ip_s, r.ip_r)

    r.lo[NX - 1 - s, 0] = jnp.zeros((192, 128), BF16)
    up_total = tn(r.low[...], r.proj_grad[...]).astype(BF16)
    for t in range(9):
        r.lo[(4 * (t // 3) + s) // 3, 0, (t % 3) * 64 : (t % 3 + 1) * 64, :] = up_total[:, t * 128 : (t + 1) * 128]
    down_total = tn(r.low_grad[...], r.modded[...]).astype(BF16)
    for t in range(12):
        r.lo[t // 3, 1, (t % 3) * 64 : (t % 3 + 1) * 64, :] = down_total[:, t * 128 : (t + 1) * 128]
    ly = exchange(me, "dy", NY, lambda i: r.lo.at[(y + i) % NY], r.l_y, r.ly_s, r.ly_r)

    reduce_second(1)

    arrived(ly)
    total = r.lo[y].astype(F32)
    for i in range(NY - 1):
        total += r.l_y[i].astype(F32)
    for i in range(NZ):
        at = slice(24 * i, 24 * i + 24)
        r.l_plane[i] = jnp.concatenate([total[0, at], total[1, at]], axis=0).astype(BF16)
    lz = exchange(me, "dz", NZ, lambda i: r.l_plane.at[(z + i) % NZ], r.l_z, r.lz_s, r.lz_r)

    arrived(ip)
    ig_all[c, y, z] = (r.ip_own[...] + r.ip_in[0] + r.ip_in[1] + r.ip_in[2]).astype(BF16)
    own_ig = ig_all.at[c, y, z]
    iz = exchange_at(me, "dz", NZ, lambda i: own_ig, own_ig, r.iz_s, r.iz_r)

    arrived(lz)
    total = r.l_plane[z].astype(F32)
    for i in range(NZ - 1):
        total += r.l_z[i].astype(F32)
    r.l_own[...] = total
    lc = remote(r.l_own, r.l_core, r.lc_s.at[0], r.lc_r.at[0], me.at(flip=True))
    lc.start()

    arrived(iz)
    column = ig_all.at[c, y]
    iy = exchange_at(me, "dy", NY, lambda i: column, column, r.iy_s, r.iy_r)

    arrived([lc])
    r.l_piece[...] = (r.l_own[...] + r.l_core[...]).astype(BF16)
    r.l_x[s] = r.l_piece[...]
    lx = exchange_at(me, "dx", NX, lambda i: r.l_piece, r.l_x.at[s], r.lx_s, r.lx_r)

    arrived(iy)
    ic = remote(ig_all.at[c], ig_all.at[c], r.ic_s.at[0], r.ic_r.at[0], me.at(flip=True))
    ic.start()

    arrived(lx)
    pieces = [r.l_x[(3 * y + i) % 4].astype(F32)[0:24] for i in range(3)]
    total = r.l_x[0].astype(F32)[24:48]
    for i in range(1, NX):
        total += r.l_x[i].astype(F32)[24:48]
    f_all[z] = jnp.concatenate(pieces + [total], axis=0).astype(BF16)
    lg = exchange_at(me, "dz", NZ, lambda i: f_all.at[z], f_all.at[z], r.lg_s, r.lg_r)

    for img in range(2):
        for slot in range(2, 6):
            grad_copy(img, slot).wait_recv()
        grad_out[img * part : (img + 1) * part, :] = (
            r.pg[img, s].astype(F32) + r.from_l[img].astype(F32) + r.from_r[img].astype(F32)
        ).astype(BF16)
    arrived([ic])
    arrived(lg)

    for copy in sent:
        copy.wait_send()
    for img in range(2):
        for i in range(1, NX):
            remote(
                r.attn.at[0, img],
                attn_out.at[img * part : (img + 1) * part, aligned(((s + NX - i) % NX) * att, att)],
                r.ot_s.at[3 * img + i - 1], r.ot_r.at[3 * img + i - 1], right,
            ).wait_recv()
    for copy in weights.sent + others.sent + swap.sent:
        copy.wait_send()


def whole(counts, tok, cot, cond, wq, up, down, mm):
    return pl.pallas_call(
        whole_kernel,
        out_shape=(
            jax.ShapeDtypeStruct((192, 1536), BF16),
            jax.ShapeDtypeStruct((192, 1536), BF16),
            jax.ShapeDtypeStruct((8, 3072), F32),
            jax.ShapeDtypeStruct((128, 128), BF16),
            jax.ShapeDtypeStruct((NC, NY, NZ, 48, 128), BF16),
            jax.ShapeDtypeStruct((NZ, 96, 128), BF16),
        ),
        in_specs=[pl.BlockSpec(memory_space=pltpu.SMEM), VM, VM, VM, VM, ANY, ANY, ANY],
        out_specs=(VM, VM, VM, VM, VM, VM),
        scratch_shapes=scratch_list(),
        compiler_params=pltpu.CompilerParams(
            collective_id=1, has_side_effects=True, vmem_limit_bytes=60 * 1024 * 1024
        ),
        name="whole",
    )(counts, tok, cot, cond, wq, up, down, mm)


def tail_kernel(
    counts, attn, grad, tok, mod, act, ig, pieces,
    attn_out, token_grad, down_out, up_out, mod_grad,
    ig_wide, sorted_grad,
):
    rows, width = tok.shape
    part = rows // 2
    dp = lax.axis_index("dp")
    perm = sorting(counts[0, dp], counts[1, dp], rows)
    attn_out[...] = tn(perm, attn[...]).astype(BF16)
    for img in range(2):
        at = slice(img * part, (img + 1) * part)
        x = nn(perm[at], tok[...])
        centred = x - jnp.mean(x, axis=1, keepdims=True)
        inverse = lax.rsqrt(jnp.mean(centred * centred, axis=1, keepdims=True) + EPSILON)
        normed = centred * inverse
        g = (1.0 + mod[img : img + 1, width:]) * grad[at, :].astype(F32)
        sorted_grad[at, :] = (
            inverse
            * (g - jnp.mean(g, axis=1, keepdims=True) - normed * jnp.mean(g * normed, axis=1, keepdims=True))
        ).astype(BF16)
    token_grad[...] = tn(perm, sorted_grad[...]).astype(BF16)

    ig_wide[...] = ig[...].reshape(3072, 128).astype(F32)
    for j in range(24):
        total = jnp.zeros((128, 128), F32)
        for img in range(2):
            part = ig_wide[pl.ds(img * 24 + j, 64, stride=48), :].astype(BF16)
            total += tn(act[img * 64 : (img + 1) * 64], part)
        mod_grad[:, j * 128 : (j + 1) * 128] = total[0:48]

    place = dp % (NZ * NC)
    flat = pieces[...].astype(F32)

    def tiles(i):
        triple = jnp.concatenate([flat[k, 24 * i : 24 * i + 24] for k in range(NZ)], axis=0).astype(BF16)
        return [triple[j * 64 : (j + 1) * 64] for j in range(3)]

    row = lax.broadcasted_iota(jnp.int32, (128, 128), 0)
    col = lax.broadcasted_iota(jnp.int32, (128, 128), 1)
    total = jnp.zeros((64, 128), F32)
    for i, tile in enumerate(tiles(0) + tiles(1) + tiles(2)):
        total += nn(tile, jnp.where(row + 128 * i == col + 72 * place, 1.0, 0.0).astype(BF16))
    up_out[...] = total[:, :72]
    total = jnp.zeros((128, 64), F32)
    for i, tile in enumerate(tiles(3)):
        total += nt(jnp.where(col + 128 * i == row + 24 * place, 1.0, 0.0).astype(BF16), tile)
    down_out[...] = total[:24]


def tail(counts, attn, grad, tok, mod, act, ig, pieces):
    return pl.pallas_call(
        tail_kernel,
        out_shape=(
            jax.ShapeDtypeStruct((192, 1536), BF16),
            jax.ShapeDtypeStruct((192, 1536), BF16),
            jax.ShapeDtypeStruct((24, 64), F32),
            jax.ShapeDtypeStruct((64, 72), F32),
            jax.ShapeDtypeStruct((48, 3072), F32),
        ),
        in_specs=[pl.BlockSpec(memory_space=pltpu.SMEM)] + [VM] * 7,
        out_specs=(VM, VM, VM, VM, VM),
        scratch_shapes=[pltpu.VMEM((3072, 128), F32), pltpu.VMEM((192, 1536), BF16)],
        compiler_params=pltpu.CompilerParams(vmem_limit_bytes=60 * 1024 * 1024),
        name="tail",
    )(counts, attn, grad, tok, mod, act, ig, pieces)


def body(
    tokens,
    cotangent,
    condition,
    per_image_rows,
    query_key_value_weight,
    adapter_down,
    adapter_up,
    modulation_matrix,
):
    counts = per_image_rows.T
    attn, grad, mod, act, ig, pieces = whole(
        counts,
        tokens[0],
        cotangent[0],
        condition[0],
        query_key_value_weight,
        adapter_up,
        adapter_down.T,
        modulation_matrix,
    )
    attention, token_grad, down_grad, up_grad, mod_grad = tail(
        counts, attn, grad, tokens[0], mod, act, ig, pieces
    )
    return attention[None], token_grad[None], down_grad, up_grad, mod_grad


def solution(mesh):
    in_specs = (
        P("dp", "seq", None),
        P("dp", "seq", None),
        P("dp", None, None),
        P(),
        P("dp", None),
        P(),
        P(),
        P("dp", None),
    )
    out_specs = (
        P("dp", "seq", None),
        P("dp", "seq", None),
        P("dp", None),
        P(None, "dp"),
        P("dp", None),
    )
    return jax.shard_map(body, mesh=mesh, in_specs=in_specs, out_specs=out_specs, check_vma=False)
```

time: 116 us -> 97 us (0.84)
  the two profiles are of different devices: /device:TPU:4 before, /device:TPU:16 now
where the time goes in v4:
time: 97 us; the launch traced here: 96.8 us
  Pallas kernels  96.2 us (99%)
    pallas_call x1, Pallas kernels, whole(): pl.pallas_call(whole_kernel, out_shape=(jax.ShapeDtypeStruct((192, 1536),...  91.4 us
    pallas_call x1, Pallas kernels, tail(): pl.pallas_call(tail_kernel, out_shape=(jax.ShapeDtypeStruct((192, 1536),...  4.75 us

profile of v4, /device:TPU:16, one launch (start us, length us, event | category | flops | bytes accessed | tf_op | source)
XLA Modules:
  0.0 96.8 jit_solution(1831214581065190323)
XLA Ops:
  0.6 91.4 %whole.1 = (bf16[192,1536]{1,0:T(8,128)(2,1)}, bf16[192,1536]{1,0:T(8,128)(2,1)}, f32[8,3072]{1,0:T(8,128)}, bf16[128,128]{1,0:T(8,128)(2,1)}, bf16[2,4,8,48,128...) custom-call(s32[2,64]{1,0:T(2,128)} %bitcast.12, bf16[192,1536]{1,0:T(8,128)(2,1)} %bitcast.7, bf16[192,1536]{1,0:T(8,128)(2,1)} %bitcast.9, ...), custom_call_target="tpu_custom_call" | custom-call | tf_op jit(solution)/shard_map/whole/pallas_call | solution.py:727
  92.1 4.7 %tail.1 = (bf16[192,1536]{1,0:T(8,128)(2,1)}, bf16[192,1536]{1,0:T(8,128)(2,1)}, f32[24,64]{1,0:T(8,128)}, f32[64,72]{1,0:T(8,128)}, f32[48,3072]{1,0:T(8,128)}) custom-call(s32[2,64]{1,0:T(2,128)} %bitcast.13, bf16[192,1536]{1,0:T(8,128)(2,1)} %get-tuple-element.16.attn, bf16[192,1536]{1,0:T(8,128)(2,1)} %get-tuple-element.17.grad, ...), custom_call_target="tpu_custom_call" | custom-call | tf_op jit(solution)/shard_map/tail/pallas_call | solution.py:798

commit v5 on v4

--- a/solution.py
+++ b/solution.py
@@ -42,15 +42,22 @@
         return (y * (NZ * NC) + z * NC + c, s)
 
 
-def enter(me):
-    barrier = pltpu.get_barrier_semaphore()
+def peers_of(me):
     peers = [me.at(dx=i) for i in range(1, NX)]
+    peers += [me.at(dx=i, flip=True) for i in range(1, NX)]
     peers += [me.at(dy=i) for i in range(1, NY)]
     peers += [me.at(dz=i) for i in range(1, NZ)]
     peers += [me.at(dy=i, flip=True) for i in range(NY)]
-    for peer in peers:
-        pl.semaphore_signal(barrier, inc=1, device_id=peer, device_id_type=MESH)
-    pl.semaphore_wait(barrier, len(peers))
+    return peers
+
+
+def greet(me):
+    for peer in peers_of(me):
+        pl.semaphore_signal(pltpu.get_barrier_semaphore(), inc=1, device_id=peer, device_id_type=MESH)
+
+
+def enter(me):
+    pl.semaphore_wait(pltpu.get_barrier_semaphore(), len(peers_of(me)))
 
 
 HALF = 112
@@ -218,6 +225,8 @@
 
 
 SCRATCH = dict(
+    tok_raw=pltpu.VMEM((192, 1536), BF16),
+    cot_raw=pltpu.VMEM((192, 1536), BF16),
     tok_all=pltpu.VMEM((NX, 192, 1536), BF16),
     cot_all=pltpu.VMEM((NX, 192, 384), BF16),
     w_all=pltpu.VMEM((NC, NZ, NY, 224, 128), BF16),
@@ -256,18 +265,16 @@
     comb_r=pltpu.VMEM((2, 48, 1536), BF16),
     from_l=pltpu.VMEM((2, 96, 1536), BF16),
     from_r=pltpu.VMEM((2, 96, 1536), BF16),
-    ip_own=pltpu.VMEM((48, 128), F32),
-    ip_in=pltpu.VMEM((3, 48, 128), F32),
+    ip_own=pltpu.VMEM((2, 24, 128), F32),
+    ip_in=pltpu.VMEM((2, 3, 24, 128), F32),
     lo=pltpu.VMEM((NY, 2, 192, 128), BF16),
     l_y=pltpu.VMEM((NY - 1, 2, 192, 128), BF16),
     l_plane=pltpu.VMEM((NZ, 48, 128), BF16),
     l_z=pltpu.VMEM((NZ - 1, 48, 128), BF16),
-    l_own=pltpu.VMEM((48, 128), F32),
-    l_core=pltpu.VMEM((48, 128), F32),
     l_piece=pltpu.VMEM((48, 128), BF16),
-    l_x=pltpu.VMEM((NX, 48, 128), BF16),
+    l_x=pltpu.VMEM((NC, NX, 48, 128), BF16),
 )
-PAIRS = dict(tk=12, ck=6, az=7, ay=7, my=7, mz=7, mx=3, gr=12, ot=6, ip=3, iz=7, iy=3, ic=1, ly=3, lz=7, lc=1, lx=3, lg=7)
+PAIRS = dict(tk=12, ck=6, az=7, ay=7, my=7, mz=7, mx=3, gr=12, ot=6, ip=6, iz=14, iy=6, ic=2, ly=3, lz=7, lx=7, lg=7)
 PLANES = dict(wy=3, wz=32, vz=8, vy=24, wc=8)
 LOCAL = 8
 
@@ -313,8 +320,13 @@
     sl, sr, so = (s + NX - 1) % NX, (s + 1) % NX, (s + 2) % NX
     c0, c1 = rows_ref[0, me.dp], rows_ref[1, me.dp]
 
+    greet(me)
     offset = 48 * me.dp - 128 * ((96 * (me.dp // 2)) // 128)
     r.mm[...] = jnp.zeros_like(r.mm)
+    raw_tok = pltpu.make_async_copy(tok, r.tok_raw, r.local.at[5])
+    raw_tok.start()
+    raw_cot = pltpu.make_async_copy(cot, r.cot_raw, r.local.at[6])
+    raw_cot.start()
     locals_ = [
         pltpu.make_async_copy(
             mm_in.at[:, aligned(s * 768, 768)], r.mm.at[pl.ds(pl.multiple_of(offset, 16), 48)], r.local.at[0]
@@ -349,7 +361,8 @@
     r.a_z[z] = r.a_src[z]
     r.m_plane[...] = jnp.zeros_like(r.m_plane)
     perm = sorting(c0, c1, rows)
-    r.tok_all[s] = nn(perm, tok[...]).astype(BF16)
+    raw_tok.wait()
+    r.tok_all[s] = nn(perm, r.tok_raw[...]).astype(BF16)
 
     enter(me)
 
@@ -359,13 +372,6 @@
         for copy in copies:
             copy.wait_recv()
             sent.append(copy)
-
-    az = exchange_at(me, "dz", NZ, lambda i: r.a_src.at[(z + i) % NZ], r.a_z.at[z], r.az_s, r.az_r)
-    weights = RowGather(me, r.w_all, *r.wy, *r.wz)
-    weights.start_y()
-    others = ColumnGather(me, r.w_all, *r.vz, *r.vy)
-    others.step(1)
-    swap = CoreSwap(me, r.w_all, *r.wc)
 
     def row_chunk(i):
         return pl.ds(i * chunk, chunk)
@@ -416,7 +422,14 @@
             cot_copy(img, i, aligned(0, att), (s + NX - i) % NX).wait_recv()
 
     own_tokens(0)
-    r.cot_own[...] = nn(perm, cot[...]).astype(BF16)
+    az = exchange_at(me, "dz", NZ, lambda i: r.a_src.at[(z + i) % NZ], r.a_z.at[z], r.az_s, r.az_r)
+    weights = RowGather(me, r.w_all, *r.wy, *r.wz)
+    weights.start_y()
+    others = ColumnGather(me, r.w_all, *r.vz, *r.vy)
+    others.step(1)
+    swap = CoreSwap(me, r.w_all, *r.wc)
+    raw_cot.wait()
+    r.cot_own[...] = nn(perm, r.cot_raw[...]).astype(BF16)
     arrived(az)
     turned = r.a_z[...].astype(F32)
     for at_y in range(NY):
@@ -524,15 +537,17 @@
             r.stats[at, 0:1] = mean
             r.stats[at, 1:2] = inverse
 
+    wait_tokens(0)
+    normalize(0)
+    for shift in (0, 1, NZ - 1):
+        place(shift)
     weights.step(5)
     for shift in (3, 5, 4):
         others.wait_spread(shift)
         swap.start(shift)
-    wait_tokens(0)
-    normalize(0)
     forward(1)
     own_cotangent(1)
-    for shift in (0, 1, NZ - 1, 2, NZ - 2, 3, 5, 4):
+    for shift in (2, NZ - 2, 3, 5, 4):
         place(shift)
     for copy in locals_[1:]:
         copy.wait()
@@ -586,9 +601,12 @@
             )
         attn_out[img * part : (img + 1) * part, mine] = r.attn[s, img]
 
+    def low_grads(img):
+        at = slice(img * image_rows, (img + 1) * image_rows)
+        r.low_grad[at, :] = nt(r.proj_grad[at, :], r.up[...]).astype(BF16)
+
     def grads(img):
         at = slice(img * image_rows, (img + 1) * image_rows)
-        r.low_grad[at, :] = nt(r.proj_grad[at, :], r.up[...]).astype(BF16)
 
         @pl.loop(0, width // att)
         def _(n):
@@ -630,22 +648,59 @@
     wait_cotangent(0)
     attend(0)
     give(0)
+    low_grads(0)
     grads(0)
     reduce_first(0)
+
+    def image_x(img):
+        for j in range(24):
+            r.ip_own[img, j : j + 1, :] = r.ip[img : img + 1, j * 128 : (j + 1) * 128]
+        return [
+            remote(
+                r.ip_own.at[img], r.ip_in.at[img, i - 1], r.ip_s.at[3 * img + i - 1], r.ip_r.at[3 * img + i - 1],
+                me.at(dx=i),
+            )
+            for i in range(1, NX)
+        ]
+
+    def image_z(img):
+        total = r.ip_own[img] + r.ip_in[img, 0] + r.ip_in[img, 1] + r.ip_in[img, 2]
+        ig_all[img, c, y, z] = jnp.concatenate([total, jnp.zeros((8, 128), F32)], axis=0).astype(BF16)
+        own = ig_all.at[img, c, y, z]
+        return [
+            remote(own, own, r.iz_s.at[7 * img + i - 1], r.iz_r.at[7 * img + i - 1], me.at(dz=i))
+            for i in range(1, NZ)
+        ]
+
+    def image_y(img):
+        own = ig_all.at[img, c, y]
+        return [
+            remote(own, own, r.iy_s.at[3 * img + i - 1], r.iy_r.at[3 * img + i - 1], me.at(dy=i))
+            for i in range(1, NY)
+        ]
+
+    def image_core(img):
+        own = ig_all.at[img, c]
+        return [remote(own, own, r.ic_s.at[img], r.ic_r.at[img], me.at(flip=True))]
+
+    def go(copies):
+        for copy in copies:
+            copy.start()
+        return copies
+
+    ix = go(image_x(0))
     wait_tokens(1)
     normalize(1)
     project(1)
+    arrived(ix)
+    iz = go(image_z(0))
+    reduce_second(0)
     wait_cotangent(1)
     attend(1)
     give(1)
-    reduce_second(0)
-    grads(1)
-    reduce_first(1)
-
-    for img in range(2):
-        for j in range(24):
-            r.ip_own[img * 24 + j : img * 24 + j + 1, :] = r.ip[img : img + 1, j * 128 : (j + 1) * 128]
-    ip = exchange(me, "dx", NX, lambda i: r.ip_own, r.ip_in, r.ip_s, r.ip_r)
+    arrived(iz)
+    iy = go(image_y(0))
+    low_grads(1)
 
     r.lo[NX - 1 - s, 0] = jnp.zeros((192, 128), BF16)
     up_total = tn(r.low[...], r.proj_grad[...]).astype(BF16)
@@ -656,7 +711,11 @@
         r.lo[t // 3, 1, (t % 3) * 64 : (t % 3 + 1) * 64, :] = down_total[:, t * 128 : (t + 1) * 128]
     ly = exchange(me, "dy", NY, lambda i: r.lo.at[(y + i) % NY], r.l_y, r.ly_s, r.ly_r)
 
-    reduce_second(1)
+    grads(1)
+    reduce_first(1)
+    ix = go(image_x(1))
+    arrived(iy)
+    ic0 = go(image_core(0))
 
     arrived(ly)
     total = r.lo[y].astype(F32)
@@ -667,47 +726,45 @@
         r.l_plane[i] = jnp.concatenate([total[0, at], total[1, at]], axis=0).astype(BF16)
     lz = exchange(me, "dz", NZ, lambda i: r.l_plane.at[(z + i) % NZ], r.l_z, r.lz_s, r.lz_r)
 
-    arrived(ip)
-    ig_all[c, y, z] = (r.ip_own[...] + r.ip_in[0] + r.ip_in[1] + r.ip_in[2]).astype(BF16)
-    own_ig = ig_all.at[c, y, z]
-    iz = exchange_at(me, "dz", NZ, lambda i: own_ig, own_ig, r.iz_s, r.iz_r)
-
+    arrived(ix)
+    iz = go(image_z(1))
     arrived(lz)
     total = r.l_plane[z].astype(F32)
     for i in range(NZ - 1):
         total += r.l_z[i].astype(F32)
-    r.l_own[...] = total
-    lc = remote(r.l_own, r.l_core, r.lc_s.at[0], r.lc_r.at[0], me.at(flip=True))
-    lc.start()
-
+    r.l_piece[...] = total.astype(BF16)
+    r.l_x[c, s] = r.l_piece[...]
+    lx = [
+        remote(
+            r.l_piece, r.l_x.at[c, s], r.lx_s.at[i - 1], r.lx_r.at[i - 1], me.at(dx=i // 2, flip=i % 2 == 1)
+        )
+        for i in range(1, 2 * NX)
+    ]
+    go(lx)
     arrived(iz)
-    column = ig_all.at[c, y]
-    iy = exchange_at(me, "dy", NY, lambda i: column, column, r.iy_s, r.iy_r)
-
-    arrived([lc])
-    r.l_piece[...] = (r.l_own[...] + r.l_core[...]).astype(BF16)
-    r.l_x[s] = r.l_piece[...]
-    lx = exchange_at(me, "dx", NX, lambda i: r.l_piece, r.l_x.at[s], r.lx_s, r.lx_r)
+    iy = go(image_y(1))
+    reduce_second(1)
+
+    arrived(lx)
+    sums = [r.l_x[0, i].astype(F32) + r.l_x[1, i].astype(F32) for i in range(NX)]
+    pieces = []
+    for i in range(3):
+        k = (3 * y + i) % 4
+        pieces.append((r.l_x[0, k].astype(F32) + r.l_x[1, k].astype(F32))[0:24])
+    pieces.append((sums[0] + sums[1] + sums[2] + sums[3])[24:48])
+    f_all[z] = jnp.concatenate(pieces, axis=0).astype(BF16)
+    lg = exchange_at(me, "dz", NZ, lambda i: f_all.at[z], f_all.at[z], r.lg_s, r.lg_r)
 
     arrived(iy)
-    ic = remote(ig_all.at[c], ig_all.at[c], r.ic_s.at[0], r.ic_r.at[0], me.at(flip=True))
-    ic.start()
-
-    arrived(lx)
-    pieces = [r.l_x[(3 * y + i) % 4].astype(F32)[0:24] for i in range(3)]
-    total = r.l_x[0].astype(F32)[24:48]
-    for i in range(1, NX):
-        total += r.l_x[i].astype(F32)[24:48]
-    f_all[z] = jnp.concatenate(pieces + [total], axis=0).astype(BF16)
-    lg = exchange_at(me, "dz", NZ, lambda i: f_all.at[z], f_all.at[z], r.lg_s, r.lg_r)
-
+    ic1 = go(image_core(1))
     for img in range(2):
         for slot in range(2, 6):
             grad_copy(img, slot).wait_recv()
         grad_out[img * part : (img + 1) * part, :] = (
             r.pg[img, s].astype(F32) + r.from_l[img].astype(F32) + r.from_r[img].astype(F32)
         ).astype(BF16)
-    arrived([ic])
+    arrived(ic0)
+    arrived(ic1)
     arrived(lg)
 
     for copy in sent:
@@ -731,10 +788,10 @@
             jax.ShapeDtypeStruct((192, 1536), BF16),
             jax.ShapeDtypeStruct((8, 3072), F32),
             jax.ShapeDtypeStruct((128, 128), BF16),
-            jax.ShapeDtypeStruct((NC, NY, NZ, 48, 128), BF16),
+            jax.ShapeDtypeStruct((2, NC, NY, NZ, 32, 128), BF16),
             jax.ShapeDtypeStruct((NZ, 96, 128), BF16),
         ),
-        in_specs=[pl.BlockSpec(memory_space=pltpu.SMEM), VM, VM, VM, VM, ANY, ANY, ANY],
+        in_specs=[pl.BlockSpec(memory_space=pltpu.SMEM), ANY, ANY, VM, VM, ANY, ANY, ANY],
         out_specs=(VM, VM, VM, VM, VM, VM),
         scratch_shapes=scratch_list(),
         compiler_params=pltpu.CompilerParams(
@@ -767,11 +824,11 @@
         ).astype(BF16)
     token_grad[...] = tn(perm, sorted_grad[...]).astype(BF16)
 
-    ig_wide[...] = ig[...].reshape(3072, 128).astype(F32)
+    ig_wide[...] = ig[...].reshape(4096, 128).astype(F32)
     for j in range(24):
         total = jnp.zeros((128, 128), F32)
         for img in range(2):
-            part = ig_wide[pl.ds(img * 24 + j, 64, stride=48), :].astype(BF16)
+            part = ig_wide[pl.ds(img * 2048 + j, 64, stride=32), :].astype(BF16)
             total += tn(act[img * 64 : (img + 1) * 64], part)
         mod_grad[:, j * 128 : (j + 1) * 128] = total[0:48]
 
@@ -806,7 +863,7 @@
         ),
         in_specs=[pl.BlockSpec(memory_space=pltpu.SMEM)] + [VM] * 7,
         out_specs=(VM, VM, VM, VM, VM),
-        scratch_shapes=[pltpu.VMEM((3072, 128), F32), pltpu.VMEM((192, 1536), BF16)],
+        scratch_shapes=[pltpu.VMEM((4096, 128), F32), pltpu.VMEM((192, 1536), BF16)],
         compiler_params=pltpu.CompilerParams(vmem_limit_bytes=60 * 1024 * 1024),
         name="tail",
     )(counts, attn, grad, tok, mod, act, ig, pieces)

time: 97 us -> 100 us (1.031)
  the two profiles are of different devices: /device:TPU:16 before, /device:TPU:1 now
where the time goes in v5:
time: 100 us; the launch traced here: 98.3 us
  Pallas kernels  97.7 us (98%)
    pallas_call x1, Pallas kernels, whole(): pl.pallas_call(whole_kernel, out_shape=(jax.ShapeDtypeStruct((192, 1536),...  92.3 us
    pallas_call x1, Pallas kernels, tail(): pl.pallas_call(tail_kernel, out_shape=(jax.ShapeDtypeStruct((192, 1536),...  5.44 us

profile of v5, /device:TPU:1, one launch (start us, length us, event | category | flops | bytes accessed | tf_op | source)
XLA Modules:
  0.0 98.3 jit_solution(14557906489479655134)
XLA Ops:
  0.6 92.3 %whole.1 = (bf16[192,1536]{1,0:T(8,128)(2,1)}, bf16[192,1536]{1,0:T(8,128)(2,1)}, f32[8,3072]{1,0:T(8,128)}, bf16[128,128]{1,0:T(8,128)(2,1)}, bf16[2,2,4,8,32,1...) custom-call(s32[2,64]{1,0:T(2,128)} %bitcast.12, bf16[192,1536]{1,0:T(8,128)(2,1)} %bitcast.7, ...), custom_call_target="tpu_custom_call" | custom-call | tf_op jit(solution)/shard_map/whole/pallas_call | solution.py:784
  92.9 5.4 %tail.1 = (bf16[192,1536]{1,0:T(8,128)(2,1)}, bf16[192,1536]{1,0:T(8,128)(2,1)}, f32[24,64]{1,0:T(8,128)}, f32[64,72]{1,0:T(8,128)}, f32[48,3072]{1,0:T(8,128)}) custom-call(s32[2,64]{1,0:T(2,128)} %bitcast.13, bf16[192,1536]{1,0:T(8,128)(2,1)} %get-tuple-element.16.attn, bf16[192,1536]{1,0:T(8,128)(2,1)} %get-tuple-element.17.grad, ...), custom_call_target="tpu_custom_call" | custom-call | tf_op jit(solution)/shard_map/tail/pallas_call | solution.py:855

commit v6 on v5

--- a/solution.py
+++ b/solution.py
@@ -63,86 +63,78 @@
 HALF = 112
 
 
+class Batch:
+    def __init__(self, me, copies, sample, send, recv):
+        self.all = remote(sample, sample, send, recv, me.at(dx=1))
+        for copy in copies:
+            copy.start()
+
+    def arrived(self):
+        self.all.wait_recv()
+
+    def left(self):
+        self.all.wait_send()
+
+
 class RowGather:
     def __init__(self, me, buf, ysend, yrecv, zsend, zrecv):
         self.me, self.buf = me, buf
-        self.ysend, self.yrecv = ysend, yrecv
-        self.zsend, self.zrecv = zsend, zrecv
-        self.sent = []
-
-    def block(self, at_z, at_y):
-        return self.buf.at[self.me.c, at_z, at_y, pl.ds(0, HALF)]
-
-    def launch(self, copy):
-        copy.start()
-        self.sent.append(copy)
+        self.ysend, self.yrecv = ysend.at[0], yrecv.at[0]
+        self.zsend, self.zrecv = zsend.at[0], zrecv
 
     def start_y(self):
         me = self.me
-        own = self.block(me.z, me.y)
-        for i in range(1, NY):
-            self.launch(remote(own, own, self.ysend.at[i - 1], self.yrecv.at[i - 1], me.at(dy=i)))
-
-    def wait_y(self):
-        me = self.me
-        for i in range(1, NY):
-            block = self.block(me.z, (me.y + NY - i) % NY)
-            remote(block, block, self.ysend.at[i - 1], self.yrecv.at[i - 1], me.at(dy=i)).wait_recv()
-
-    def ring(self, way, step, part, arriving):
+        own = self.buf.at[me.c, me.z, me.y, pl.ds(0, HALF)]
+        copies = [remote(own, own, self.ysend, self.yrecv, me.at(dy=i)) for i in range(1, NY)]
+        sample = self.buf.at[me.c, me.z, pl.ds(0, 3), pl.ds(0, HALF)]
+        self.first = Batch(me, copies, sample, self.ysend, self.yrecv)
+
+    def ring(self, way, step, arriving):
         me = self.me
         far = step if arriving else step - 1
         source = (me.z + NZ - far) % NZ if way == 0 else (me.z + far) % NZ
-        block = self.block(source, part)
-        at = (way * 4 + step - 1) * NY + part
+        ys = pl.ds(0, NY) if step < 4 else pl.ds(2 * way, 2)
+        block = self.buf.at[me.c, source, ys, pl.ds(0, HALF)]
         there = me.at(dz=1) if way == 0 else me.at(dz=NZ - 1)
-        return remote(block, block, self.zsend.at[at], self.zrecv.at[at], there)
-
-    def carried(self, way, step, part):
-        return step < 4 or (part // 2) == way
+        return remote(block, block, self.zsend, self.zrecv.at[way * 4 + step - 1], there)
 
     def step(self, step):
-        for turn in range(NY):
-            for way in (0, 1):
-                part = turn if way == 0 else NY - 1 - turn
-                if step > 1 and self.carried(way, step - 1, part):
-                    self.ring(way, step - 1, part, True).wait_recv()
-                if step <= 4 and self.carried(way, step, part):
-                    self.launch(self.ring(way, step, part, False))
+        for way in (0, 1):
+            if step > 1:
+                self.ring(way, step - 1, True).wait_recv()
+            if step <= 4:
+                self.ring(way, step, False).start()
+
+    def left(self):
+        me = self.me
+        self.first.left()
+        sample = self.buf.at[me.c, pl.ds(0, 7), pl.ds(0, NY), pl.ds(0, HALF)]
+        remote(sample, sample, self.zsend, self.zrecv.at[0], me.at(dz=1)).wait_send()
 
 
 class ColumnGather:
     def __init__(self, me, buf, zsend, zrecv, ysend, yrecv):
         self.me, self.buf = me, buf
-        self.ysend, self.yrecv = ysend, yrecv
-        self.zsend, self.zrecv = zsend, zrecv
-        self.sent = []
-
-    def block(self, shift, at_y):
-        return self.buf.at[self.me.c, (self.me.z + shift) % NZ, at_y, pl.ds(HALF, HALF)]
-
-    def launch(self, copy):
-        copy.start()
-        self.sent.append(copy)
+        self.ysend, self.yrecv = ysend.at[0], yrecv
+        self.zsend, self.zrecv = zsend.at[0], zrecv
+
+    def block(self, shift, ys):
+        return self.buf.at[self.me.c, (self.me.z + shift) % NZ, ys, pl.ds(HALF, HALF)]
 
     def ring(self, way, step, arriving):
         far = step if arriving else step - 1
         block = self.block((NZ - far) % NZ if way == 0 else far, self.me.y)
-        at = way * 4 + step - 1
         there = self.me.at(dz=1) if way == 0 else self.me.at(dz=NZ - 1)
-        return remote(block, block, self.zsend.at[at], self.zrecv.at[at], there)
+        return remote(block, block, self.zsend, self.zrecv.at[way * 4 + step - 1], there)
 
     def spread(self, shift):
         block = self.block(shift, self.me.y)
         for i in range(1, NY):
-            at = shift * (NY - 1) + i - 1
-            self.launch(remote(block, block, self.ysend.at[at], self.yrecv.at[at], self.me.at(dy=i)))
+            remote(block, block, self.ysend, self.yrecv.at[shift], self.me.at(dy=i)).start()
 
     def wait_spread(self, shift):
-        for i in range(1, NY):
-            block = self.block(shift, (self.me.y + NY - i) % NY)
-            at = shift * (NY - 1) + i - 1
-            remote(block, block, self.ysend.at[at], self.yrecv.at[at], self.me.at(dy=i)).wait_recv()
+        sample = self.block(shift, pl.ds(0, 3))
+        remote(sample, sample, self.ysend, self.yrecv.at[shift], self.me.at(dy=1)).wait_recv()
 
     def step(self, step):
         for way in (0, 1):
@@ -150,7 +142,7 @@
             if 1 < step <= last + 1:
                 self.ring(way, step - 1, True).wait_recv()
             if step <= last:
-                self.launch(self.ring(way, step, False))
+                self.ring(way, step, False).start()
         if step == 1:
             self.spread(0)
         else:
@@ -158,42 +150,38 @@
             if step < 5:
                 self.spread(step - 1)
 
+    def left(self):
+        me = self.me
+        sample = self.buf.at[me.c, pl.ds(0, 7), 0, pl.ds(HALF, HALF)]
+        remote(sample, sample, self.zsend, self.zrecv.at[0], me.at(dz=1)).wait_send()
+        sample = self.buf.at[me.c, pl.ds(0, NZ), pl.ds(0, 3), pl.ds(HALF, HALF)]
+        remote(sample, sample, self.ysend, self.yrecv.at[0], me.at(dy=1)).wait_send()
+
 
 class CoreSwap:
     def __init__(self, me, buf, send, recv):
-        self.me, self.buf, self.send, self.recv = me, buf, send, recv
-        self.sent = []
+        self.me, self.buf, self.send, self.recv = me, buf, send.at[0], recv
 
     def copy(self, at_c, shift):
         block = self.buf.at[at_c, (self.me.z + shift) % NZ]
-        return remote(block, block, self.send.at[shift], self.recv.at[shift], self.me.at(flip=True))
+        return remote(block, block, self.send, self.recv.at[shift], self.me.at(flip=True))
 
     def start(self, shift):
-        copy = self.copy(self.me.c, shift)
-        copy.start()
-        self.sent.append(copy)
+        self.copy(self.me.c, shift).start()
 
     def wait(self, shift):
         self.copy(1 - self.me.c, shift).wait_recv()
 
-
-def exchange(me, axis, count, source, slots, send, recv):
-    copies = []
-    for i in range(1, count):
-        copy = remote(source(i), slots.at[i - 1], send.at[i - 1], recv.at[i - 1], me.at(**{axis: i}))
-        copy.start()
-        copies.append(copy)
-    return copies
-
-
-def exchange_at(me, axis, count, source, target, send, recv):
-    copies = []
-    for i in range(1, count):
-        copy = remote(source(i), target, send.at[i - 1], recv.at[i - 1], me.at(**{axis: i}))
-        copy.start()
-        copies.append(copy)
-    return copies
-
+    def left(self):
+        block = self.buf.at[self.me.c]
+        remote(block, block, self.send, self.recv.at[0], self.me.at(flip=True)).wait_send()
+
+
+def exchange(me, axis, count, source, target, sample, send, recv):
+    copies = [
+        remote(source(i), target(i), send.at[0], recv.at[0], me.at(**{axis: i})) for i in range(1, count)
+    ]
+    return Batch(me, copies, sample, send.at[0], recv.at[0])
 
 def nt(a, b):
     return lax.dot_general(a, b, (((1,), (1,)), ((), ())), preferred_element_type=F32)
@@ -239,7 +227,7 @@
     a_z=pltpu.VMEM((NZ, 16, 128), BF16),
     a_turn=pltpu.VMEM((NY, 32, 128), F32),
     a_low=pltpu.VMEM((NY, 32, 128), BF16),
-    a_y=pltpu.VMEM((NC, NY, 32, 128), BF16),
+    a_y=pltpu.VMEM((NC * NY, 32, 128), BF16),
     a_wide=pltpu.VMEM((256, 128), F32),
     a_pair=pltpu.VMEM((128, 256), BF16),
     part_wide=pltpu.VMEM((768, 128), F32),
@@ -265,27 +253,28 @@
     comb_r=pltpu.VMEM((2, 48, 1536), BF16),
     from_l=pltpu.VMEM((2, 96, 1536), BF16),
     from_r=pltpu.VMEM((2, 96, 1536), BF16),
-    ip_own=pltpu.VMEM((2, 24, 128), F32),
-    ip_in=pltpu.VMEM((2, 3, 24, 128), F32),
+    ip_own=pltpu.VMEM((48, 128), F32),
+    ip_in=pltpu.VMEM((3, 48, 128), F32),
     lo=pltpu.VMEM((NY, 2, 192, 128), BF16),
     l_y=pltpu.VMEM((NY - 1, 2, 192, 128), BF16),
     l_plane=pltpu.VMEM((NZ, 48, 128), BF16),
     l_z=pltpu.VMEM((NZ - 1, 48, 128), BF16),
     l_piece=pltpu.VMEM((48, 128), BF16),
-    l_x=pltpu.VMEM((NC, NX, 48, 128), BF16),
+    l_x=pltpu.VMEM((NC * NX, 48, 128), BF16),
 )
-PAIRS = dict(tk=12, ck=6, az=7, ay=7, my=7, mz=7, mx=3, gr=12, ot=6, ip=6, iz=14, iy=6, ic=2, ly=3, lz=7, lx=7, lg=7)
-PLANES = dict(wy=3, wz=32, vz=8, vy=24, wc=8)
+PAIRS = dict(
+    tk=(1, 12), ck=(2, 2), az=(1, 1), ay=(1, 1), my=(1, 1), mz=(1, 1), mx=(1, 1), gr=(2, 12), ot=(2, 2),
+    ip=(1, 1), iz=(1, 1), iy=(1, 1), ic=(1, 1), ly=(1, 1), lz=(1, 1), lx=(1, 1), lg=(1, 1),
+)
+PLANES = dict(wy=(1, 1), wz=(1, 8), vz=(1, 8), vy=(1, 8), wc=(1, 8))
 LOCAL = 8
 
 
 def scratch_list():
     dma = pltpu.SemaphoreType.DMA
     out = list(SCRATCH.values())
-    for count in PAIRS.values():
-        out += [dma((count,)), dma((count,))]
-    for count in PLANES.values():
-        out += [dma((count,)), dma((count,))]
+    for send, recv in list(PAIRS.values()) + list(PLANES.values()):
+        out += [dma((send,)), dma((recv,))]
     return out + [dma((LOCAL,))]
 
 
@@ -366,37 +355,32 @@
 
     enter(me)
 
-    sent = []
-
-    def arrived(copies):
-        for copy in copies:
-            copy.wait_recv()
-            sent.append(copy)
+    batches = []
+
+    def send(batch):
+        batches.append(batch)
+        return batch
 
     def row_chunk(i):
         return pl.ds(i * chunk, chunk)
 
     def token_copy(source, owner, i, slot, there):
-        return remote(source, r.tok_all.at[owner, row_chunk(i)], r.tk_s.at[slot], r.tk_r.at[slot], there)
-
-    def launch(copy):
-        copy.start()
-        sent.append(copy)
+        return remote(source, r.tok_all.at[owner, row_chunk(i)], r.tk_s.at[0], r.tk_r.at[slot], there)
 
     def own_tokens(img):
         i = 2 * img
-        launch(token_copy(r.tok_all.at[s, row_chunk(i)], s, i, i, right))
-        launch(token_copy(r.tok_all.at[s, row_chunk(i + 1)], s, i + 1, 4 + i + 1, left))
-        launch(token_copy(r.tok_all.at[s, row_chunk(i + 1)], s, i + 1, i + 1, right))
-        launch(token_copy(r.tok_all.at[s, row_chunk(i)], s, i, 4 + i, left))
+        token_copy(r.tok_all.at[s, row_chunk(i)], s, i, i, right).start()
+        token_copy(r.tok_all.at[s, row_chunk(i + 1)], s, i + 1, 4 + i + 1, left).start()
+        token_copy(r.tok_all.at[s, row_chunk(i + 1)], s, i + 1, i + 1, right).start()
+        token_copy(r.tok_all.at[s, row_chunk(i)], s, i, 4 + i, left).start()
 
     def forward(img):
         i = 2 * img
         token_copy(r.tok_all.at[s, row_chunk(i)], sl, i, i, right).wait_recv()
-        launch(token_copy(r.tok_all.at[sl, row_chunk(i)], sl, i, 8 + i, right))
+        token_copy(r.tok_all.at[sl, row_chunk(i)], sl, i, 8 + i, right).start()
         i = i + 1
         token_copy(r.tok_all.at[s, row_chunk(i)], sr, i, 4 + i, left).wait_recv()
-        launch(token_copy(r.tok_all.at[sr, row_chunk(i)], sr, i, 8 + i, left))
+        token_copy(r.tok_all.at[sr, row_chunk(i)], sr, i, 8 + i, left).start()
 
     def wait_tokens(img):
         i = 2 * img
@@ -406,56 +390,57 @@
         token_copy(own, so, i, 8 + i, right).wait_recv()
         token_copy(own, so, i + 1, 8 + i + 1, left).wait_recv()
 
-    def cot_copy(img, i, columns, source):
+    def own_cotangent(img):
         at = pl.ds(img * part, part)
-        return remote(
-            r.cot_own.at[at, columns], r.cot_all.at[source, at],
-            r.ck_s.at[3 * img + i - 1], r.ck_r.at[3 * img + i - 1], me.at(dx=i),
+        copies = [
+            remote(
+                r.cot_own.at[at, aligned(((s + i) % NX) * att, att)], r.cot_all.at[s, at],
+                r.ck_s.at[img], r.ck_r.at[img], me.at(dx=i),
+            )
+            for i in range(1, NX)
+        ]
+        return send(Batch(me, copies, r.cot_all.at[pl.ds(0, 3), at], r.ck_s.at[img], r.ck_r.at[img]))
+
+    az = send(
+        exchange(
+            me, "dz", NZ, lambda i: r.a_src.at[(z + i) % NZ], lambda i: r.a_z.at[z], r.a_z.at[pl.ds(0, 7)],
+            r.az_s, r.az_r,
         )
-
-    def own_cotangent(img):
-        for i in range(1, NX):
-            launch(cot_copy(img, i, aligned(((s + i) % NX) * att, att), s))
-
-    def wait_cotangent(img):
-        for i in range(1, NX):
-            cot_copy(img, i, aligned(0, att), (s + NX - i) % NX).wait_recv()
-
-    own_tokens(0)
-    az = exchange_at(me, "dz", NZ, lambda i: r.a_src.at[(z + i) % NZ], r.a_z.at[z], r.az_s, r.az_r)
+    )
     weights = RowGather(me, r.w_all, *r.wy, *r.wz)
     weights.start_y()
     others = ColumnGather(me, r.w_all, *r.vz, *r.vy)
     others.step(1)
     swap = CoreSwap(me, r.w_all, *r.wc)
+    own_tokens(0)
     raw_cot.wait()
     r.cot_own[...] = nn(perm, r.cot_raw[...]).astype(BF16)
-    arrived(az)
+    az.arrived()
     turned = r.a_z[...].astype(F32)
     for at_y in range(NY):
         for at_z in range(NZ):
             r.a_turn[at_y, 4 * at_z : 4 * at_z + 4, :] = turned[at_z, 4 * at_y : 4 * at_y + 4]
     r.a_low[...] = r.a_turn[...].astype(BF16)
-    r.a_y[c, y] = r.a_low[y]
-
-    def plane_exchange(source, target, send, recv):
+    r.a_y[NY * c + y] = r.a_low[y]
+
+    def plane_exchange(source, target, sample, send_sem, recv_sem):
         copies = []
         for i in range(1, 2 * NY):
             dy, flip = i // 2, i % 2 == 1
             there = (y + dy) % NY
             at = (1 - c) if flip else c
-            copy = remote(
-                source(at, there), target(i - 1), send.at[i - 1], recv.at[i - 1], me.at(dy=dy, flip=flip)
+            copies.append(
+                remote(source(at, there), target(i - 1), send_sem.at[0], recv_sem.at[0], me.at(dy=dy, flip=flip))
             )
-            copy.start()
-            copies.append(copy)
-        return copies
-
-    ay = plane_exchange(lambda at, there: r.a_low.at[there], lambda i: r.a_y.at[c, y], r.ay_s, r.ay_r)
-    weights.wait_y()
+        return send(Batch(me, copies, sample, send_sem.at[0], recv_sem.at[0]))
+
+    ay = plane_exchange(
+        lambda at, there: r.a_low.at[there], lambda i: r.a_y.at[NY * c + y], r.a_y.at[pl.ds(0, 7)], r.ay_s, r.ay_r
+    )
+    weights.first.arrived()
     weights.step(1)
     others.step(2)
-    arrived(ay)
+    ay.arrived()
     locals_[0].wait()
     r.a_wide[...] = r.a_y[...].reshape(256, 128).astype(F32)
     for img in range(2):
@@ -468,9 +453,11 @@
         for img in range(2):
             r.part_wide[pl.ds(img * 6 + j, 64, stride=12), :] = columns[img * 64 : (img + 1) * 64]
     r.part_low[...] = r.part_wide[...].astype(BF16).reshape(r.part_low.shape)
-    my = plane_exchange(lambda at, there: r.part_low.at[at, there], lambda i: r.m_in.at[i], r.my_s, r.my_r)
+    my = plane_exchange(
+        lambda at, there: r.part_low.at[at, there], lambda i: r.m_in.at[i], r.m_in, r.my_s, r.my_r
+    )
     forward(0)
-    own_cotangent(0)
+    cot0 = own_cotangent(0)
     own_tokens(1)
     others.step(3)
     row = lax.broadcasted_iota(jnp.int32, (256, 128), 0)
@@ -479,28 +466,17 @@
     a_own[...] = nn(r.a_pair[...], pick).astype(BF16)
     weights.step(2)
     r.cot_all[s] = r.cot_own[:, aligned(s * att, att)]
-    arrived(my)
+    my.arrived()
     total = r.part_low[c, y].astype(F32)
     for i in range(7):
         total += r.m_in[i].astype(F32)
     for at_z in range(NZ):
         r.m_plane[at_z, 0:12, :] = total[12 * at_z : 12 * at_z + 12]
-    mz = exchange(me, "dz", NZ, lambda i: r.m_plane.at[(z + i) % NZ], r.m_z, r.mz_s, r.mz_r)
-    others.step(4)
-    weights.step(3)
-    arrived(mz)
-    total = r.m_plane[z]
-    for i in range(NZ - 1):
-        total += r.m_z[i]
-    r.m_own[...] = total
-    r.m_all[s] = total
-    mx = exchange_at(me, "dx", NX, lambda i: r.m_own, r.m_all.at[s], r.mx_s, r.mx_r)
-    others.step(5)
-    weights.step(4)
-    for shift in (0, 1, NZ - 1, 2, NZ - 2):
-        others.wait_spread(shift)
-        swap.start(shift)
-
+    mz = send(
+        exchange(
+            me, "dz", NZ, lambda i: r.m_plane.at[(z + i) % NZ], lambda i: r.m_z.at[i - 1], r.m_z, r.mz_s, r.mz_r
+        )
+    )
     def place(shift):
         swap.wait(shift)
         at_z = (z + shift) % NZ
@@ -514,7 +490,31 @@
                 both = jnp.concatenate([first[24 * t : 24 * t + 24], other[24 * t : 24 * t + 24]], axis=0)
                 r.w[at, t * 128 : (t + 1) * 128] = both.astype(BF16)
 
-    arrived(mx)
+    others.step(4)
+    weights.step(3)
+    for shift in (0, 1, NZ - 1):
+        others.wait_spread(shift)
+        swap.start(shift)
+    mz.arrived()
+    total = r.m_plane[z]
+    for i in range(NZ - 1):
+        total += r.m_z[i]
+    r.m_own[...] = total
+    r.m_all[s] = total
+    mx = send(
+        exchange(
+            me, "dx", NX, lambda i: r.m_own, lambda i: r.m_all.at[s], r.m_all.at[pl.ds(0, 3)], r.mx_s, r.mx_r
+        )
+    )
+    others.step(5)
+    weights.step(4)
+    for shift in (2, NZ - 2):
+        others.wait_spread(shift)
+        swap.start(shift)
+    for shift in (0, 1, NZ - 1):
+        place(shift)
+
+    mx.arrived()
     mod[...] = jnp.zeros_like(mod)
     for k in range(NX):
         for img in range(2):
@@ -537,16 +537,14 @@
             r.stats[at, 0:1] = mean
             r.stats[at, 1:2] = inverse
 
-    wait_tokens(0)
-    normalize(0)
-    for shift in (0, 1, NZ - 1):
-        place(shift)
     weights.step(5)
     for shift in (3, 5, 4):
         others.wait_spread(shift)
         swap.start(shift)
+    wait_tokens(0)
+    normalize(0)
     forward(1)
-    own_cotangent(1)
+    cot1 = own_cotangent(1)
     for shift in (2, NZ - 2, 3, 5, 4):
         place(shift)
     for copy in locals_[1:]:
@@ -590,16 +588,15 @@
     mine = aligned(s * att, att)
 
     def give(img):
-        for i in range(1, NX):
-            there = me.at(dx=i)
-            launch(
-                remote(
-                    r.attn.at[there[1], img],
-                    attn_out.at[img * part : (img + 1) * part, mine],
-                    r.ot_s.at[3 * img + i - 1], r.ot_r.at[3 * img + i - 1], there,
-                )
+        at = slice(img * part, (img + 1) * part)
+        copies = [
+            remote(
+                r.attn.at[(s + i) % NX, img], attn_out.at[at, mine], r.ot_s.at[img], r.ot_r.at[img], me.at(dx=i)
             )
-        attn_out[img * part : (img + 1) * part, mine] = r.attn[s, img]
+            for i in range(1, NX)
+        ]
+        attn_out[at, mine] = r.attn[s, img]
+        return send(Batch(me, copies, attn_out.at[at, pl.ds(0, 3 * att)], r.ot_s.at[img], r.ot_r.at[img]))
 
     def low_grads(img):
         at = slice(img * image_rows, (img + 1) * image_rows)
@@ -630,76 +627,34 @@
             (r.comb_r.at[img], r.from_l.at[img, first], right),
             (r.comb_l.at[img], r.from_r.at[img, second], left),
         )[slot]
-        return remote(src, dst, r.gr_s.at[6 * img + slot], r.gr_r.at[6 * img + slot], there)
+        return remote(src, dst, r.gr_s.at[img], r.gr_r.at[6 * img + slot], there)
 
     def reduce_first(img):
         for slot in range(4):
-            launch(grad_copy(img, slot))
+            grad_copy(img, slot).start()
 
     def reduce_second(img):
         grad_copy(img, 0).wait_recv()
         r.comb_r[img] = (r.pg[img, sr, 0:half].astype(F32) + r.half_l[img].astype(F32)).astype(BF16)
-        launch(grad_copy(img, 4))
+        grad_copy(img, 4).start()
         grad_copy(img, 1).wait_recv()
         r.comb_l[img] = (r.pg[img, sl, half:part].astype(F32) + r.half_r[img].astype(F32)).astype(BF16)
-        launch(grad_copy(img, 5))
+        grad_copy(img, 5).start()
 
     project(0)
-    wait_cotangent(0)
+    cot0.arrived()
     attend(0)
-    give(0)
+    out0 = give(0)
     low_grads(0)
     grads(0)
     reduce_first(0)
-
-    def image_x(img):
-        for j in range(24):
-            r.ip_own[img, j : j + 1, :] = r.ip[img : img + 1, j * 128 : (j + 1) * 128]
-        return [
-            remote(
-                r.ip_own.at[img], r.ip_in.at[img, i - 1], r.ip_s.at[3 * img + i - 1], r.ip_r.at[3 * img + i - 1],
-                me.at(dx=i),
-            )
-            for i in range(1, NX)
-        ]
-
-    def image_z(img):
-        total = r.ip_own[img] + r.ip_in[img, 0] + r.ip_in[img, 1] + r.ip_in[img, 2]
-        ig_all[img, c, y, z] = jnp.concatenate([total, jnp.zeros((8, 128), F32)], axis=0).astype(BF16)
-        own = ig_all.at[img, c, y, z]
-        return [
-            remote(own, own, r.iz_s.at[7 * img + i - 1], r.iz_r.at[7 * img + i - 1], me.at(dz=i))
-            for i in range(1, NZ)
-        ]
-
-    def image_y(img):
-        own = ig_all.at[img, c, y]
-        return [
-            remote(own, own, r.iy_s.at[3 * img + i - 1], r.iy_r.at[3 * img + i - 1], me.at(dy=i))
-            for i in range(1, NY)
-        ]
-
-    def image_core(img):
-        own = ig_all.at[img, c]
-        return [remote(own, own, r.ic_s.at[img], r.ic_r.at[img], me.at(flip=True))]
-
-    def go(copies):
-        for copy in copies:
-            copy.start()
-        return copies
-
-    ix = go(image_x(0))
     wait_tokens(1)
     normalize(1)
     project(1)
-    arrived(ix)
-    iz = go(image_z(0))
+    cot1.arrived()
+    attend(1)
+    out1 = give(1)
     reduce_second(0)
-    wait_cotangent(1)
-    attend(1)
-    give(1)
-    arrived(iz)
-    iy = go(image_y(0))
     low_grads(1)
 
     r.lo[NX - 1 - s, 0] = jnp.zeros((192, 128), BF16)
@@ -709,75 +664,102 @@
     down_total = tn(r.low_grad[...], r.modded[...]).astype(BF16)
     for t in range(12):
         r.lo[t // 3, 1, (t % 3) * 64 : (t % 3 + 1) * 64, :] = down_total[:, t * 128 : (t + 1) * 128]
-    ly = exchange(me, "dy", NY, lambda i: r.lo.at[(y + i) % NY], r.l_y, r.ly_s, r.ly_r)
+    ly = send(
+        exchange(me, "dy", NY, lambda i: r.lo.at[(y + i) % NY], lambda i: r.l_y.at[i - 1], r.l_y, r.ly_s, r.ly_r)
+    )
 
     grads(1)
     reduce_first(1)
-    ix = go(image_x(1))
-    arrived(iy)
-    ic0 = go(image_core(0))
-
-    arrived(ly)
+    for img in range(2):
+        for j in range(24):
+            at = img * 24 + j
+            r.ip_own[at : at + 1, :] = r.ip[img : img + 1, j * 128 : (j + 1) * 128]
+    ip = send(exchange(me, "dx", NX, lambda i: r.ip_own, lambda i: r.ip_in.at[i - 1], r.ip_in, r.ip_s, r.ip_r))
+
+    ly.arrived()
     total = r.lo[y].astype(F32)
     for i in range(NY - 1):
         total += r.l_y[i].astype(F32)
     for i in range(NZ):
         at = slice(24 * i, 24 * i + 24)
         r.l_plane[i] = jnp.concatenate([total[0, at], total[1, at]], axis=0).astype(BF16)
-    lz = exchange(me, "dz", NZ, lambda i: r.l_plane.at[(z + i) % NZ], r.l_z, r.lz_s, r.lz_r)
-
-    arrived(ix)
-    iz = go(image_z(1))
-    arrived(lz)
+    lz = send(
+        exchange(
+            me, "dz", NZ, lambda i: r.l_plane.at[(z + i) % NZ], lambda i: r.l_z.at[i - 1], r.l_z, r.lz_s, r.lz_r
+        )
+    )
+
+    ip.arrived()
+    ig_all[c, y, z] = (r.ip_own[...] + r.ip_in[0] + r.ip_in[1] + r.ip_in[2]).astype(BF16)
+    own_ig = ig_all.at[c, y, z]
+    iz = send(
+        exchange(me, "dz", NZ, lambda i: own_ig, lambda i: own_ig, ig_all.at[c, y, pl.ds(0, 7)], r.iz_s, r.iz_r)
+    )
+
+    lz.arrived()
     total = r.l_plane[z].astype(F32)
     for i in range(NZ - 1):
         total += r.l_z[i].astype(F32)
     r.l_piece[...] = total.astype(BF16)
-    r.l_x[c, s] = r.l_piece[...]
-    lx = [
+    r.l_x[NX * c + s] = r.l_piece[...]
+    copies = [
         remote(
-            r.l_piece, r.l_x.at[c, s], r.lx_s.at[i - 1], r.lx_r.at[i - 1], me.at(dx=i // 2, flip=i % 2 == 1)
+            r.l_piece, r.l_x.at[NX * c + s], r.lx_s.at[0], r.lx_r.at[0], me.at(dx=i // 2, flip=i % 2 == 1)
         )
         for i in range(1, 2 * NX)
     ]
-    go(lx)
-    arrived(iz)
-    iy = go(image_y(1))
+    lx = send(Batch(me, copies, r.l_x.at[pl.ds(0, 7)], r.lx_s.at[0], r.lx_r.at[0]))
+
+    iz.arrived()
+    column = ig_all.at[c, y]
+    iy = send(
+        exchange(me, "dy", NY, lambda i: column, lambda i: column, ig_all.at[c, pl.ds(0, 3)], r.iy_s, r.iy_r)
+    )
     reduce_second(1)
 
-    arrived(lx)
-    sums = [r.l_x[0, i].astype(F32) + r.l_x[1, i].astype(F32) for i in range(NX)]
+    lx.arrived()
+    sums = [r.l_x[i].astype(F32) + r.l_x[NX + i].astype(F32) for i in range(NX)]
     pieces = []
     for i in range(3):
         k = (3 * y + i) % 4
-        pieces.append((r.l_x[0, k].astype(F32) + r.l_x[1, k].astype(F32))[0:24])
+        pieces.append((r.l_x[k].astype(F32) + r.l_x[NX + k].astype(F32))[0:24])
     pieces.append((sums[0] + sums[1] + sums[2] + sums[3])[24:48])
     f_all[z] = jnp.concatenate(pieces, axis=0).astype(BF16)
-    lg = exchange_at(me, "dz", NZ, lambda i: f_all.at[z], f_all.at[z], r.lg_s, r.lg_r)
-
-    arrived(iy)
-    ic1 = go(image_core(1))
+    lg = send(
+        exchange(
+            me, "dz", NZ, lambda i: f_all.at[z], lambda i: f_all.at[z], f_all.at[pl.ds(0, 7)], r.lg_s, r.lg_r
+        )
+    )
+
+    iy.arrived()
+    whole_core = ig_all.at[c]
+    ic = send(
+        Batch(
+            me, [remote(whole_core, whole_core, r.ic_s.at[0], r.ic_r.at[0], me.at(flip=True))], whole_core,
+            r.ic_s.at[0], r.ic_r.at[0],
+        )
+    )
     for img in range(2):
         for slot in range(2, 6):
             grad_copy(img, slot).wait_recv()
         grad_out[img * part : (img + 1) * part, :] = (
             r.pg[img, s].astype(F32) + r.from_l[img].astype(F32) + r.from_r[img].astype(F32)
         ).astype(BF16)
-    arrived(ic0)
-    arrived(ic1)
-    arrived(lg)
-
-    for copy in sent:
-        copy.wait_send()
+    ic.arrived()
+    lg.arrived()
+    out0.arrived()
+    out1.arrived()
+
+    for batch in batches:
+        batch.left()
+    tokens_sent = r.tok_all.at[pl.ds(0, 3)]
+    remote(tokens_sent, tokens_sent, r.tk_s.at[0], r.tk_r.at[0], right).wait_send()
     for img in range(2):
-        for i in range(1, NX):
-            remote(
-                r.attn.at[0, img],
-                attn_out.at[img * part : (img + 1) * part, aligned(((s + NX - i) % NX) * att, att)],
-                r.ot_s.at[3 * img + i - 1], r.ot_r.at[3 * img + i - 1], right,
-            ).wait_recv()
-    for copy in weights.sent + others.sent + swap.sent:
-        copy.wait_send()
+        grads_sent = r.pg.at[img, pl.ds(0, 3)]
+        remote(grads_sent, grads_sent, r.gr_s.at[img], r.gr_r.at[0], right).wait_send()
+    weights.left()
+    others.left()
+    swap.left()
 
 
 def whole(counts, tok, cot, cond, wq, up, down, mm):
@@ -788,7 +770,7 @@
             jax.ShapeDtypeStruct((192, 1536), BF16),
             jax.ShapeDtypeStruct((8, 3072), F32),
             jax.ShapeDtypeStruct((128, 128), BF16),
-            jax.ShapeDtypeStruct((2, NC, NY, NZ, 32, 128), BF16),
+            jax.ShapeDtypeStruct((NC, NY, NZ, 48, 128), BF16),
             jax.ShapeDtypeStruct((NZ, 96, 128), BF16),
         ),
         in_specs=[pl.BlockSpec(memory_space=pltpu.SMEM), ANY, ANY, VM, VM, ANY, ANY, ANY],
@@ -824,11 +806,11 @@
         ).astype(BF16)
     token_grad[...] = tn(perm, sorted_grad[...]).astype(BF16)
 
-    ig_wide[...] = ig[...].reshape(4096, 128).astype(F32)
+    ig_wide[...] = ig[...].reshape(3072, 128).astype(F32)
     for j in range(24):
         total = jnp.zeros((128, 128), F32)
         for img in range(2):
-            part = ig_wide[pl.ds(img * 2048 + j, 64, stride=32), :].astype(BF16)
+            part = ig_wide[pl.ds(img * 24 + j, 64, stride=48), :].astype(BF16)
             total += tn(act[img * 64 : (img + 1) * 64], part)
         mod_grad[:, j * 128 : (j + 1) * 128] = total[0:48]
 
@@ -863,7 +845,7 @@
         ),
         in_specs=[pl.BlockSpec(memory_space=pltpu.SMEM)] + [VM] * 7,
         out_specs=(VM, VM, VM, VM, VM),
-        scratch_shapes=[pltpu.VMEM((4096, 128), F32), pltpu.VMEM((192, 1536), BF16)],
+        scratch_shapes=[pltpu.VMEM((3072, 128), F32), pltpu.VMEM((192, 1536), BF16)],
         compiler_params=pltpu.CompilerParams(vmem_limit_bytes=60 * 1024 * 1024),
         name="tail",
     )(counts, attn, grad, tok, mod, act, ig, pieces)

time: 100 us -> 91.4 us (0.914); the launches traced: 98.3 us -> 91.3 us
  Pallas kernels: 97.7 us -> 90.6 us
    pallas_call x1, Pallas kernels: 92.3 us -> 85.9 us  [whole(): pl.pallas_call(whole_kernel, out_shape=(jax.ShapeDtypeStruct((192, 1536),...]
where the time goes in v6:
time: 91.4 us; the launch traced here: 91.3 us
  Pallas kernels  90.6 us (99%)
    pallas_call x1, Pallas kernels, whole(): pl.pallas_call(whole_kernel, out_shape=(jax.ShapeDtypeStruct((192, 1536),...  85.9 us
    pallas_call x1, Pallas kernels, tail(): pl.pallas_call(tail_kernel, out_shape=(jax.ShapeDtypeStruct((192, 1536),...  4.75 us

profile of v6, /device:TPU:1, one launch (start us, length us, event | category | flops | bytes accessed | tf_op | source)
XLA Modules:
  0.0 91.3 jit_solution(3326420148510458589)
XLA Ops:
  0.6 85.9 %whole.1 = (bf16[192,1536]{1,0:T(8,128)(2,1)}, bf16[192,1536]{1,0:T(8,128)(2,1)}, f32[8,3072]{1,0:T(8,128)}, bf16[128,128]{1,0:T(8,128)(2,1)}, bf16[2,4,8,48,128...) custom-call(s32[2,64]{1,0:T(2,128)} %bitcast.12, bf16[192,1536]{1,0:T(8,128)(2,1)} %bitcast.7, bf16[192,1536]{1,0:T(8,128)(2,1)} %bitcast.9, ...), custom_call_target="tpu_custom_call" | custom-call | tf_op jit(solution)/shard_map/whole/pallas_call | solution.py:766
  86.5 4.7 %tail.1 = (bf16[192,1536]{1,0:T(8,128)(2,1)}, bf16[192,1536]{1,0:T(8,128)(2,1)}, f32[24,64]{1,0:T(8,128)}, f32[64,72]{1,0:T(8,128)}, f32[48,3072]{1,0:T(8,128)}) custom-call(s32[2,64]{1,0:T(2,128)} %bitcast.13, bf16[192,1536]{1,0:T(8,128)(2,1)} %get-tuple-element.16.attn, bf16[192,1536]{1,0:T(8,128)(2,1)} %get-tuple-element.17.grad, ...), custom_call_target="tpu_custom_call" | custom-call | tf_op jit(solution)/shard_map/tail/pallas_call | solution.py:837

commit v7 on v6

--- a/solution.py
+++ b/solution.py
@@ -60,7 +60,7 @@
     pl.semaphore_wait(pltpu.get_barrier_semaphore(), len(peers_of(me)))
 
 
-HALF = 112
+SPLIT = 128
 
 
 class Batch:
@@ -84,97 +84,54 @@
 
     def start_y(self):
         me = self.me
-        own = self.buf.at[me.c, me.z, me.y, pl.ds(0, HALF)]
+        own = self.buf.at[me.c, 3, me.y, pl.ds(0, SPLIT)]
         copies = [remote(own, own, self.ysend, self.yrecv, me.at(dy=i)) for i in range(1, NY)]
-        sample = self.buf.at[me.c, me.z, pl.ds(0, 3), pl.ds(0, HALF)]
+        sample = self.buf.at[me.c, 3, pl.ds(0, 3), pl.ds(0, SPLIT)]
         self.first = Batch(me, copies, sample, self.ysend, self.yrecv)
 
-    def ring(self, way, step, arriving):
+    def ring(self, way, step):
         me = self.me
-        far = step if arriving else step - 1
-        source = (me.z + NZ - far) % NZ if way == 0 else (me.z + far) % NZ
+        here, there = (4 - step, 3 - step) if way == 0 else (2 + step, 3 + step)
         ys = pl.ds(0, NY) if step < 4 else pl.ds(2 * way, 2)
-        block = self.buf.at[me.c, source, ys, pl.ds(0, HALF)]
-        there = me.at(dz=1) if way == 0 else me.at(dz=NZ - 1)
-        return remote(block, block, self.zsend, self.zrecv.at[way * 4 + step - 1], there)
+        source = self.buf.at[me.c, here, ys, pl.ds(0, SPLIT)]
+        target = self.buf.at[me.c, there % NZ, ys, pl.ds(0, SPLIT)]
+        device = me.at(dz=1) if way == 0 else me.at(dz=NZ - 1)
+        return remote(source, target, self.zsend, self.zrecv.at[way * 4 + step - 1], device)
 
     def step(self, step):
         for way in (0, 1):
             if step > 1:
-                self.ring(way, step - 1, True).wait_recv()
+                self.ring(way, step - 1).wait_recv()
             if step <= 4:
-                self.ring(way, step, False).start()
+                self.ring(way, step).start()
 
     def left(self):
         me = self.me
         self.first.left()
-        sample = self.buf.at[me.c, pl.ds(0, 7), pl.ds(0, NY), pl.ds(0, HALF)]
+        sample = self.buf.at[me.c, pl.ds(0, 7), pl.ds(0, NY), pl.ds(0, SPLIT)]
         remote(sample, sample, self.zsend, self.zrecv.at[0], me.at(dz=1)).wait_send()
 
 
-class ColumnGather:
-    def __init__(self, me, buf, zsend, zrecv, ysend, yrecv):
-        self.me, self.buf = me, buf
-        self.ysend, self.yrecv = ysend.at[0], yrecv
-        self.zsend, self.zrecv = zsend.at[0], zrecv
-
-    def block(self, shift, ys):
-        return self.buf.at[self.me.c, (self.me.z + shift) % NZ, ys, pl.ds(HALF, HALF)]
-
-    def ring(self, way, step, arriving):
-        far = step if arriving else step - 1
-        block = self.block((NZ - far) % NZ if way == 0 else far, self.me.y)
-        there = self.me.at(dz=1) if way == 0 else self.me.at(dz=NZ - 1)
-        return remote(block, block, self.zsend, self.zrecv.at[way * 4 + step - 1], there)
-
-    def spread(self, shift):
-        block = self.block(shift, self.me.y)
-        for i in range(1, NY):
-            remote(block, block, self.ysend, self.yrecv.at[shift], self.me.at(dy=i)).start()
-
-    def wait_spread(self, shift):
-        sample = self.block(shift, pl.ds(0, 3))
-        remote(sample, sample, self.ysend, self.yrecv.at[shift], self.me.at(dy=1)).wait_recv()
-
-    def step(self, step):
-        for way in (0, 1):
-            last = 4 - way
-            if 1 < step <= last + 1:
-                self.ring(way, step - 1, True).wait_recv()
-            if step <= last:
-                self.ring(way, step, False).start()
-        if step == 1:
-            self.spread(0)
-        else:
-            self.spread(NZ - step + 1)
-            if step < 5:
-                self.spread(step - 1)
-
-    def left(self):
-        me = self.me
-        sample = self.buf.at[me.c, pl.ds(0, 7), 0, pl.ds(HALF, HALF)]
-        remote(sample, sample, self.zsend, self.zrecv.at[0], me.at(dz=1)).wait_send()
-        sample = self.buf.at[me.c, pl.ds(0, NZ), pl.ds(0, 3), pl.ds(HALF, HALF)]
-        remote(sample, sample, self.ysend, self.yrecv.at[0], me.at(dy=1)).wait_send()
-
-
-class CoreSwap:
-    def __init__(self, me, buf, send, recv):
-        self.me, self.buf, self.send, self.recv = me, buf, send.at[0], recv
-
-    def copy(self, at_c, shift):
-        block = self.buf.at[at_c, (self.me.z + shift) % NZ]
-        return remote(block, block, self.send, self.recv.at[shift], self.me.at(flip=True))
-
-    def start(self, shift):
-        self.copy(self.me.c, shift).start()
-
-    def wait(self, shift):
-        self.copy(1 - self.me.c, shift).wait_recv()
-
-    def left(self):
-        block = self.buf.at[self.me.c]
-        remote(block, block, self.send, self.recv.at[0], self.me.at(flip=True)).wait_send()
+def rest_over_z(me, buf, send, recv):
+    rows = pl.ds(SPLIT, buf.shape[3] - SPLIT)
+    source = buf.at[me.c, 3, me.y, rows]
+    copies = [
+        remote(source, buf.at[me.c, (3 - i) % NZ, me.y, rows], send.at[0], recv.at[0], me.at(dz=i))
+        for i in range(1, NZ)
+    ]
+    return Batch(me, copies, buf.at[me.c, pl.ds(0, 7), me.y, rows], send.at[0], recv.at[0])
+
+
+def rest_over_y(me, buf, send, recv):
+    rows = pl.ds(SPLIT, buf.shape[3] - SPLIT)
+    block = buf.at[me.c, pl.ds(0, NZ), me.y, rows]
+    copies = [remote(block, block, send.at[0], recv.at[0], me.at(dy=i)) for i in range(1, NY)]
+    return Batch(me, copies, buf.at[me.c, pl.ds(0, NZ), pl.ds(0, 3), rows], send.at[0], recv.at[0])
+
+
+def swap(me, buf, first, count, rows, send, recv):
+    block = buf.at[me.c, pl.ds(first, count), pl.ds(0, NY), rows]
+    return Batch(me, [remote(block, block, send, recv, me.at(flip=True))], block, send, recv)
 
 
 def exchange(me, axis, count, source, target, sample, send, recv):
@@ -263,10 +220,10 @@
     l_x=pltpu.VMEM((NC * NX, 48, 128), BF16),
 )
 PAIRS = dict(
-    tk=(1, 12), ck=(2, 2), az=(1, 1), ay=(1, 1), my=(1, 1), mz=(1, 1), mx=(1, 1), gr=(2, 12), ot=(2, 2),
+    tk=(1, 8), ck=(2, 2), az=(1, 1), ay=(1, 1), my=(1, 1), mz=(1, 1), mx=(1, 1), gr=(2, 12), ot=(2, 2),
     ip=(1, 1), iz=(1, 1), iy=(1, 1), ic=(1, 1), ly=(1, 1), lz=(1, 1), lx=(1, 1), lg=(1, 1),
 )
-PLANES = dict(wy=(1, 1), wz=(1, 8), vz=(1, 8), vy=(1, 8), wc=(1, 8))
+PLANES = dict(wy=(1, 1), wz=(1, 8), vz=(1, 1), vy=(1, 1), wc=(4, 4))
 LOCAL = 8
 
 
@@ -335,7 +292,7 @@
         block = wq[:, aligned(b * width + s * att, att)].astype(F32)
         pieces += [block[:, i * 128 : (i + 1) * 128] for i in range(3)]
     pieces.append(jnp.zeros((8, 128), F32))
-    r.w_all[c, z, y] = jnp.concatenate(pieces, axis=0).astype(BF16)
+    r.w_all[c, 3, y] = jnp.concatenate(pieces, axis=0).astype(BF16)
     wide = cond[...].astype(F32)
     wide = (wide / (1.0 + jnp.exp(-wide))).astype(BF16).astype(F32)
     r.a_rows[...] = jnp.zeros_like(r.a_rows)
@@ -361,34 +318,31 @@
         batches.append(batch)
         return batch
 
-    def row_chunk(i):
-        return pl.ds(i * chunk, chunk)
-
-    def token_copy(source, owner, i, slot, there):
-        return remote(source, r.tok_all.at[owner, row_chunk(i)], r.tk_s.at[0], r.tk_r.at[slot], there)
+    quarter = part // 2
+
+    def token_copy(img, slot):
+        start = img * part
+        owner, at, there = (
+            (s, pl.ds(start, part), right),
+            (s, pl.ds(start, part), left),
+            (sl, pl.ds(start, quarter), right),
+            (sr, pl.ds(start + quarter, quarter), left),
+        )[slot]
+        block = r.tok_all.at[owner, at]
+        return remote(block, block, r.tk_s.at[0], r.tk_r.at[4 * img + slot], there)
 
     def own_tokens(img):
-        i = 2 * img
-        token_copy(r.tok_all.at[s, row_chunk(i)], s, i, i, right).start()
-        token_copy(r.tok_all.at[s, row_chunk(i + 1)], s, i + 1, 4 + i + 1, left).start()
-        token_copy(r.tok_all.at[s, row_chunk(i + 1)], s, i + 1, i + 1, right).start()
-        token_copy(r.tok_all.at[s, row_chunk(i)], s, i, 4 + i, left).start()
+        token_copy(img, 0).start()
+        token_copy(img, 1).start()
 
     def forward(img):
-        i = 2 * img
-        token_copy(r.tok_all.at[s, row_chunk(i)], sl, i, i, right).wait_recv()
-        token_copy(r.tok_all.at[sl, row_chunk(i)], sl, i, 8 + i, right).start()
-        i = i + 1
-        token_copy(r.tok_all.at[s, row_chunk(i)], sr, i, 4 + i, left).wait_recv()
-        token_copy(r.tok_all.at[sr, row_chunk(i)], sr, i, 8 + i, left).start()
+        for slot in (0, 1):
+            token_copy(img, slot).wait_recv()
+            token_copy(img, slot + 2).start()
 
     def wait_tokens(img):
-        i = 2 * img
-        own = r.tok_all.at[s, row_chunk(i)]
-        token_copy(own, sl, i + 1, i + 1, right).wait_recv()
-        token_copy(own, sr, i, 4 + i, left).wait_recv()
-        token_copy(own, so, i, 8 + i, right).wait_recv()
-        token_copy(own, so, i + 1, 8 + i + 1, left).wait_recv()
+        token_copy(img, 2).wait_recv()
+        token_copy(img, 3).wait_recv()
 
     def own_cotangent(img):
         at = pl.ds(img * part, part)
@@ -409,9 +363,7 @@
     )
     weights = RowGather(me, r.w_all, *r.wy, *r.wz)
     weights.start_y()
-    others = ColumnGather(me, r.w_all, *r.vz, *r.vy)
-    others.step(1)
-    swap = CoreSwap(me, r.w_all, *r.wc)
+    rest = send(rest_over_z(me, r.w_all, *r.vz))
     own_tokens(0)
     raw_cot.wait()
     r.cot_own[...] = nn(perm, r.cot_raw[...]).astype(BF16)
@@ -439,7 +391,6 @@
     )
     weights.first.arrived()
     weights.step(1)
-    others.step(2)
     ay.arrived()
     locals_[0].wait()
     r.a_wide[...] = r.a_y[...].reshape(256, 128).astype(F32)
@@ -459,7 +410,8 @@
     forward(0)
     cot0 = own_cotangent(0)
     own_tokens(1)
-    others.step(3)
+    rest.arrived()
+    spread = send(rest_over_y(me, r.w_all, *r.vy))
     row = lax.broadcasted_iota(jnp.int32, (256, 128), 0)
     col = lax.broadcasted_iota(jnp.int32, (256, 128), 1)
     pick = jnp.where((row == col + offset) & (col < 48), 1.0, 0.0).astype(BF16)
@@ -477,24 +429,24 @@
             me, "dz", NZ, lambda i: r.m_plane.at[(z + i) % NZ], lambda i: r.m_z.at[i - 1], r.m_z, r.mz_s, r.mz_r
         )
     )
-    def place(shift):
-        swap.wait(shift)
-        at_z = (z + shift) % NZ
-
-        @pl.loop(0, NY)
-        def _(at_y):
-            first = r.w_all[0, at_z, at_y].astype(F32)
-            other = r.w_all[1, at_z, at_y].astype(F32)
+    def place(first, count):
+        @pl.loop(0, NY * count)
+        def _(i):
+            at_y, at_d = i // count, first + i % count
+            one = r.w_all[0, at_d, at_y].astype(F32)
+            other = r.w_all[1, at_d, at_y].astype(F32)
+            at_z = (z + at_d + NZ - 3) % NZ
             at = pl.ds(pl.multiple_of(48 * (NZ * at_y + at_z), 16), 48)
             for t in range(9):
-                both = jnp.concatenate([first[24 * t : 24 * t + 24], other[24 * t : 24 * t + 24]], axis=0)
+                both = jnp.concatenate([one[24 * t : 24 * t + 24], other[24 * t : 24 * t + 24]], axis=0)
                 r.w[at, t * 128 : (t + 1) * 128] = both.astype(BF16)
 
-    others.step(4)
+    def swap_part(index, first, count, rows):
+        return send(swap(me, r.w_all, first, count, rows, r.wc[0].at[index], r.wc[1].at[index]))
+
+    upper, lower = pl.ds(0, SPLIT), pl.ds(SPLIT, r.w_all.shape[3] - SPLIT)
     weights.step(3)
-    for shift in (0, 1, NZ - 1):
-        others.wait_spread(shift)
-        swap.start(shift)
+    near = swap_part(0, 1, 5, upper)
     mz.arrived()
     total = r.m_plane[z]
     for i in range(NZ - 1):
@@ -506,14 +458,10 @@
             me, "dx", NX, lambda i: r.m_own, lambda i: r.m_all.at[s], r.m_all.at[pl.ds(0, 3)], r.mx_s, r.mx_r
         )
     )
-    others.step(5)
     weights.step(4)
-    for shift in (2, NZ - 2):
-        others.wait_spread(shift)
-        swap.start(shift)
-    for shift in (0, 1, NZ - 1):
-        place(shift)
-
+    left_end = swap_part(1, 0, 1, upper)
+    spread.arrived()
+    lower_part = swap_part(3, 0, NZ, lower)
     mx.arrived()
     mod[...] = jnp.zeros_like(mod)
     for k in range(NX):
@@ -538,15 +486,18 @@
             r.stats[at, 1:2] = inverse
 
     weights.step(5)
-    for shift in (3, 5, 4):
-        others.wait_spread(shift)
-        swap.start(shift)
+    right_end = swap_part(2, 6, 2, upper)
     wait_tokens(0)
     normalize(0)
     forward(1)
     cot1 = own_cotangent(1)
-    for shift in (2, NZ - 2, 3, 5, 4):
-        place(shift)
+    near.arrived()
+    lower_part.arrived()
+    place(1, 5)
+    left_end.arrived()
+    right_end.arrived()
+    place(0, 1)
+    place(6, 2)
     for copy in locals_[1:]:
         copy.wait()
 
@@ -758,8 +709,6 @@
         grads_sent = r.pg.at[img, pl.ds(0, 3)]
         remote(grads_sent, grads_sent, r.gr_s.at[img], r.gr_r.at[0], right).wait_send()
     weights.left()
-    others.left()
-    swap.left()
 
 
 def whole(counts, tok, cot, cond, wq, up, down, mm):
@@ -807,12 +756,10 @@
     token_grad[...] = tn(perm, sorted_grad[...]).astype(BF16)
 
     ig_wide[...] = ig[...].reshape(3072, 128).astype(F32)
+    turned = act[...].astype(F32).T.astype(BF16)[:48]
     for j in range(24):
-        total = jnp.zeros((128, 128), F32)
-        for img in range(2):
-            part = ig_wide[pl.ds(img * 24 + j, 64, stride=48), :].astype(BF16)
-            total += tn(act[img * 64 : (img + 1) * 64], part)
-        mod_grad[:, j * 128 : (j + 1) * 128] = total[0:48]
+        parts = [ig_wide[pl.ds(img * 24 + j, 64, stride=48), :].astype(BF16) for img in range(2)]
+        mod_grad[:, j * 128 : (j + 1) * 128] = nn(turned, jnp.concatenate(parts, axis=0))
 
     place = dp % (NZ * NC)
     flat = pieces[...].astype(F32)

time: 91.4 us -> 91.7 us (level)
  no operation moved by 1% of the time
where the time goes in v7:
time: 91.7 us; the launch traced here: 91.5 us
  Pallas kernels  90.9 us (99%)
    pallas_call x1, Pallas kernels, whole(): pl.pallas_call(whole_kernel, out_shape=(jax.ShapeDtypeStruct((192, 1536),...  86.1 us
    pallas_call x1, Pallas kernels, tail(): pl.pallas_call(tail_kernel, out_shape=(jax.ShapeDtypeStruct((192, 1536),...  4.78 us

profile of v7, /device:TPU:1, one launch (start us, length us, event | category | flops | bytes accessed | tf_op | source)
XLA Modules:
  0.0 91.5 jit_solution(3030908523126664007)
XLA Ops:
  0.6 86.1 %whole.1 = (bf16[192,1536]{1,0:T(8,128)(2,1)}, bf16[192,1536]{1,0:T(8,128)(2,1)}, f32[8,3072]{1,0:T(8,128)}, bf16[128,128]{1,0:T(8,128)(2,1)}, bf16[2,4,8,48,128...) custom-call(s32[2,64]{1,0:T(2,128)} %bitcast.12, bf16[192,1536]{1,0:T(8,128)(2,1)} %bitcast.7, bf16[192,1536]{1,0:T(8,128)(2,1)} %bitcast.9, ...), custom_call_target="tpu_custom_call" | custom-call | tf_op jit(solution)/shard_map/whole/pallas_call | solution.py:715
  86.7 4.8 %tail.1 = (bf16[192,1536]{1,0:T(8,128)(2,1)}, bf16[192,1536]{1,0:T(8,128)(2,1)}, f32[24,64]{1,0:T(8,128)}, f32[64,72]{1,0:T(8,128)}, f32[48,3072]{1,0:T(8,128)}) custom-call(s32[2,64]{1,0:T(2,128)} %bitcast.13, bf16[192,1536]{1,0:T(8,128)(2,1)} %get-tuple-element.16.attn, bf16[192,1536]{1,0:T(8,128)(2,1)} %get-tuple-element.17.grad, ...), custom_call_target="tpu_custom_call" | custom-call | tf_op jit(solution)/shard_map/tail/pallas_call | solution.py:784

commit v8 on v7

--- a/solution.py
+++ b/solution.py
@@ -60,7 +60,7 @@
     pl.semaphore_wait(pltpu.get_barrier_semaphore(), len(peers_of(me)))
 
 
-SPLIT = 128
+SPLIT = 96
 
 
 class Batch:
@@ -367,6 +367,7 @@
     own_tokens(0)
     raw_cot.wait()
     r.cot_own[...] = nn(perm, r.cot_raw[...]).astype(BF16)
+    cot0 = own_cotangent(0)
     az.arrived()
     turned = r.a_z[...].astype(F32)
     for at_y in range(NY):
@@ -407,17 +408,8 @@
     my = plane_exchange(
         lambda at, there: r.part_low.at[at, there], lambda i: r.m_in.at[i], r.m_in, r.my_s, r.my_r
     )
-    forward(0)
-    cot0 = own_cotangent(0)
-    own_tokens(1)
     rest.arrived()
     spread = send(rest_over_y(me, r.w_all, *r.vy))
-    row = lax.broadcasted_iota(jnp.int32, (256, 128), 0)
-    col = lax.broadcasted_iota(jnp.int32, (256, 128), 1)
-    pick = jnp.where((row == col + offset) & (col < 48), 1.0, 0.0).astype(BF16)
-    a_own[...] = nn(r.a_pair[...], pick).astype(BF16)
-    weights.step(2)
-    r.cot_all[s] = r.cot_own[:, aligned(s * att, att)]
     my.arrived()
     total = r.part_low[c, y].astype(F32)
     for i in range(7):
@@ -429,47 +421,34 @@
             me, "dz", NZ, lambda i: r.m_plane.at[(z + i) % NZ], lambda i: r.m_z.at[i - 1], r.m_z, r.mz_s, r.mz_r
         )
     )
-    def place(first, count):
+    weights.step(2)
+    forward(0)
+    own_tokens(1)
+    row = lax.broadcasted_iota(jnp.int32, (256, 128), 0)
+    col = lax.broadcasted_iota(jnp.int32, (256, 128), 1)
+    pick = jnp.where((row == col + offset) & (col < 48), 1.0, 0.0).astype(BF16)
+    a_own[...] = nn(r.a_pair[...], pick).astype(BF16)
+    r.cot_all[s] = r.cot_own[:, aligned(s * att, att)]
+
+    def place(first, count, tiles, start):
         @pl.loop(0, NY * count)
         def _(i):
             at_y, at_d = i // count, first + i % count
-            one = r.w_all[0, at_d, at_y].astype(F32)
-            other = r.w_all[1, at_d, at_y].astype(F32)
+            rows_at = pl.ds(start, 24 * len(tiles))
+            one = r.w_all[0, at_d, at_y, rows_at].astype(F32)
+            other = r.w_all[1, at_d, at_y, rows_at].astype(F32)
             at_z = (z + at_d + NZ - 3) % NZ
             at = pl.ds(pl.multiple_of(48 * (NZ * at_y + at_z), 16), 48)
-            for t in range(9):
-                both = jnp.concatenate([one[24 * t : 24 * t + 24], other[24 * t : 24 * t + 24]], axis=0)
+            for k, t in enumerate(tiles):
+                both = jnp.concatenate([one[24 * k : 24 * k + 24], other[24 * k : 24 * k + 24]], axis=0)
                 r.w[at, t * 128 : (t + 1) * 128] = both.astype(BF16)
+
+    upper_tiles, lower_tiles = range(4), range(4, 9)
 
     def swap_part(index, first, count, rows):
         return send(swap(me, r.w_all, first, count, rows, r.wc[0].at[index], r.wc[1].at[index]))
 
     upper, lower = pl.ds(0, SPLIT), pl.ds(SPLIT, r.w_all.shape[3] - SPLIT)
-    weights.step(3)
-    near = swap_part(0, 1, 5, upper)
-    mz.arrived()
-    total = r.m_plane[z]
-    for i in range(NZ - 1):
-        total += r.m_z[i]
-    r.m_own[...] = total
-    r.m_all[s] = total
-    mx = send(
-        exchange(
-            me, "dx", NX, lambda i: r.m_own, lambda i: r.m_all.at[s], r.m_all.at[pl.ds(0, 3)], r.mx_s, r.mx_r
-        )
-    )
-    weights.step(4)
-    left_end = swap_part(1, 0, 1, upper)
-    spread.arrived()
-    lower_part = swap_part(3, 0, NZ, lower)
-    mx.arrived()
-    mod[...] = jnp.zeros_like(mod)
-    for k in range(NX):
-        for img in range(2):
-            for j in range(6):
-                at = 768 * k + 128 * j
-                mod[img : img + 1, at : at + 128] = r.m_all[k, img * 6 + j : img * 6 + j + 1, :]
-
     def normalize(img):
         @pl.loop(0, NX)
         def _(block):
@@ -485,19 +464,45 @@
             r.stats[at, 0:1] = mean
             r.stats[at, 1:2] = inverse
 
+    mz.arrived()
+    total = r.m_plane[z]
+    for i in range(NZ - 1):
+        total += r.m_z[i]
+    r.m_own[...] = total
+    r.m_all[s] = total
+    mx = send(
+        exchange(
+            me, "dx", NX, lambda i: r.m_own, lambda i: r.m_all.at[s], r.m_all.at[pl.ds(0, 3)], r.mx_s, r.mx_r
+        )
+    )
+    weights.step(3)
+    near = swap_part(0, 1, 5, upper)
+    mx.arrived()
+    mod[...] = jnp.zeros_like(mod)
+    for k in range(NX):
+        for img in range(2):
+            for j in range(6):
+                at = 768 * k + 128 * j
+                mod[img : img + 1, at : at + 128] = r.m_all[k, img * 6 + j : img * 6 + j + 1, :]
+
+    wait_tokens(0)
+    normalize(0)
+    weights.step(4)
+    left_end = swap_part(1, 0, 1, upper)
+    near.arrived()
+    place(1, 5, upper_tiles, 0)
+    spread.arrived()
+    lower_part = swap_part(3, 0, NZ, lower)
     weights.step(5)
     right_end = swap_part(2, 6, 2, upper)
-    wait_tokens(0)
-    normalize(0)
     forward(1)
     cot1 = own_cotangent(1)
-    near.arrived()
+    left_end.arrived()
+    place(0, 1, upper_tiles, 0)
+    right_end.arrived()
+    place(6, 2, upper_tiles, 0)
     lower_part.arrived()
-    place(1, 5)
-    left_end.arrived()
-    right_end.arrived()
-    place(0, 1)
-    place(6, 2)
+    place(0, NZ, lower_tiles, SPLIT)
     for copy in locals_[1:]:
         copy.wait()
 

time: 91.7 us -> 98.5 us (1.074)
  Pallas kernels: 90.9 us -> 97.7 us
    pallas_call x1, Pallas kernels: 86.1 us -> 93 us  [whole(): pl.pallas_call(whole_kernel, out_shape=(jax.ShapeDtypeStruct((192, 1536),...]
where the time goes in v8:
time: 98.5 us; the launch traced here: 98.4 us
  Pallas kernels  97.7 us (99%)
    pallas_call x1, Pallas kernels, whole(): pl.pallas_call(whole_kernel, out_shape=(jax.ShapeDtypeStruct((192, 1536),...  93 us
    pallas_call x1, Pallas kernels, tail(): pl.pallas_call(tail_kernel, out_shape=(jax.ShapeDtypeStruct((192, 1536),...  4.78 us

profile of v8, /device:TPU:1, one launch (start us, length us, event | category | flops | bytes accessed | tf_op | source)
XLA Modules:
  0.0 98.4 jit_solution(7989851221661061008)
XLA Ops:
  0.6 93.0 %whole.1 = (bf16[192,1536]{1,0:T(8,128)(2,1)}, bf16[192,1536]{1,0:T(8,128)(2,1)}, f32[8,3072]{1,0:T(8,128)}, bf16[128,128]{1,0:T(8,128)(2,1)}, bf16[2,4,8,48,128...) custom-call(s32[2,64]{1,0:T(2,128)} %bitcast.12, bf16[192,1536]{1,0:T(8,128)(2,1)} %bitcast.7, bf16[192,1536]{1,0:T(8,128)(2,1)} %bitcast.9, ...), custom_call_target="tpu_custom_call" | custom-call | tf_op jit(solution)/shard_map/whole/pallas_call | solution.py:720
  93.6 4.8 %tail.1 = (bf16[192,1536]{1,0:T(8,128)(2,1)}, bf16[192,1536]{1,0:T(8,128)(2,1)}, f32[24,64]{1,0:T(8,128)}, f32[64,72]{1,0:T(8,128)}, f32[48,3072]{1,0:T(8,128)}) custom-call(s32[2,64]{1,0:T(2,128)} %bitcast.13, bf16[192,1536]{1,0:T(8,128)(2,1)} %get-tuple-element.16.attn, bf16[192,1536]{1,0:T(8,128)(2,1)} %get-tuple-element.17.grad, ...), custom_call_target="tpu_custom_call" | custom-call | tf_op jit(solution)/shard_map/tail/pallas_call | solution.py:789

commit v9 on v8

--- a/solution.py
+++ b/solution.py
@@ -122,11 +122,38 @@
     return Batch(me, copies, buf.at[me.c, pl.ds(0, 7), me.y, rows], send.at[0], recv.at[0])
 
 
-def rest_over_y(me, buf, send, recv):
-    rows = pl.ds(SPLIT, buf.shape[3] - SPLIT)
-    block = buf.at[me.c, pl.ds(0, NZ), me.y, rows]
-    copies = [remote(block, block, send.at[0], recv.at[0], me.at(dy=i)) for i in range(1, NY)]
-    return Batch(me, copies, buf.at[me.c, pl.ds(0, NZ), pl.ds(0, 3), rows], send.at[0], recv.at[0])
+class Spread:
+    def __init__(self, me, buf, send, recv):
+        self.me, self.buf, self.send, self.recv = me, buf, send.at[0], recv
+        self.rows = pl.ds(SPLIT, buf.shape[3] - SPLIT)
+
+    def copy(self, slot):
+        me = self.me
+        owner, blocks, there = (
+            (me.y, pl.ds(0, NZ), 1),
+            (me.y, pl.ds(0, NZ), NY - 1),
+            ((me.y + NY - 1) % NY, pl.ds(0, NZ // 2), 1),
+            ((me.y + 1) % NY, pl.ds(NZ // 2, NZ // 2), NY - 1),
+        )[slot]
+        block = self.buf.at[me.c, blocks, owner, self.rows]
+        return remote(block, block, self.send, self.recv.at[slot], me.at(dy=there))
+
+    def start(self):
+        self.copy(0).start()
+        self.copy(1).start()
+
+    def forward(self):
+        for slot in (0, 1):
+            self.copy(slot).wait_recv()
+            self.copy(slot + 2).start()
+
+    def arrived(self):
+        self.copy(2).wait_recv()
+        self.copy(3).wait_recv()
+
+    def left(self):
+        sample = self.buf.at[self.me.c, pl.ds(0, NZ), pl.ds(0, 3), self.rows]
+        remote(sample, sample, self.send, self.recv.at[0], self.me.at(dy=1)).wait_send()
 
 
 def swap(me, buf, first, count, rows, send, recv):
@@ -202,6 +229,8 @@
     low_grad=pltpu.VMEM((768, 64), BF16),
     cot_own=pltpu.VMEM((192, 1536), BF16),
     attn=pltpu.VMEM((NX, 2, 96, 384), BF16),
+    stage_l=pltpu.VMEM((2, 48, 384), BF16),
+    stage_r=pltpu.VMEM((2, 48, 384), BF16),
     pg=pltpu.VMEM((2, NX, 96, 1536), BF16),
     ip=pltpu.VMEM((8, 3072), F32),
     half_l=pltpu.VMEM((2, 48, 1536), BF16),
@@ -220,10 +249,10 @@
     l_x=pltpu.VMEM((NC * NX, 48, 128), BF16),
 )
 PAIRS = dict(
-    tk=(1, 8), ck=(2, 2), az=(1, 1), ay=(1, 1), my=(1, 1), mz=(1, 1), mx=(1, 1), gr=(2, 12), ot=(2, 2),
+    tk=(1, 8), ck=(2, 2), az=(1, 1), ay=(1, 1), my=(1, 1), mz=(1, 1), mx=(1, 1), gr=(2, 12), ot=(2, 12),
     ip=(1, 1), iz=(1, 1), iy=(1, 1), ic=(1, 1), ly=(1, 1), lz=(1, 1), lx=(1, 1), lg=(1, 1),
 )
-PLANES = dict(wy=(1, 1), wz=(1, 8), vz=(1, 1), vy=(1, 1), wc=(4, 4))
+PLANES = dict(wy=(1, 1), wz=(1, 8), vz=(1, 1), vy=(1, 4), wc=(4, 4))
 LOCAL = 8
 
 
@@ -409,7 +438,8 @@
         lambda at, there: r.part_low.at[at, there], lambda i: r.m_in.at[i], r.m_in, r.my_s, r.my_r
     )
     rest.arrived()
-    spread = send(rest_over_y(me, r.w_all, *r.vy))
+    spread = send(Spread(me, r.w_all, *r.vy))
+    spread.start()
     my.arrived()
     total = r.part_low[c, y].astype(F32)
     for i in range(7):
@@ -485,6 +515,7 @@
                 at = 768 * k + 128 * j
                 mod[img : img + 1, at : at + 128] = r.m_all[k, img * 6 + j : img * 6 + j + 1, :]
 
+    spread.forward()
     wait_tokens(0)
     normalize(0)
     weights.step(4)
@@ -543,16 +574,28 @@
 
     mine = aligned(s * att, att)
 
+    def attn_copy(img, slot):
+        start, half = img * part, part // 2
+        upper_half, lower_half = pl.ds(start, half), pl.ds(start + half, half)
+        source, target, there = (
+            (r.attn.at[sr, img], attn_out.at[pl.ds(start, part), mine], right),
+            (r.attn.at[sl, img], attn_out.at[pl.ds(start, part), mine], left),
+            (r.attn.at[so, img, pl.ds(0, half)], r.stage_l.at[img], right),
+            (r.attn.at[so, img, pl.ds(half, half)], r.stage_r.at[img], left),
+            (r.stage_l.at[img], attn_out.at[upper_half, aligned(sl * att, att)], right),
+            (r.stage_r.at[img], attn_out.at[lower_half, aligned(sr * att, att)], left),
+        )[slot]
+        return remote(source, target, r.ot_s.at[img], r.ot_r.at[6 * img + slot], there)
+
     def give(img):
-        at = slice(img * part, (img + 1) * part)
-        copies = [
-            remote(
-                r.attn.at[(s + i) % NX, img], attn_out.at[at, mine], r.ot_s.at[img], r.ot_r.at[img], me.at(dx=i)
-            )
-            for i in range(1, NX)
-        ]
-        attn_out[at, mine] = r.attn[s, img]
-        return send(Batch(me, copies, attn_out.at[at, pl.ds(0, 3 * att)], r.ot_s.at[img], r.ot_r.at[img]))
+        for slot in (2, 3, 0, 1):
+            attn_copy(img, slot).start()
+        attn_out[img * part : (img + 1) * part, mine] = r.attn[s, img]
+
+    def pass_on(img):
+        for slot in (2, 3):
+            attn_copy(img, slot).wait_recv()
+            attn_copy(img, slot + 2).start()
 
     def low_grads(img):
         at = slice(img * image_rows, (img + 1) * image_rows)
@@ -600,16 +643,17 @@
     project(0)
     cot0.arrived()
     attend(0)
-    out0 = give(0)
+    give(0)
     low_grads(0)
     grads(0)
     reduce_first(0)
+    pass_on(0)
     wait_tokens(1)
     normalize(1)
     project(1)
     cot1.arrived()
     attend(1)
-    out1 = give(1)
+    give(1)
     reduce_second(0)
     low_grads(1)
 
@@ -626,6 +670,7 @@
 
     grads(1)
     reduce_first(1)
+    pass_on(1)
     for img in range(2):
         for j in range(24):
             at = img * 24 + j
@@ -703,8 +748,11 @@
         ).astype(BF16)
     ic.arrived()
     lg.arrived()
-    out0.arrived()
-    out1.arrived()
+    for img in range(2):
+        for slot in (0, 1, 4, 5):
+            attn_copy(img, slot).wait_recv()
+        sent = attn_out.at[pl.ds(img * part, part)]
+        remote(sent, sent, r.ot_s.at[img], r.ot_r.at[0], right).wait_send()
 
     for batch in batches:
         batch.left()

time: 98.5 us -> 99.6 us (1.011)
  Pallas kernels: 97.7 us -> 98.8 us
    pallas_call x1, Pallas kernels: 93 us -> 94.1 us  [whole(): pl.pallas_call(whole_kernel, out_shape=(jax.ShapeDtypeStruct((192, 1536),...]
where the time goes in v9:
time: 99.6 us; the launch traced here: 99.5 us
  Pallas kernels  98.8 us (99%)
    pallas_call x1, Pallas kernels, whole(): pl.pallas_call(whole_kernel, out_shape=(jax.ShapeDtypeStruct((192, 1536),...  94.1 us
    pallas_call x1, Pallas kernels, tail(): pl.pallas_call(tail_kernel, out_shape=(jax.ShapeDtypeStruct((192, 1536),...  4.78 us

profile of v9, /device:TPU:1, one launch (start us, length us, event | category | flops | bytes accessed | tf_op | source)
XLA Modules:
  0.0 99.5 jit_solution(18101857127712614907)
XLA Ops:
  0.6 94.1 %whole.1 = (bf16[192,1536]{1,0:T(8,128)(2,1)}, bf16[192,1536]{1,0:T(8,128)(2,1)}, f32[8,3072]{1,0:T(8,128)}, bf16[128,128]{1,0:T(8,128)(2,1)}, bf16[2,4,8,48,128...) custom-call(s32[2,64]{1,0:T(2,128)} %bitcast.12, bf16[192,1536]{1,0:T(8,128)(2,1)} %bitcast.7, bf16[192,1536]{1,0:T(8,128)(2,1)} %bitcast.9, ...), custom_call_target="tpu_custom_call" | custom-call | tf_op jit(solution)/shard_map/whole/pallas_call | solution.py:768
  94.7 4.8 %tail.1 = (bf16[192,1536]{1,0:T(8,128)(2,1)}, bf16[192,1536]{1,0:T(8,128)(2,1)}, f32[24,64]{1,0:T(8,128)}, f32[64,72]{1,0:T(8,128)}, f32[48,3072]{1,0:T(8,128)}) custom-call(s32[2,64]{1,0:T(2,128)} %bitcast.13, bf16[192,1536]{1,0:T(8,128)(2,1)} %get-tuple-element.16.attn, bf16[192,1536]{1,0:T(8,128)(2,1)} %get-tuple-element.17.grad, ...), custom_call_target="tpu_custom_call" | custom-call | tf_op jit(solution)/shard_map/tail/pallas_call | solution.py:837

commit v10 on v6

--- a/solution.py
+++ b/solution.py
@@ -401,20 +401,22 @@
         ]
         return send(Batch(me, copies, r.cot_all.at[pl.ds(0, 3), at], r.ck_s.at[img], r.ck_r.at[img]))
 
+    weights = RowGather(me, r.w_all, *r.wy, *r.wz)
+    weights.start_y()
     az = send(
         exchange(
             me, "dz", NZ, lambda i: r.a_src.at[(z + i) % NZ], lambda i: r.a_z.at[z], r.a_z.at[pl.ds(0, 7)],
             r.az_s, r.az_r,
         )
     )
-    weights = RowGather(me, r.w_all, *r.wy, *r.wz)
-    weights.start_y()
     others = ColumnGather(me, r.w_all, *r.vz, *r.vy)
     others.step(1)
     swap = CoreSwap(me, r.w_all, *r.wc)
     own_tokens(0)
     raw_cot.wait()
     r.cot_own[...] = nn(perm, r.cot_raw[...]).astype(BF16)
+    weights.first.arrived()
+    weights.step(1)
     az.arrived()
     turned = r.a_z[...].astype(F32)
     for at_y in range(NY):
@@ -437,8 +439,6 @@
     ay = plane_exchange(
         lambda at, there: r.a_low.at[there], lambda i: r.a_y.at[NY * c + y], r.a_y.at[pl.ds(0, 7)], r.ay_s, r.ay_r
     )
-    weights.first.arrived()
-    weights.step(1)
     others.step(2)
     ay.arrived()
     locals_[0].wait()
@@ -456,6 +456,7 @@
     my = plane_exchange(
         lambda at, there: r.part_low.at[at, there], lambda i: r.m_in.at[i], r.m_in, r.my_s, r.my_r
     )
+    weights.step(2)
     forward(0)
     cot0 = own_cotangent(0)
     own_tokens(1)
@@ -464,7 +465,6 @@
     col = lax.broadcasted_iota(jnp.int32, (256, 128), 1)
     pick = jnp.where((row == col + offset) & (col < 48), 1.0, 0.0).astype(BF16)
     a_own[...] = nn(r.a_pair[...], pick).astype(BF16)
-    weights.step(2)
     r.cot_all[s] = r.cot_own[:, aligned(s * att, att)]
     my.arrived()
     total = r.part_low[c, y].astype(F32)
@@ -490,8 +490,8 @@
                 both = jnp.concatenate([first[24 * t : 24 * t + 24], other[24 * t : 24 * t + 24]], axis=0)
                 r.w[at, t * 128 : (t + 1) * 128] = both.astype(BF16)
 
+    weights.step(3)
     others.step(4)
-    weights.step(3)
     for shift in (0, 1, NZ - 1):
         others.wait_spread(shift)
         swap.start(shift)
@@ -506,8 +506,8 @@
             me, "dx", NX, lambda i: r.m_own, lambda i: r.m_all.at[s], r.m_all.at[pl.ds(0, 3)], r.mx_s, r.mx_r
         )
     )
+    weights.step(4)
     others.step(5)
-    weights.step(4)
     for shift in (2, NZ - 2):
         others.wait_spread(shift)
         swap.start(shift)
@@ -696,6 +696,7 @@
         exchange(me, "dz", NZ, lambda i: own_ig, lambda i: own_ig, ig_all.at[c, y, pl.ds(0, 7)], r.iz_s, r.iz_r)
     )
 
+    reduce_second(1)
     lz.arrived()
     total = r.l_plane[z].astype(F32)
     for i in range(NZ - 1):
@@ -715,8 +716,6 @@
     iy = send(
         exchange(me, "dy", NY, lambda i: column, lambda i: column, ig_all.at[c, pl.ds(0, 3)], r.iy_s, r.iy_r)
     )
-    reduce_second(1)
-
     lx.arrived()
     sums = [r.l_x[i].astype(F32) + r.l_x[NX + i].astype(F32) for i in range(NX)]
     pieces = []

time: 91.4 us -> 93.7 us (1.025)
  Pallas kernels: 90.6 us -> 92.9 us
    pallas_call x1, Pallas kernels: 85.9 us -> 88.1 us  [whole(): pl.pallas_call(whole_kernel, out_shape=(jax.ShapeDtypeStruct((192, 1536),...]
where the time goes in v10:
time: 93.7 us; the launch traced here: 93.5 us
  Pallas kernels  92.9 us (99%)
    pallas_call x1, Pallas kernels, whole(): pl.pallas_call(whole_kernel, out_shape=(jax.ShapeDtypeStruct((192, 1536),...  88.1 us
    pallas_call x1, Pallas kernels, tail(): pl.pallas_call(tail_kernel, out_shape=(jax.ShapeDtypeStruct((192, 1536),...  4.75 us

profile of v10, /device:TPU:1, one launch (start us, length us, event | category | flops | bytes accessed | tf_op | source)
XLA Modules:
  0.0 93.5 jit_solution(10241397109304589076)
XLA Ops:
  0.6 88.1 %whole.1 = (bf16[192,1536]{1,0:T(8,128)(2,1)}, bf16[192,1536]{1,0:T(8,128)(2,1)}, f32[8,3072]{1,0:T(8,128)}, bf16[128,128]{1,0:T(8,128)(2,1)}, bf16[2,4,8,48,128...) custom-call(s32[2,64]{1,0:T(2,128)} %bitcast.12, bf16[192,1536]{1,0:T(8,128)(2,1)} %bitcast.7, bf16[192,1536]{1,0:T(8,128)(2,1)} %bitcast.9, ...), custom_call_target="tpu_custom_call" | custom-call | tf_op jit(solution)/shard_map/whole/pallas_call | solution.py:765
  88.8 4.7 %tail.1 = (bf16[192,1536]{1,0:T(8,128)(2,1)}, bf16[192,1536]{1,0:T(8,128)(2,1)}, f32[24,64]{1,0:T(8,128)}, f32[64,72]{1,0:T(8,128)}, f32[48,3072]{1,0:T(8,128)}) custom-call(s32[2,64]{1,0:T(2,128)} %bitcast.13, bf16[192,1536]{1,0:T(8,128)(2,1)} %get-tuple-element.16.attn, bf16[192,1536]{1,0:T(8,128)(2,1)} %get-tuple-element.17.grad, ...), custom_call_target="tpu_custom_call" | custom-call | tf_op jit(solution)/shard_map/tail/pallas_call | solution.py:836
